TPU v7x, 32 devices: a whole 2x2x4 slice. The times are simulated.
32 devices in a mesh: seq: 16 (over z, y, x), batch: 2 (over core).
Axes of the slice: x: 2, y: 2, z: 4, core: 2. Of those that a mesh axis runs over, the one named last changes fastest.
Arguments:
- tokens: bfloat16 [2, 2, 2048, 768], P('batch', None, 'seq'), may hold values from -6 to 6
- cotangent: bfloat16 [2, 2, 2048, 768], P('batch', None, 'seq'), may hold values from -6 to 6
- lengths: int32 [2, 2], P('batch'), may hold values from 256 to 2048, as said below
- norm_gain: float32 [4, 768], replicated, may hold values from 0.25 to 1.75
- norm_bias: float32 [4, 768], replicated, may hold values from -3 to 3
- w_qkv: bfloat16 [2, 768, 2304], replicated, may hold values from -0.21875 to 0.21875
- w_out: bfloat16 [2, 768, 768], replicated, may hold values from -0.4375 to 0.4375
- w_up: bfloat16 [2, 768, 3072], replicated, may hold values from -0.21875 to 0.21875
- w_down: bfloat16 [2, 3072, 768], replicated, may hold values from -0.109375 to 0.109375
- taps: float32 [4, 768], replicated, may hold values from -3 to 3
- skip: float32 [768], replicated, may hold values from -3 to 3
- ssm_rate: float32 [768, 64], replicated, may hold values from 0.00024414062 to 0.03
- ssm_out: float32 [768, 64], replicated, may hold values from -0.078125 to 0.078125
Outputs:
- mixed: bfloat16 [2, 2, 2048, 768], P('batch', None, 'seq')
- d_tokens: float32 [2, 2, 2048, 768], P('batch', None, 'seq')
- gain_grad: float32 [4, 768], P(None, 'seq')
- bias_grad: float32 [3, 768], P(None, 'seq')
- last_bias_grad: float32 [768], P('seq')
- w_qkv_grad: float32 [2, 768, 2304], P(None, 'seq')
- w_out_grad: float32 [2, 768, 768], P(None, 'seq')
- w_up_grad: float32 [2, 768, 3072], P(None, 'seq')
- w_down_grad: float32 [2, 3072, 768], P(None, 'seq')
- taps_grad: float32 [4, 768], P(None, 'seq')
- skip_grad: float32 [768], P('seq')
- rate_grad: float32 [768, 64], P('seq')
- ssm_out_grad: float32 [768, 64], P('seq')
Inputs may be any that keep to these rules, and one draw needn't show every extreme that they name: `lengths`: in every row one sequence, drawn from the seed, has all 2048 positions valid.
All inputs are finite; a program needn't handle non-finite values.
Results may differ from a plain program's by a relative error of at most 0.022.
Values may be sent and summed in bfloat16 or wider, within the bound.
A program may use at most 448 MiB of HBM per device.

v0:
```python
import math

import jax
import jax.numpy as jnp
from jax import lax
from jax.sharding import PartitionSpec as P

HEADS = 12
HEAD = 64
TAPS = 4


norm_eps = 1e-05
highest = lax.Precision.HIGHEST
masked_score = -1e30


def for_sending(array):
    return jax.tree.map(lambda a: a.astype(jnp.bfloat16) if a.dtype == jnp.float32 else a, array)


def passed_along(value, axis, steps):
    count = lax.axis_size(axis)
    initial, last = (max(0, -steps), min(count, count - steps))
    return lax.ppermute(value, axis, [(source, source + steps) for source in range(initial, last)])


def layer_norm(inputs, scale_row, shift_row):
    center = inputs - jnp.mean(inputs, -1, keepdims=True)
    spread = jnp.mean(center * center, -1, keepdims=True)
    return center * lax.rsqrt(spread + norm_eps) * scale_row + shift_row


def dense_product(operand_a, operand_b):
    return jnp.dot(operand_a, operand_b, preferred_element_type=jnp.float32)


def product_left(operand_a, operand_b):
    return lax.dot_general(
        operand_a, operand_b, (((0,), (0,)), ((), ())), preferred_element_type=jnp.float32
    )


def product_right(operand_a, operand_b):
    return lax.dot_general(
        operand_a, operand_b, (((1,), (1,)), ((), ())), preferred_element_type=jnp.float32
    )


def angle_table(count_rows, count_cols, period):
    product_index = (
        jnp.arange(count_rows, dtype=jnp.int32)[:, None]
        * jnp.arange(count_cols, dtype=jnp.int32)[None, :]
        % period
    )
    angles = product_index.astype(jnp.float32) * (2.0 * math.pi / period)
    return (jnp.cos(angles), jnp.sin(angles))


def table_einsum(form, table, data):
    return jnp.einsum(form, table, data, precision=highest)


def forward_spectrum(time_parts):
    count_parts = time_parts.shape[0]
    span_rows = time_parts.shape[2]
    count_freq = 2 * count_parts
    cos_parts, sin_parts = angle_table(count_freq, count_parts, count_freq)
    first_real = table_einsum("fp,pjsc->fjsc", cos_parts, time_parts)
    first_imag = -table_einsum("fp,pjsc->fjsc", sin_parts, time_parts)
    cos_twist, sin_twist = angle_table(count_freq, span_rows, count_freq * span_rows)
    cos_twist = cos_twist[:, None, :, None]
    sin_twist = sin_twist[:, None, :, None]
    twist_real = first_real * cos_twist + first_imag * sin_twist
    twist_imag = first_imag * cos_twist - first_real * sin_twist
    cos_span, sin_span = angle_table(span_rows, span_rows, span_rows)
    out_real = table_einsum("ts,fjsc->fjtc", cos_span, twist_real) + table_einsum(
        "ts,fjsc->fjtc", sin_span, twist_imag
    )
    out_imag = table_einsum("ts,fjsc->fjtc", cos_span, twist_imag) - table_einsum(
        "ts,fjsc->fjtc", sin_span, twist_real
    )
    return (out_real, out_imag)


def inverse_spectrum(freq_real, freq_imag):
    count_freq = freq_real.shape[0]
    span_rows = freq_real.shape[2]
    count_parts = count_freq // 2
    fft_length = count_freq * span_rows
    cos_span, sin_span = angle_table(span_rows, span_rows, span_rows)
    first_real = table_einsum("st,fjtc->fjsc", cos_span, freq_real) - table_einsum(
        "st,fjtc->fjsc", sin_span, freq_imag
    )
    first_imag = table_einsum("st,fjtc->fjsc", cos_span, freq_imag) + table_einsum(
        "st,fjtc->fjsc", sin_span, freq_real
    )
    cos_twist, sin_twist = angle_table(count_freq, span_rows, fft_length)
    cos_twist = cos_twist[:, None, :, None]
    sin_twist = sin_twist[:, None, :, None]
    twist_real = first_real * cos_twist - first_imag * sin_twist
    twist_imag = first_imag * cos_twist + first_real * sin_twist
    cos_parts, sin_parts = angle_table(count_parts, count_freq, count_freq)
    summed = table_einsum("pf,fjsc->pjsc", cos_parts, twist_real) - table_einsum(
        "pf,fjsc->pjsc", sin_parts, twist_imag
    )
    return summed / fft_length


def to_frequency(data_low):
    parts = lax.all_to_all(data_low[None], "seq", split_axis=3, concat_axis=0, tiled=True)
    return forward_spectrum(parts.astype(jnp.float32))


def from_frequency(freq_real, freq_imag):
    time_parts = inverse_spectrum(freq_real, freq_imag)
    joined = lax.all_to_all(
        for_sending(time_parts), "seq", split_axis=0, concat_axis=3, tiled=True
    ).astype(time_parts.dtype)
    return joined[0]


def kernel_parts(rate_slice, weight_slice, count_freq, span_rows):
    fft_length = count_freq * span_rows
    length_full = fft_length // 2
    frequency = (
        jnp.arange(count_freq, dtype=jnp.int32)[:, None]
        + count_freq * jnp.arange(span_rows, dtype=jnp.int32)[None, :]
    )
    angles = (frequency.astype(jnp.float32) * (2.0 * math.pi / fft_length))[:, None, :, None, None]
    odd_mask = (frequency % 2 == 1)[:, None, :, None, None]
    channels = rate_slice.shape[0]
    blocks = rate_slice.shape[1] // 8
    rate_blocks = rate_slice.reshape(channels, blocks, 8).transpose(1, 0, 2)
    weight_blocks = weight_slice.reshape(channels, blocks, 8).transpose(1, 0, 2)

    def add_block(running, piece_pair):
        rate_part, weight_part = piece_pair
        decays = jnp.exp(-rate_part)
        half_sine = jnp.sin(angles / 2.0)
        real_den = -jnp.expm1(-rate_part) + decays * 2.0 * half_sine * half_sine
        imag_den = decays * jnp.sin(angles)
        numerator = jnp.where(
            odd_mask, 1.0 + jnp.exp(-rate_part * length_full), -jnp.expm1(-rate_part * length_full)
        )
        factor = weight_part * numerator / (real_den * real_den + imag_den * imag_den)
        return (
            (
                running[0] + jnp.sum(factor * real_den, -1),
                running[1] - jnp.sum(factor * imag_den, -1),
            ),
            None,
        )

    zeros_init = jnp.zeros((count_freq, 1, span_rows, channels), jnp.float32)
    return lax.scan(
        jax.checkpoint(add_block), (zeros_init, zeros_init), (rate_blocks, weight_blocks)
    )[0]


def attention_mask(query_positions, key_count, length_value):
    key_positions = jnp.arange(key_count, dtype=jnp.int32)
    return (key_positions[None, :] <= query_positions[:, None]) & (
        key_positions[None, :] < length_value
    )


def head_slice(matrix, head_index):
    return lax.dynamic_slice_in_dim(matrix, head_index * HEAD, HEAD, 1)


def attend_forward(query_low, keys_low, values_low, length_value, query_positions):
    whole_keys, whole_values = (
        lax.all_gather(keys_low, "seq", axis=0, tiled=True),
        lax.all_gather(values_low, "seq", axis=0, tiled=True),
    )
    allowed = attention_mask(query_positions, whole_keys.shape[0], length_value)
    score_scale = HEAD ** (-0.5)

    def head_forward(head_index):
        scores = jnp.where(
            allowed,
            score_scale
            * product_right(head_slice(query_low, head_index), head_slice(whole_keys, head_index)),
            masked_score,
        )
        top_score = jnp.max(scores, -1, keepdims=True)
        expos = jnp.exp(scores - top_score)
        totals = jnp.sum(expos, -1, keepdims=True)
        probs_low = (expos / totals).astype(jnp.bfloat16)
        return (
            dense_product(probs_low, head_slice(whole_values, head_index)),
            (top_score + jnp.log(totals))[:, 0],
        )

    head_outputs, log_totals = lax.map(head_forward, jnp.arange(HEADS, dtype=jnp.int32))
    attended = head_outputs.transpose(1, 0, 2).reshape(query_low.shape[0], HEADS * HEAD)
    return (attended, log_totals, whole_keys, whole_values)


def join_heads(head_rows):
    return head_rows.transpose(1, 0, 2).reshape(head_rows.shape[1], HEADS * HEAD)


def attend_backward(
    query_low, whole_keys, whole_values, log_totals, grad_low, length_value, query_positions
):
    allowed = attention_mask(query_positions, whole_keys.shape[0], length_value)
    score_scale = HEAD ** (-0.5)
    span_rows = query_low.shape[0]

    def query_side(head_index):
        head_query = head_slice(query_low, head_index)
        head_keys = head_slice(whole_keys, head_index)
        head_grad = head_slice(grad_low, head_index)
        scores = jnp.where(
            allowed, score_scale * product_right(head_query, head_keys), masked_score
        )
        weights = jnp.exp(scores - log_totals[head_index][:, None])
        d_weights = product_right(head_grad, head_slice(whole_values, head_index))
        row_term = jnp.sum(weights * d_weights, -1, keepdims=True)
        d_scores = (weights * (d_weights - row_term)).astype(jnp.bfloat16)
        d_query = score_scale * dense_product(d_scores, head_keys)
        return (d_query, row_term[:, 0], d_scores, weights)

    def head_backward(head_index):
        d_query, row_term, d_scores, weights = query_side(head_index)
        head_query = head_slice(query_low, head_index)
        head_grad = head_slice(grad_low, head_index)
        d_keys = score_scale * product_left(d_scores, head_query)
        d_values = product_left(weights.astype(jnp.bfloat16), head_grad)
        return (d_query, d_keys, d_values)

    query_grads, key_grads, value_grads = lax.map(head_backward, jnp.arange(HEADS, dtype=jnp.int32))
    count_rows = span_rows * lax.axis_size("seq")
    key_part = (
        lax.slice_in_dim(key_grads, 0, count_rows, axis=1)
        .transpose(1, 0, 2)
        .reshape(count_rows, HEADS * HEAD)
    )
    value_part = (
        lax.slice_in_dim(value_grads, 0, count_rows, axis=1)
        .transpose(1, 0, 2)
        .reshape(count_rows, HEADS * HEAD)
    )
    key_value = lax.psum_scatter(
        jnp.stack([key_part, value_part], 1), "seq", scatter_dimension=0, tiled=True
    )
    return (join_heads(query_grads), key_value[:, 0], key_value[:, 1])


def per_device(
    tokens,
    cotangent,
    lengths,
    norm_gain,
    norm_bias,
    w_qkv,
    w_out,
    w_up,
    w_down,
    taps,
    skip,
    ssm_rate,
    ssm_out,
):
    seq_count = tokens.shape[1]
    span_rows = tokens.shape[2]
    width = tokens.shape[3]
    devices = lax.axis_size("seq")
    place = lax.axis_index("seq")
    channels = width // devices
    count_freq = 2 * devices
    fft_length = count_freq * span_rows
    rim = TAPS - 1
    row_count = seq_count * span_rows
    query_positions = place * span_rows + jnp.arange(span_rows, dtype=jnp.int32)
    validity = (query_positions[None, :] < lengths[0][:, None]).astype(jnp.float32)[:, :, None]
    rate_slice = lax.dynamic_slice_in_dim(ssm_rate, place * channels, channels, 0)
    weight_slice = lax.dynamic_slice_in_dim(ssm_out, place * channels, channels, 0)

    def spectrum_of(rate_in, weight_in):
        return kernel_parts(rate_in, weight_in, count_freq, span_rows)

    def feed_forward(inputs, norm_row, layer):
        normed_low = layer_norm(inputs, norm_gain[norm_row], norm_bias[norm_row]).astype(
            jnp.bfloat16
        )
        raised = dense_product(normed_low, w_up[layer])
        active_low = jax.nn.gelu(raised).astype(jnp.bfloat16)
        return (normed_low, raised, active_low, inputs + dense_product(active_low, w_down[layer]))

    def norm_backward(inputs, norm_row, d_normed):
        norm_pull = jax.vjp(layer_norm, inputs, norm_gain[norm_row], norm_bias[norm_row])[1]
        return norm_pull(d_normed)

    def feed_backward(grad_rows, inputs, normed_low, raised, active_low, norm_row, layer):
        branch_low = grad_rows.astype(jnp.bfloat16)
        down_grad = product_left(active_low, branch_low)
        d_active = product_right(branch_low, w_down[layer])
        gelu_pull = jax.vjp(jax.nn.gelu, raised)[1]
        d_raised = gelu_pull(d_active)[0].astype(jnp.bfloat16)
        up_grad = product_left(normed_low, d_raised)
        d_inputs, gain_part, bias_part = norm_backward(
            inputs, norm_row, product_right(d_raised, w_up[layer])
        )
        return (grad_rows + d_inputs, down_grad, up_grad, gain_part, bias_part)

    def forward_pass(token_block):
        masked_in = token_block[0].astype(jnp.float32) * validity
        flat_in = masked_in.reshape(row_count, width)
        normed_one = layer_norm(flat_in, norm_gain[0], norm_bias[0]).astype(jnp.bfloat16)
        qkv_one = dense_product(normed_one, w_qkv[0]).reshape(seq_count, span_rows, 3 * width)
        queries_one = qkv_one[:, :, :width]
        keys_one = qkv_one[:, :, width : 2 * width].astype(jnp.bfloat16)
        values_one = qkv_one[:, :, 2 * width :]
        earlier = passed_along(keys_one[:, span_rows - rim :], "seq", 1)
        extended = jnp.concatenate([earlier, keys_one], 1)
        shifted = sum(
            (
                taps[offset]
                * extended[:, rim - offset : rim - offset + span_rows].astype(jnp.float32)
                for offset in range(TAPS)
            )
        )
        carried_low = (shifted * values_one * validity).astype(jnp.bfloat16)
        carried_real, carried_imag = to_frequency(carried_low)
        kernel_both, kernel_pull = jax.vjp(spectrum_of, rate_slice, weight_slice)
        kernel_real, kernel_imag = kernel_both
        convolved = from_frequency(
            carried_real * kernel_real - carried_imag * kernel_imag,
            carried_real * kernel_imag + carried_imag * kernel_real,
        )
        carried = carried_low.astype(jnp.float32)
        mixer = convolved + skip * carried
        gated_low = (queries_one * mixer).reshape(row_count, width).astype(jnp.bfloat16)
        hidden_one = flat_in + dense_product(gated_low, w_out[0])
        normed_two, raised_one, active_one, hidden_two = feed_forward(hidden_one, 1, 0)
        normed_three = layer_norm(hidden_two, norm_gain[2], norm_bias[2]).astype(jnp.bfloat16)
        qkv_two = (
            dense_product(normed_three, w_qkv[1])
            .astype(jnp.bfloat16)
            .reshape(seq_count, span_rows, 3 * width)
        )
        attended_list = []
        totals_list = []
        keys_list = []
        values_list = []
        for seq_index in range(seq_count):
            attended, log_totals, whole_keys, whole_values = attend_forward(
                qkv_two[seq_index, :, :width],
                qkv_two[seq_index, :, width : 2 * width],
                qkv_two[seq_index, :, 2 * width :],
                lengths[0, seq_index],
                query_positions,
            )
            attended_list.append(attended)
            totals_list.append(log_totals)
            keys_list.append(whole_keys)
            values_list.append(whole_values)
        attended_low = jnp.concatenate(attended_list, 0).astype(jnp.bfloat16)
        hidden_three = hidden_two + dense_product(attended_low, w_out[1])
        normed_four, raised_two, active_two, hidden_four = feed_forward(hidden_three, 3, 1)
        output = hidden_four.reshape(seq_count, span_rows, width) * validity
        saved = dict(
            flat_in=flat_in,
            normed_one=normed_one,
            queries_one=queries_one,
            values_one=values_one,
            extended=extended,
            shifted=shifted,
            carried=carried,
            carried_real=carried_real,
            carried_imag=carried_imag,
            kernel_real=kernel_real,
            kernel_imag=kernel_imag,
            kernel_pull=kernel_pull,
            mixer=mixer,
            gated_low=gated_low,
            hidden_one=hidden_one,
            normed_two=normed_two,
            raised_one=raised_one,
            active_one=active_one,
            hidden_two=hidden_two,
            normed_three=normed_three,
            qkv_two=qkv_two,
            totals_list=totals_list,
            keys_list=keys_list,
            values_list=values_list,
            attended_low=attended_low,
            hidden_three=hidden_three,
            normed_four=normed_four,
            raised_two=raised_two,
            active_two=active_two,
        )
        return (output, saved)

    output = forward_pass(tokens)[0]
    saved = forward_pass(lax.optimization_barrier(tokens))[1]
    grad_rows = (cotangent[0].astype(jnp.float32) * validity).reshape(row_count, width)
    grad_rows, down_two, up_two, gain_four, bias_four = feed_backward(
        grad_rows,
        saved["hidden_three"],
        saved["normed_four"],
        saved["raised_two"],
        saved["active_two"],
        3,
        1,
    )
    branch_low = grad_rows.astype(jnp.bfloat16)
    out_two = product_left(saved["attended_low"], branch_low)
    d_attended = (
        product_right(branch_low, w_out[1])
        .astype(jnp.bfloat16)
        .reshape(seq_count, span_rows, width)
    )
    qkv_two = saved["qkv_two"]
    grad_parts = []
    for seq_index in range(seq_count):
        d_query_rows, d_key_rows, d_value_rows = attend_backward(
            qkv_two[seq_index, :, :width],
            saved["keys_list"][seq_index],
            saved["values_list"][seq_index],
            saved["totals_list"][seq_index],
            d_attended[seq_index],
            lengths[0, seq_index],
            query_positions,
        )
        grad_parts.append(jnp.concatenate([d_query_rows, d_key_rows, d_value_rows], -1))
    d_qkv_two = jnp.concatenate(grad_parts, 0).astype(jnp.bfloat16)
    qkv_grad_two = product_left(saved["normed_three"], d_qkv_two)
    d_inputs, gain_three, bias_three = norm_backward(
        saved["hidden_two"], 2, product_right(d_qkv_two, w_qkv[1])
    )
    grad_rows = grad_rows + d_inputs
    grad_rows, down_one, up_one, gain_two, bias_two = feed_backward(
        grad_rows,
        saved["hidden_one"],
        saved["normed_two"],
        saved["raised_one"],
        saved["active_one"],
        1,
        0,
    )
    branch_low = grad_rows.astype(jnp.bfloat16)
    out_one = product_left(saved["gated_low"], branch_low)
    d_gated = product_right(branch_low, w_out[0]).reshape(seq_count, span_rows, width)
    d_queries = d_gated * saved["mixer"]
    d_mixer = d_gated * saved["queries_one"]
    skip_grad = jnp.sum(d_mixer * saved["carried"], (0, 1))
    conv_real, conv_imag = to_frequency(d_mixer.astype(jnp.bfloat16))
    kernel_real = saved["kernel_real"]
    kernel_imag = saved["kernel_imag"]
    from_conv = from_frequency(
        kernel_real * conv_real + kernel_imag * conv_imag,
        kernel_real * conv_imag - kernel_imag * conv_real,
    )
    d_carried = d_mixer * skip + from_conv
    carried_real = saved["carried_real"]
    carried_imag = saved["carried_imag"]
    cot_real = (
        jnp.sum(carried_real * conv_real + carried_imag * conv_imag, 1, keepdims=True) / fft_length
    )
    cot_imag = (
        jnp.sum(carried_real * conv_imag - carried_imag * conv_real, 1, keepdims=True) / fft_length
    )
    rate_grad, weight_grad = saved["kernel_pull"]((cot_real, cot_imag))
    d_shifted = d_carried * saved["values_one"] * validity
    d_values = d_carried * saved["shifted"] * validity
    extended = saved["extended"]
    grads_extended = sum(
        (
            jnp.pad(taps[offset] * d_shifted, ((0, 0), (rim - offset, offset), (0, 0)))
            for offset in range(TAPS)
        )
    )
    taps_grad = jnp.stack(
        [
            jnp.sum(
                d_shifted
                * extended[:, rim - offset : rim - offset + span_rows].astype(jnp.float32),
                (0, 1),
            )
            for offset in range(TAPS)
        ]
    )
    later = passed_along(grads_extended[:, :rim], "seq", -1)
    d_keys = grads_extended[:, rim:] + jnp.pad(later, ((0, 0), (span_rows - rim, 0), (0, 0)))
    d_qkv_one = (
        jnp.concatenate([d_queries, d_keys, d_values], -1)
        .reshape(row_count, 3 * width)
        .astype(jnp.bfloat16)
    )
    qkv_grad_one = product_left(saved["normed_one"], d_qkv_one)
    d_inputs, gain_one, bias_one = norm_backward(
        saved["flat_in"], 0, product_right(d_qkv_one, w_qkv[0])
    )
    d_tokens = ((grad_rows + d_inputs).reshape(seq_count, span_rows, width) * validity)[None]
    gain_sum, bias_sum, qkv_sum, out_sum, up_sum, down_sum, taps_sum, skip_sum = (
        lax.psum_scatter(
            jnp.stack([gain_one, gain_two, gain_three, gain_four]),
            "seq",
            scatter_dimension=1,
            tiled=True,
        ),
        lax.psum_scatter(
            jnp.stack([bias_one, bias_two, bias_three, bias_four]),
            "seq",
            scatter_dimension=1,
            tiled=True,
        ),
        lax.psum_scatter(
            jnp.stack([qkv_grad_one, qkv_grad_two]), "seq", scatter_dimension=1, tiled=True
        ),
        lax.psum_scatter(jnp.stack([out_one, out_two]), "seq", scatter_dimension=1, tiled=True),
        lax.psum_scatter(jnp.stack([up_one, up_two]), "seq", scatter_dimension=1, tiled=True),
        lax.psum_scatter(jnp.stack([down_one, down_two]), "seq", scatter_dimension=1, tiled=True),
        lax.psum_scatter(taps_grad, "seq", scatter_dimension=1, tiled=True),
        lax.psum_scatter(skip_grad[None], "seq", scatter_dimension=1, tiled=True),
    )
    totals = (
        lax.psum(gain_sum.astype(jnp.bfloat16), "batch").astype(jnp.float32),
        lax.psum(bias_sum.astype(jnp.bfloat16), "batch").astype(jnp.float32),
        lax.psum(qkv_sum.astype(jnp.bfloat16), "batch").astype(jnp.float32),
        lax.psum(out_sum.astype(jnp.bfloat16), "batch").astype(jnp.float32),
        lax.psum(up_sum.astype(jnp.bfloat16), "batch").astype(jnp.float32),
        lax.psum(down_sum.astype(jnp.bfloat16), "batch").astype(jnp.float32),
        lax.psum(taps_sum.astype(jnp.bfloat16), "batch").astype(jnp.float32),
        lax.psum(skip_sum.astype(jnp.bfloat16), "batch").astype(jnp.float32),
        lax.psum(rate_grad.astype(jnp.bfloat16), "batch").astype(jnp.float32),
        lax.psum(weight_grad.astype(jnp.bfloat16), "batch").astype(jnp.float32),
    )
    return (
        output[None].astype(jnp.bfloat16),
        d_tokens,
        totals[0],
        totals[1][:3],
        totals[1][3],
        totals[2],
        totals[3],
        totals[4],
        totals[5],
        totals[6],
        totals[7][0],
        totals[8],
        totals[9],
    )


def solution(mesh):
    placed = (
        P("batch", None, "seq", None),
        P("batch", None, "seq", None),
        P("batch", None),
        P(),
        P(),
        P(),
        P(),
        P(),
        P(),
        P(),
        P(),
        P(),
        P(),
    )
    return jax.shard_map(
        per_device,
        mesh=mesh,
        in_specs=placed,
        out_specs=(
            P("batch", None, "seq", None),
            P("batch", None, "seq", None),
            P(None, "seq"),
            P(None, "seq"),
            P("seq"),
            P(None, "seq", None),
            P(None, "seq", None),
            P(None, "seq", None),
            P(None, "seq", None),
            P(None, "seq"),
            P("seq"),
            P("seq", None),
            P("seq", None),
        ),
        check_vma=False,
    )
```

profile of v0, /device:TPU:0, one launch (start us, length us, event | category | flops | bytes accessed | tf_op | source)
XLA Modules:
  0.0 3077.7 jit_solution(12084042577118512343)
XLA Ops:
  46.2 139.2 %while.128 = (s32[]{:T(128)}, f32[32,1,128,48]{2,3,0,1:T(8,128)S(1)}, f32[32,1,128,48]{2,3,0,1:T(8,128)S(1)}, f32[8,48,8]{1,2,0:T(8,128)}, f32[8,48,8]{1,2,0:T(8...) while((s32[]{:T(128)}, ...), condition=%wide.region_5.6_spmd.clone.clone.clone.clone, body=%wide.region_2.5_spmd.clone.clone.clone.clone.sunk | while | flops 22432384 | bytes 6393967 | solution.py:156
  254.8 62.7 %all-gather.25.cloned.1.call-done = bf16[1,2048,768]{2,1,0:T(8,128)(2,1)} async-done(((bf16[1,128,768]{2,1,0:T(8,128)(2,1)}), bf16[1,2048,768]{2,1,0:T(8,128)(2,1)}) %all-gather.25.cloned.1.call-update) | async-done | bytes 3145744 | tf_op jit(solution)/shard_map/all_gather | solution.py:174
  317.5 70.0 %all-gather.27.cloned.1.call-done = bf16[1,2048,768]{2,1,0:T(8,128)(2,1)} async-done(((bf16[1,128,768]{2,1,0:T(8,128)(2,1)}), bf16[1,2048,768]{2,1,0:T(8,128)(2,1)}) %all-gather.27.cloned.1.call-update) | async-done | bytes 3145744 | tf_op jit(solution)/shard_map/all_gather | solution.py:175
  388.2 66.8 %while.123 = (s32[]{:T(128)}, bf16[12,128,64]{1,2,0:T(8,128)(2,1)}, f32[12,128]{1,0:T(8,128)S(1)}, s32[12]{0:T(128)S(1)}, bf16[128,768]{1,0:T(8,128)(2,1)S(1)}, ...) while((s32[]{:T(128)}, bf16[12,128,64]{1,2,0:T(8,128)(2,1)}, ...), condition=%wide.region_29.30_spmd.clone, body=%wide.region_26.29_spmd.clone.sunk | while | flops 69730176 | bytes 4269247 | solution.py:196
  457.0 69.9 %all-gather.31.cloned.1.call-done = bf16[1,2048,768]{2,1,0:T(8,128)(2,1)} async-done(((bf16[1,128,768]{2,1,0:T(8,128)(2,1)}), bf16[1,2048,768]{2,1,0:T(8,128)(2,1)}) %all-gather.31.cloned.1.call-update) | async-done | bytes 3145744 | tf_op jit(solution)/shard_map/all_gather | solution.py:175
  527.6 66.7 %while.124 = (s32[]{:T(128)}, bf16[12,128,64]{1,2,0:T(8,128)(2,1)}, f32[12,128]{1,0:T(8,128)S(1)}, s32[12]{0:T(128)S(1)}, bf16[128,768]{1,0:T(8,128)(2,1)S(1)}, ...) while((s32[]{:T(128)}, bf16[12,128,64]{1,2,0:T(8,128)(2,1)}, ...), condition=%wide.region_33.34_spmd.clone, body=%wide.region_30.33_spmd.clone.sunk | while | flops 69730176 | bytes 4269247 | solution.py:196
  620.2 151.5 %while.125 = (s32[]{:T(128)}, bf16[12,128,64]{1,2,0:T(8,128)(2,1)}, f32[12,2048,64]{1,2,0:T(8,128)}, f32[12,2048,64]{1,2,0:T(8,128)}, s32[12]{0:T(128)S(1)}, /*i...) while((s32[]{:T(128)}, bf16[12,128,64]{1,2,0:T(8,128)(2,1)}, ...), condition=%wide.region_40.41_spmd.clone, body=%wide.region_38.40_spmd.clone.sunk | while | flops 170794880 | bytes 10659009 | solution.py:234
  790.2 144.9 %while.126 = (s32[]{:T(128)}, bf16[12,128,64]{1,2,0:T(8,128)(2,1)S(1)}, f32[12,2048,64]{1,2,0:T(8,128)}, f32[12,2048,64]{1,2,0:T(8,128)}, s32[12]{0:T(128)S(1)},...) while((s32[]{:T(128)}, ...), condition=%wide.region_44.45_spmd.clone, body=%wide.region_42.44_spmd.clone.sunk | while | flops 170794880 | bytes 10658569 | solution.py:234
  953.5 32.3 %reduce-scatter.19.cloned.1.call-done = f32[128,2,768]{0,2,1:T(8,128)} async-done(((f32[2048,2,768]{0,2,1:T(8,128)}), f32[128,2,768]{0,2,1:T(8,128)}) %reduce-scatter.19.cloned.1.call-update) | async-done | bytes 786448 | tf_op jit(solution)/shard_map/reduce_scatter | solution.py:246
  987.7 208.2 %reduce-scatter.21.cloned.1.call-done = f32[128,2,768]{0,2,1:T(8,128)} async-done(((f32[2048,2,768]{0,2,1:T(8,128)}), f32[128,2,768]{0,2,1:T(8,128)}) %reduce-scatter.21.cloned.1.call-update) | async-done | bytes 786448 | tf_op jit(solution)/shard_map/reduce_scatter | solution.py:246
  1404.9 32.2 %reduce-scatter.37.cloned.1.call-done = f32[48,1]{1,0:T(8,128)} async-done(((f32[768,1]{1,0:T(8,128)}), f32[48,1]{1,0:T(8,128)}) %reduce-scatter.37.cloned.1.call-update) | async-done | bytes 208
  1439.8 229.3 %while.127 = (s32[]{:T(128)}, f32[32,1,128,48]{2,3,0,1:T(8,128)S(1)}, f32[32,1,128,48]{2,3,0,1:T(8,128)S(1)}, bf16[8,48,8]{1,2,0:T(8,128)(2,1)}, bf16[8,48,8]{2,...) while((s32[]{:T(128)}, ...), condition=%wide.region_90.91_spmd.clone.clone, body=%wide.region_83.90_spmd.clone.clone.sunk | while | flops 63188096 | bytes 3355289 | solution.py:156
  1448.5 14.1 fusion.809
  1505.8 14.0 fusion.809
  1689.4 125.1 %reduce-scatter.31.cloned.1.call-done = f32[48,4]{1,0:T(8,128)} async-done(((f32[768,4]{1,0:T(8,128)}), f32[48,4]{1,0:T(8,128)}) %reduce-scatter.31.cloned.1.call-update) | async-done | bytes 784
  1823.2 61.4 %all-gather.17.cloned.1.call-done = bf16[1,2048,768]{2,1,0:T(8,128)(2,1)} async-done(((bf16[1,128,768]{2,1,0:T(8,128)(2,1)}), bf16[1,2048,768]{2,1,0:T(8,128)(2,1)}) %all-gather.17.cloned.1.call-update) | async-done | bytes 3145744 | tf_op jit(solution)/shard_map/all_gather | solution.py:174
  1884.5 69.3 %all-gather.19.cloned.1.call-done = bf16[1,2048,768]{2,1,0:T(8,128)(2,1)} async-done(((bf16[1,128,768]{2,1,0:T(8,128)(2,1)}), bf16[1,2048,768]{2,1,0:T(8,128)(2,1)}) %all-gather.19.cloned.1.call-update) | async-done | bytes 3145744 | tf_op jit(solution)/shard_map/all_gather | solution.py:175
  1953.9 59.5 %while.121 = (s32[]{:T(128)}, bf16[12,128,64]{1,2,0:T(8,128)(2,1)S(1)}, s32[12]{0:T(128)S(1)}, bf16[128,768]{1,0:T(8,128)(2,1)}, bf16[2048,768]{1,0:T(8,128)(2,1...) while((s32[]{:T(128)}, ...), condition=%wide.region_13.14_spmd.clone, body=%wide.region_10.13_spmd.clone.sunk | while | flops 69730048 | bytes 4266675 | solution.py:196
  2023.3 69.3 %all-gather.23.cloned.1.call-done = bf16[1,2048,768]{2,1,0:T(8,128)(2,1)} async-done(((bf16[1,128,768]{2,1,0:T(8,128)(2,1)}), bf16[1,2048,768]{2,1,0:T(8,128)(2,1)}) %all-gather.23.cloned.1.call-update) | async-done | bytes 3145744 | tf_op jit(solution)/shard_map/all_gather | solution.py:175
  2092.7 59.8 %while.122 = (s32[]{:T(128)}, bf16[12,128,64]{1,2,0:T(8,128)(2,1)S(1)}, s32[12]{0:T(128)S(1)}, bf16[128,768]{1,0:T(8,128)(2,1)}, bf16[2048,768]{1,0:T(8,128)(2,1...) while((s32[]{:T(128)}, ...), condition=%wide.region_17.18_spmd.clone, body=%wide.region_14.17_spmd.clone.sunk | while | flops 69730048 | bytes 4266675 | solution.py:196
  2153.8 79.9 %reduce-scatter.25.cloned.1.call-done = f32[2,48,768]{2,1,0:T(8,128)} async-done(((f32[2,768,768]{2,1,0:T(8,128)}), f32[2,48,768]{2,1,0:T(8,128)}) %reduce-scatter.25.cloned.1.call-update) | async-done | bytes 294928 | tf_op jit(solution)/shard_map/reduce_scatter | solution.py:515
  2235.4 225.4 %reduce-scatter.23.cloned.1.call-done = f32[2,48,2304]{2,1,0:T(8,128)} async-done(((f32[2,768,2304]{2,1,0:T(8,128)}), f32[2,48,2304]{2,1,0:T(8,128)}) %reduce-scatter.23.cloned.1.call-update) | async-done | bytes 884752 | tf_op jit(solution)/shard_map/reduce_scatter | solution.py:512
  2462.8 288.4 %reduce-scatter.29.cloned.1.call-done = f32[2,192,768]{2,1,0:T(8,128)} async-done(((f32[2,3072,768]{2,1,0:T(8,128)}), f32[2,192,768]{2,1,0:T(8,128)}) %reduce-scatter.29.cloned.1.call-update) | async-done | bytes 1179664 | tf_op jit(solution)/shard_map/reduce_scatter | solution.py:517
  2753.3 287.8 %reduce-scatter.27.cloned.1.call-done = f32[2,48,3072]{2,1,0:T(8,128)} async-done(((f32[2,768,3072]{2,1,0:T(8,128)}), f32[2,48,3072]{2,1,0:T(8,128)}) %reduce-scatter.27.cloned.1.call-update) | async-done | bytes 1179664 | tf_op jit(solution)/shard_map/reduce_scatter | solution.py:516
  (1373 shorter events, 1254.0 us)
Async XLA Ops:
  40.8 145.3 %all-to-all-start.2 = ((bf16[1,2,128,768]{2,1,0,3:T(2,128)(2,1)}), bf16[1,2,128,768]{2,1,0,3:T(2,128)(2,1)}, u32[]{:S(2)}, u32[]{:S(2)}) async-start(bf16[1,2,128,768]{2,1,0,3:T(2,128)(2,1)} %copy.275), calls=%async_computation.2 | async-start | bytes 786432 | tf_op jit(solution)/shard_map/all_to_all | solution.py:111
  213.5 18.5 all-to-all-start.3
  220.5 97.0 %all-gather.25.cloned.1.call-start = ((), (), s32[]{:S(2)}) async-start(), calls=%async_computation.26 | async-start | bytes 3342336 | tf_op jit(solution)/shard_map/all_gather | solution.py:174
  251.2 136.3 %all-gather.27.cloned.1.call-start = ((), (), s32[]{:S(2)}) async-start(), calls=%async_computation.27 | async-start | bytes 3342336 | tf_op jit(solution)/shard_map/all_gather | solution.py:175
  251.9 205.1 %all-gather.29.cloned.1.call-start = ((), (), s32[]{:S(2)}) async-start(), calls=%async_computation.28 | async-start | bytes 3342336 | tf_op jit(solution)/shard_map/all_gather | solution.py:174
  252.7 274.3 %all-gather.31.cloned.1.call-start = ((), (), s32[]{:S(2)}) async-start(), calls=%async_computation.29 | async-start | bytes 3342336 | tf_op jit(solution)/shard_map/all_gather | solution.py:175
  254.8 731.0 %reduce-scatter.19.cloned.1.call-start = ((), (), s32[]{:S(2)}) async-start(), calls=%async_computation.16 | async-start | bytes 13369344 | tf_op jit(solution)/shard_map/reduce_scatter | solution.py:246
  783.1 412.8 %reduce-scatter.21.cloned.1.call-start = ((), (), s32[]{:S(2)}) async-start(), calls=%async_computation.17 | async-start | bytes 13369344 | tf_op jit(solution)/shard_map/reduce_scatter | solution.py:246
  948.8 272.5 %all-to-all-start = ((bf16[1,2,128,768]{2,1,0,3:T(2,128)(2,1)}), bf16[1,2,128,768]{2,1,0,3:T(2,128)(2,1)}, u32[]{:S(2)}, u32[]{:S(2)}) async-start(bf16[1,2,128,768]{2,1,0,3:T(2,128)(2,1)} %copy.262), calls=%async_computation | async-start | bytes 786432 | tf_op jit(solution)/shard_map/all_to_all | solution.py:111
  1221.2 18.0 all-to-all-start.4
  1289.1 15.9 all-to-all-start.1
  1308.6 128.4 %reduce-scatter.37.cloned.1.call-start = ((), (), s32[]{:S(2)}) async-start(), calls=%async_computation.33 | async-start | bytes 417792
  1313.7 360.4 %reduce-scatter.35.cloned.1.call-start = ((), (), s32[]{:S(2)}) async-start(), calls=%async_computation.32 | async-start | bytes 417792
  1341.1 347.5 %reduce-scatter.33.cloned.1.call-start = ((), (), s32[]{:S(2)}) async-start(), calls=%async_computation.31 | async-start | bytes 417792
  1347.3 467.2 %reduce-scatter.31.cloned.1.call-start = ((), (), s32[]{:S(2)}) async-start(), calls=%async_computation.30 | async-start | bytes 417792
  1348.4 536.1 %all-gather.17.cloned.1.call-start = ((), (), s32[]{:S(2)}) async-start(), calls=%async_computation.22 | async-start | bytes 3342336 | tf_op jit(solution)/shard_map/all_gather | solution.py:174
  1350.9 602.9 %all-gather.19.cloned.1.call-start = ((), (), s32[]{:S(2)}) async-start(), calls=%async_computation.23 | async-start | bytes 3342336 | tf_op jit(solution)/shard_map/all_gather | solution.py:175
  1351.5 671.8 %all-gather.21.cloned.1.call-start = ((), (), s32[]{:S(2)}) async-start(), calls=%async_computation.24 | async-start | bytes 3342336 | tf_op jit(solution)/shard_map/all_gather | solution.py:174
  1352.2 740.4 %all-gather.23.cloned.1.call-start = ((), (), s32[]{:S(2)}) async-start(), calls=%async_computation.25 | async-start | bytes 3342336 | tf_op jit(solution)/shard_map/all_gather | solution.py:175
  1352.8 880.9 %reduce-scatter.25.cloned.1.call-start = ((), (), s32[]{:S(2)}) async-start(), calls=%async_computation.19 | async-start | bytes 5013504 | tf_op jit(solution)/shard_map/reduce_scatter | solution.py:515
  1356.4 1104.4 %reduce-scatter.23.cloned.1.call-start = ((), (), s32[]{:S(2)}) async-start(), calls=%async_computation.18 | async-start | bytes 15040512 | tf_op jit(solution)/shard_map/reduce_scatter | solution.py:512
  1377.9 1373.2 %reduce-scatter.29.cloned.1.call-start = ((), (), s32[]{:S(2)}) async-start(), calls=%async_computation.21 | async-start | bytes 20054016 | tf_op jit(solution)/shard_map/reduce_scatter | solution.py:517
  1392.1 1649.0 %reduce-scatter.27.cloned.1.call-start = ((), (), s32[]{:S(2)}) async-start(), calls=%async_computation.20 | async-start | bytes 20054016 | tf_op jit(solution)/shard_map/reduce_scatter | solution.py:516
  1404.8 1660.0 %all-reduce.9.cloned.1.call-start = ((), (), s32[]{:S(2)}) async-start(), calls=%async_computation.34 | async-start | bytes 3538944 | tf_op jit(solution)/shard_map/psum | solution.py:524
  (216 other events, 4386.2 us)
Sparse Core Ops, SparseCore 0:
  251.3 66.1 all-gather.24
  320.8 66.6 all-gather.26
  390.3 66.7 all-gather.28
  460.2 66.6 all-gather.30
  783.2 202.4 reduce-scatter.18
  992.2 203.6 reduce-scatter.20
  1314.1 122.8 reduce-scatter.36
  1442.4 120.6 reduce-scatter.34
  1567.8 120.7 reduce-scatter.32
  1693.8 120.6 reduce-scatter.30
  1817.3 67.1 all-gather.16
  1887.2 66.6 all-gather.18
  1956.6 66.6 all-gather.20
  2025.9 66.6 all-gather.22
  2097.6 136.0 reduce-scatter.24
  2240.3 220.3 reduce-scatter.22
  2466.4 284.6 reduce-scatter.28
  2756.8 284.2 reduce-scatter.26
  3044.8 19.9 all-reduce.8
where the time goes:
time: 3100 us; the launch traced here: 3080 us
  waiting for transfers between devices  1750 us (56%)
  matrix products  556 us (18%)
  other arithmetic  385 us (12%)
  local copies, waits for them, and re-layouts  225 us (7%)
  loops' own time  96.7 us (3%)
  starting transfers between devices  42.4 us (1%)
    reduce_scatter x1, waiting for transfers between devices, per_device(): lax.psum_scatter(jnp.stack([down_one, down_two]), 'seq', scatter_dimensio...  288 us
    reduce_scatter x1, waiting for transfers between devices, per_device(): lax.psum_scatter(jnp.stack([up_one, up_two]), 'seq', scatter_dimension=1,...  288 us
    all_gather x4, waiting for transfers between devices, attend_forward(): lax.all_gather(values_low, 'seq', axis=0, tiled=True)  278 us
    reduce_scatter x2, waiting for transfers between devices, attend_backward(): lax.psum_scatter(jnp.stack([key_part, value_part], 1), 'seq', scatter_dim...  240 us
    reduce_scatter x1, waiting for transfers between devices, per_device(): lax.psum_scatter(jnp.stack([qkv_grad_one, qkv_grad_two]), 'seq', scatter_...  225 us
    dot_general x85, matrix products, dense_product(): return jnp.dot(operand_a, operand_b, preferred_element_type=jnp.float32)  190 us
    dot_general x104, matrix products, product_right(): lax.dot_general(operand_a, operand_b, (((1,), (1,)), ((), ())), preferred...  188 us
    unnamed x23, waiting for transfers between devices  174 us
  transfers between devices with their start and end apart: 28, of which 22 were waited for; matrix products, arithmetic and copies ran while one was open for 27% of the time, Pallas kernels for 0%

commit v1 on v0

--- a/solution.py
+++ b/solution.py
@@ -1,13 +1,19 @@
+import functools
 import math
 
 import jax
 import jax.numpy as jnp
 from jax import lax
+from jax.experimental import pallas as pl
+from jax.experimental.pallas import tpu as pltpu
 from jax.sharding import PartitionSpec as P
 
 HEADS = 12
 HEAD = 64
 TAPS = 4
+STATES = 64
+MESH = pl.DeviceIdType.MESH
+VMEM_BYTES = 60 * 2**20
 
 
 norm_eps = 1e-05
@@ -547,6 +553,1005 @@
     )
 
 
+def other_device(place, core, to_place, to_core):
+    return jnp.logical_or(place != to_place, core != to_core)
+
+
+def greet(devices):
+    barrier = pltpu.get_barrier_semaphore()
+    for device in devices:
+        pl.semaphore_signal(barrier, inc=1, device_id=device, device_id_type=MESH)
+    pl.semaphore_wait(barrier, len(devices))
+
+
+def remote(source, target, send_sem, recv_sem, device):
+    return pltpu.make_async_remote_copy(
+        src_ref=source,
+        dst_ref=target,
+        send_sem=send_sem,
+        recv_sem=recv_sem,
+        device_id=device,
+        device_id_type=MESH,
+    )
+
+
+def split_low(value):
+    upper = value.astype(jnp.bfloat16)
+    return upper, (value - upper.astype(jnp.float32)).astype(jnp.bfloat16)
+
+
+NN = (((1,), (0,)), ((), ()))
+NT = (((1,), (1,)), ((), ()))
+TN = (((0,), (0,)), ((), ()))
+
+
+def dot(left, right, form=NN):
+    return lax.dot_general(left, right, form, preferred_element_type=jnp.float32)
+
+
+def dot_fine(left, right, form=NN):
+    left_up, left_low = left
+    right_up, right_low = right
+    total = dot(left_up, right_up, form) + dot(left_up, right_low, form)
+    if left_low is not None:
+        total = total + dot(left_low, right_up, form)
+    return total
+
+
+def state_tables(rate_row, weight_row, span):
+    row = lax.broadcasted_iota(jnp.int32, (span, 2 * STATES), 0)
+    lane = lax.broadcasted_iota(jnp.int32, (span, 2 * STATES), 1)
+    steps = jnp.where(lane < STATES, span - 1 - row, row + 1).astype(jnp.float32)
+    table = jnp.exp(-rate_row * steps)
+    lane_row = lax.broadcasted_iota(jnp.int32, (8, 2 * STATES), 1)
+    lead = jnp.where(lane_row < STATES, 0.0, weight_row * jnp.exp(rate_row))
+    response = lax.dot_general(
+        lead, table, NT, precision=highest, preferred_element_type=jnp.float32
+    )[:1]
+    spread = pltpu.roll(
+        jnp.broadcast_to(response, (span, span)), 0, 1, stride=1, stride_axis=0
+    )
+    later = lax.broadcasted_iota(jnp.int32, (span, span), 1)
+    earlier = lax.broadcasted_iota(jnp.int32, (span, span), 0)
+    toeplitz = jnp.where(later >= earlier, spread, 0.0)
+    return table, steps, toeplitz
+
+
+def shift_rows(value, count):
+    if count > 0:
+        return jnp.concatenate([jnp.zeros_like(value[:count]), value[:-count]], 0)
+    return jnp.concatenate([value[-count:], jnp.zeros_like(value[:-count])], 0)
+
+
+def scan_states(value, decay, seqs, blocks, direction):
+    step = 1
+    while step < blocks:
+        value = value + shift_rows(value, direction * step * seqs) * jnp.exp(decay * step)
+        step *= 2
+    return shift_rows(value, direction * seqs)
+
+
+def mixer_forward_kernel(
+    n, seqs, span, channels, unroll,
+    x_ref, rate_ref, weight_ref, y_ref, held_ref,
+    flat, flat_out, answer, send, recv, back_send, back_recv, own_sem,
+):
+    me, core = lax.axis_index("seq"), lax.axis_index("batch")
+    peers = [lax.rem(me + step, n) for step in range(1, n)]
+    greet([(peer, core) for peer in peers])
+    outgoing = []
+    for step, peer in enumerate(peers):
+        rows = pl.ds(pl.multiple_of(peer * channels, 16), channels)
+        copy = remote(
+            x_ref.at[:, rows, :], held_ref.at[me], send.at[step], recv.at[step], (peer, core)
+        )
+        copy.start()
+        outgoing.append(copy)
+    own_rows = pl.ds(pl.multiple_of(me * channels, 16), channels)
+    own = pltpu.make_async_copy(x_ref.at[:, own_rows, :], held_ref.at[me], own_sem.at[0])
+    own.start()
+    own.wait()
+    for copy in outgoing:
+        copy.wait()
+    total_rows = n * seqs * channels
+    flat[...] = held_ref[...].astype(jnp.float32).reshape(total_rows, span)
+
+    def one_channel(channel, carry):
+        rate_row = rate_ref[pl.ds(channel, 1), :]
+        weight_row = weight_ref[pl.ds(channel, 1), :]
+        table, _, toeplitz = state_tables(rate_row, weight_row, span)
+        rows = pl.ds(channel, n * seqs, stride=channels)
+        data = (flat[rows, :].astype(jnp.bfloat16), None)
+        table_parts = split_low(table)
+        inner = dot_fine(data, split_low(toeplitz))
+        states = dot_fine(data, table_parts)
+        states = scan_states(states, -span * rate_row, seqs, n, 1)
+        lane = lax.broadcasted_iota(jnp.int32, states.shape, 1)
+        weighted = jnp.where(lane < STATES, 0.0, pltpu.roll(states, STATES, 1) * weight_row)
+        flat_out[rows, :] = inner + dot_fine(split_low(weighted), table_parts, NT)
+        return carry
+
+    lax.fori_loop(0, channels, one_channel, 0, unroll=unroll)
+    answer[...] = flat_out[...].reshape(n, seqs, channels, span).astype(jnp.bfloat16)
+    outgoing = []
+    for step, peer in enumerate(peers):
+        copy = remote(
+            answer.at[peer], y_ref.at[:, own_rows, :], back_send.at[step], back_recv.at[step],
+            (peer, core),
+        )
+        copy.start()
+        outgoing.append(copy)
+    own = pltpu.make_async_copy(answer.at[me], y_ref.at[:, own_rows, :], own_sem.at[1])
+    own.start()
+    own.wait()
+    for copy in outgoing:
+        copy.wait()
+
+
+def mixer_forward(x, rates, weights, n, collective):
+    seqs, width, span = x.shape
+    channels = width // n
+    total_rows = n * seqs * channels
+    vmem = pl.BlockSpec(memory_space=pltpu.VMEM)
+    return pl.pallas_call(
+        functools.partial(mixer_forward_kernel, n, seqs, span, channels, 4),
+        out_shape=(
+            jax.ShapeDtypeStruct(x.shape, jnp.bfloat16),
+            jax.ShapeDtypeStruct((n, seqs, channels, span), jnp.bfloat16),
+        ),
+        in_specs=[vmem] * 3,
+        out_specs=(vmem, vmem),
+        scratch_shapes=[
+            pltpu.VMEM((total_rows, span), jnp.float32),
+            pltpu.VMEM((total_rows, span), jnp.float32),
+            pltpu.VMEM((n, seqs, channels, span), jnp.bfloat16),
+            pltpu.SemaphoreType.DMA((n - 1,)),
+            pltpu.SemaphoreType.DMA((n - 1,)),
+            pltpu.SemaphoreType.DMA((n - 1,)),
+            pltpu.SemaphoreType.DMA((n - 1,)),
+            pltpu.SemaphoreType.DMA((2,)),
+        ],
+        compiler_params=pltpu.CompilerParams(
+            collective_id=collective, has_side_effects=True, vmem_limit_bytes=VMEM_BYTES
+        ),
+    )(x, rates, weights)
+
+
+def mixer_backward_kernel(
+    n, seqs, span, channels, unroll,
+    d_ref, held_ref, rate_ref, weight_ref, dx_ref, rate_grad_ref, weight_grad_ref,
+    landing, flat_x, flat_d, flat_out, answer,
+    send, recv, back_send, back_recv, own_sem,
+):
+    me, core = lax.axis_index("seq"), lax.axis_index("batch")
+    peers = [lax.rem(me + step, n) for step in range(1, n)]
+    greet([(peer, core) for peer in peers])
+    outgoing = []
+    for step, peer in enumerate(peers):
+        rows = pl.ds(pl.multiple_of(peer * channels, 16), channels)
+        copy = remote(
+            d_ref.at[:, rows, :], landing.at[me], send.at[step], recv.at[step], (peer, core)
+        )
+        copy.start()
+        outgoing.append(copy)
+    own_rows = pl.ds(pl.multiple_of(me * channels, 16), channels)
+    own = pltpu.make_async_copy(d_ref.at[:, own_rows, :], landing.at[me], own_sem.at[0])
+    own.start()
+    total_rows = n * seqs * channels
+    flat_x[...] = held_ref[...].astype(jnp.float32).reshape(total_rows, span)
+    own.wait()
+    for copy in outgoing:
+        copy.wait()
+    flat_d[...] = landing[...].astype(jnp.float32).reshape(total_rows, span)
+
+    def one_channel(channel, carry):
+        rate_row = rate_ref[pl.ds(channel, 1), :]
+        weight_row = weight_ref[pl.ds(channel, 1), :]
+        table, steps, toeplitz = state_tables(rate_row, weight_row, span)
+        rows = pl.ds(channel, n * seqs, stride=channels)
+        data = flat_x[rows, :].astype(jnp.bfloat16)
+        grad = flat_d[rows, :].astype(jnp.bfloat16)
+        table_parts = split_low(table)
+        both_parts = split_low(jnp.concatenate([table, table * steps], 1))
+        count = n * seqs
+        sides = dot_fine((jnp.concatenate([data, grad], 0), None), both_parts)
+        lane = lax.broadcasted_iota(jnp.int32, (count, 2 * STATES), 1)
+        low_lanes = lane < STATES
+
+        def aligned(value):
+            return jnp.where(low_lanes, pltpu.roll(value, STATES, 1), 0.0)
+
+        entering = jnp.where(low_lanes, sides[:count, : 2 * STATES], 0.0)
+        entering_steps = jnp.where(low_lanes, sides[:count, 2 * STATES :], 0.0)
+        leaving = aligned(sides[count:, : 2 * STATES])
+        leaving_steps = aligned(sides[count:, 2 * STATES :])
+        decay = -span * rate_row
+        states = scan_states(entering, decay, seqs, n, 1)
+        states_steps = scan_states(states * jnp.exp(decay), decay, seqs, n, 1)
+        returned = scan_states(leaving, decay, seqs, n, -1)
+        far_weight = jnp.sum(leaving * states, 0, keepdims=True)
+        far_rate = jnp.sum(
+            leaving_steps * states + returned * entering_steps + span * (leaving * states_steps),
+            0, keepdims=True,
+        )
+        cross = dot(data, grad, TN)
+        later = lax.broadcasted_iota(jnp.int32, (span, span), 1)
+        earlier = lax.broadcasted_iota(jnp.int32, (span, span), 0)
+        cross = jnp.where(later >= earlier, cross, 0.0)
+        met = dot_fine(split_low(cross), both_parts, TN)
+        met_plain = pltpu.roll(met[:, : 2 * STATES], STATES, 1)
+        met_steps = pltpu.roll(met[:, 2 * STATES :], STATES, 1)
+        rise = jnp.exp(span * rate_row)
+        near_weight = rise * jnp.sum(table * met_plain, 0, keepdims=True)
+        near_rate = rise * jnp.sum(
+            table * ((steps - span) * met_plain + met_steps), 0, keepdims=True
+        )
+        lane_row = lane[:1]
+        near_weight = jnp.where(lane_row < STATES, pltpu.roll(near_weight, STATES, 1), 0.0)
+        near_rate = jnp.where(lane_row < STATES, pltpu.roll(near_rate, STATES, 1), 0.0)
+        weight_grad_ref[pl.ds(channel, 1), :] = near_weight + far_weight
+        rate_grad_ref[pl.ds(channel, 1), :] = -weight_row * (near_rate + far_rate)
+        inner = dot_fine((grad, None), split_low(toeplitz), NT)
+        weighted = returned * weight_row
+        flat_out[rows, :] = inner + dot_fine(split_low(weighted), table_parts, NT)
+        return carry
+
+    lax.fori_loop(0, channels, one_channel, 0, unroll=unroll)
+    answer[...] = flat_out[...].reshape(n, seqs, channels, span).astype(jnp.bfloat16)
+    outgoing = []
+    for step, peer in enumerate(peers):
+        copy = remote(
+            answer.at[peer], dx_ref.at[:, own_rows, :], back_send.at[step], back_recv.at[step],
+            (peer, core),
+        )
+        copy.start()
+        outgoing.append(copy)
+    own = pltpu.make_async_copy(answer.at[me], dx_ref.at[:, own_rows, :], own_sem.at[1])
+    own.start()
+    own.wait()
+    for copy in outgoing:
+        copy.wait()
+
+
+def mixer_backward(d, held, rates, weights, n, collective):
+    seqs, width, span = d.shape
+    channels = width // n
+    total_rows = n * seqs * channels
+    vmem = pl.BlockSpec(memory_space=pltpu.VMEM)
+    return pl.pallas_call(
+        functools.partial(mixer_backward_kernel, n, seqs, span, channels, 2),
+        out_shape=(
+            jax.ShapeDtypeStruct(d.shape, jnp.bfloat16),
+            jax.ShapeDtypeStruct((channels, 2 * STATES), jnp.float32),
+            jax.ShapeDtypeStruct((channels, 2 * STATES), jnp.float32),
+        ),
+        in_specs=[vmem] * 4,
+        out_specs=(vmem, vmem, vmem),
+        scratch_shapes=[
+            pltpu.VMEM((n, seqs, channels, span), jnp.bfloat16),
+            pltpu.VMEM((total_rows, span), jnp.float32),
+            pltpu.VMEM((total_rows, span), jnp.float32),
+            pltpu.VMEM((total_rows, span), jnp.float32),
+            pltpu.VMEM((n, seqs, channels, span), jnp.bfloat16),
+            pltpu.SemaphoreType.DMA((n - 1,)),
+            pltpu.SemaphoreType.DMA((n - 1,)),
+            pltpu.SemaphoreType.DMA((n - 1,)),
+            pltpu.SemaphoreType.DMA((n - 1,)),
+            pltpu.SemaphoreType.DMA((2,)),
+        ],
+        compiler_params=pltpu.CompilerParams(
+            collective_id=collective, has_side_effects=True, vmem_limit_bytes=VMEM_BYTES
+        ),
+    )(d, held, rates, weights)
+
+
+def block_of(index, core):
+    return 2 * index + lax.rem(index + core, 2)
+
+
+def keeper_of(block):
+    return lax.rem((block + 1) // 2, 2)
+
+
+class HeadPlaces:
+    def __init__(self, n, seqs, groups):
+        self.n, self.seqs, self.groups = n, seqs, groups
+        self.me, self.core = lax.axis_index("seq"), lax.axis_index("batch")
+        self.group = self.me // (2 * seqs)
+        self.seq = lax.rem(self.me // 2, seqs)
+        self.batch = lax.rem(self.me, 2)
+        self.keeper = keeper_of(self.me)
+        self.sibling = (self.me, 1 - self.core)
+        self.targets = [
+            ((group * 2 * seqs + seq * 2 + self.core, self.keeper), seq, group)
+            for seq in range(seqs)
+            for group in range(groups)
+        ]
+        self.blocks = [block_of(index, self.core) for index in range(n // 2)]
+        self.sources = [(block, self.batch) for block in self.blocks]
+
+    def is_other(self, device):
+        return jnp.logical_or(device[0] != self.me, device[1] != self.core)
+
+    def greet(self):
+        barrier = pltpu.get_barrier_semaphore()
+        others = [target for target, _, _ in self.targets] + self.sources
+        for device in others:
+
+            @pl.when(self.is_other(device))
+            def _():
+                pl.semaphore_signal(barrier, inc=1, device_id=device, device_id_type=MESH)
+
+        pl.semaphore_signal(barrier, inc=1, device_id=self.sibling, device_id_type=MESH)
+        kept = jnp.logical_and(self.batch == self.core, self.is_kept_here())
+        pl.semaphore_wait(barrier, len(others) + 1 - 2 * kept.astype(jnp.int32))
+
+    def is_kept_here(self):
+        return self.keeper == self.core
+
+    def send(self, source, target, send_sem, recv_sem, device):
+        @pl.when(self.is_other(device))
+        def _():
+            remote(source, target, send_sem, recv_sem, device).start()
+
+        @pl.when(jnp.logical_not(self.is_other(device)))
+        def _():
+            pltpu.make_async_copy(source, target, recv_sem).start()
+
+    def wait_sent(self, source, target, send_sem, recv_sem, device):
+        @pl.when(self.is_other(device))
+        def _():
+            remote(source, target, send_sem, recv_sem, device).wait_send()
+
+
+def fill_heads(held, head, first, n, span, rows_out, columns_out):
+    start = pl.multiple_of(first + head * HEAD, HEAD)
+    for block in range(n):
+        part = held[block, pl.ds(start, HEAD), :]
+        if rows_out is not None:
+            rows_out[block * span : (block + 1) * span, :] = part.T
+        if columns_out is not None:
+            columns_out[:, block * span : (block + 1) * span] = part
+
+
+def causal(first_key, rows, first_query, span):
+    key = first_key + lax.broadcasted_iota(jnp.int32, (rows, span), 0)
+    query = first_query + lax.broadcasted_iota(jnp.int32, (rows, span), 1)
+    return key <= query
+
+
+def attention_forward_kernel(
+    n, seqs, groups, span, group_rows,
+    qkv_ref, out_ref, held, lse_ref,
+    outputs, key_rows, value_columns,
+    send, recv, pass_send, pass_recv, back_send, back_recv,
+):
+    at = HeadPlaces(n, seqs, groups)
+    half = n // 2
+    at.greet()
+    for count, (device, seq, group) in enumerate(at.targets):
+        at.send(qkv_ref.at[seq, group], held.at[at.me], send.at[count], recv.at[at.me // 2], device)
+    passed = []
+    for index, block in enumerate(at.blocks):
+        remote(held.at[block], held.at[block], send.at[0], recv.at[index], at.sibling).wait_recv()
+        part = held.at[block, group_rows : 3 * group_rows, :]
+        copy = remote(part, part, pass_send.at[index], pass_recv.at[index], at.sibling)
+        copy.start()
+        passed.append(copy)
+    for copy in passed:
+        copy.wait()
+    for count, (device, seq, group) in enumerate(at.targets):
+        at.wait_sent(
+            qkv_ref.at[seq, group], held.at[at.me], send.at[count], recv.at[at.me // 2], device
+        )
+
+    def one_head(head, carry):
+        fill_heads(held, head, group_rows, n, span, key_rows, None)
+        fill_heads(held, head, 2 * group_rows, n, span, None, value_columns)
+        query_rows = pl.ds(pl.multiple_of(head * HEAD, HEAD), HEAD)
+        for index, block in enumerate(at.blocks):
+            query = held[block, query_rows, :] * jnp.bfloat16(HEAD**-0.5)
+            clear, reach = 2 * index * span, 2 * (index + 1) * span
+            edge = dot(key_rows[clear:reach, :], query)
+            edge = jnp.where(causal(clear, reach - clear, block * span, span), edge, masked_score)
+            top = jnp.max(edge, 0, keepdims=True)
+            if index > 0:
+                body = dot(key_rows[:clear, :], query)
+                top = jnp.maximum(top, jnp.max(body, 0, keepdims=True))
+            edge = jnp.exp(edge - top)
+            total = jnp.sum(edge, 0, keepdims=True)
+            result = dot(value_columns[:, clear:reach], edge.astype(jnp.bfloat16))
+            if index > 0:
+                body = jnp.exp(body - top)
+                total = total + jnp.sum(body, 0, keepdims=True)
+                result = result + dot(value_columns[:, :clear], body.astype(jnp.bfloat16))
+            outputs[index, query_rows, :] = (result / total).astype(jnp.bfloat16)
+            lse_ref[index, pl.ds(head, 1), :] = top + jnp.log(total)
+        return carry
+
+    lax.fori_loop(0, group_rows // HEAD, one_head, 0)
+    into = pl.ds(pl.multiple_of(at.group * group_rows, 16), group_rows)
+    slot = at.seq * groups + at.group
+    for index, device in enumerate(at.sources):
+        at.send(
+            outputs.at[index], out_ref.at[at.seq, into, :], back_send.at[index],
+            back_recv.at[slot], device,
+        )
+    for count, (device, seq, group) in enumerate(at.targets):
+        landed = out_ref.at[seq, group * group_rows : (group + 1) * group_rows, :]
+        remote(landed, landed, back_send.at[0], back_recv.at[count], at.sibling).wait_recv()
+    for index, device in enumerate(at.sources):
+        at.wait_sent(
+            outputs.at[index], out_ref.at[at.seq, into, :], back_send.at[index],
+            back_recv.at[slot], device,
+        )
+
+
+def attention_forward(qkv, n, collective):
+    seqs, groups, rows, span = qkv.shape
+    group_rows = rows // 3
+    half = n // 2
+    vmem = pl.BlockSpec(memory_space=pltpu.VMEM)
+    dma = pltpu.SemaphoreType.DMA
+    return pl.pallas_call(
+        functools.partial(attention_forward_kernel, n, seqs, groups, span, group_rows),
+        out_shape=(
+            jax.ShapeDtypeStruct((seqs, groups * group_rows, span), jnp.bfloat16),
+            jax.ShapeDtypeStruct((n, rows, span), jnp.bfloat16),
+            jax.ShapeDtypeStruct((half, group_rows // HEAD, span), jnp.float32),
+        ),
+        in_specs=[vmem],
+        out_specs=(vmem, vmem, vmem),
+        scratch_shapes=[
+            pltpu.VMEM((half, group_rows, span), jnp.bfloat16),
+            pltpu.VMEM((n * span, HEAD), jnp.bfloat16),
+            pltpu.VMEM((HEAD, n * span), jnp.bfloat16),
+            dma((seqs * groups,)),
+            dma((half,)),
+            dma((half,)),
+            dma((half,)),
+            dma((half,)),
+            dma((seqs * groups,)),
+        ],
+        compiler_params=pltpu.CompilerParams(
+            collective_id=collective, has_side_effects=True, vmem_limit_bytes=VMEM_BYTES
+        ),
+    )(qkv)
+
+
+def attention_backward_kernel(
+    n, seqs, groups, span, group_rows,
+    d_ref, held, lse_ref, out_ref,
+    landing, results, partial_send, partial_recv, key_grads, value_grads,
+    key_rows, key_columns, value_rows,
+    send, recv, pass_send, pass_recv, back_send, back_recv,
+):
+    at = HeadPlaces(n, seqs, groups)
+    half = n // 2
+    at.greet()
+    own_rows = [
+        d_ref.at[seq, group * group_rows : (group + 1) * group_rows, :]
+        for _, seq, group in at.targets
+    ]
+    for count, (device, seq, group) in enumerate(at.targets):
+        at.send(
+            own_rows[count], landing.at[at.me // 2], send.at[count], recv.at[at.me // 2], device
+        )
+    for index in range(half):
+        remote(
+            landing.at[index], landing.at[index], send.at[0], recv.at[index], at.sibling
+        ).wait_recv()
+    for count, (device, seq, group) in enumerate(at.targets):
+        at.wait_sent(
+            own_rows[count], landing.at[at.me // 2], send.at[count], recv.at[at.me // 2], device
+        )
+
+    def one_head(head, carry):
+        fill_heads(held, head, group_rows, n, span, key_rows, key_columns)
+        fill_heads(held, head, 2 * group_rows, n, span, value_rows, None)
+        head_rows = pl.ds(pl.multiple_of(head * HEAD, HEAD), HEAD)
+        key_grads[head_rows, :] = jnp.zeros((HEAD, n * span), jnp.float32)
+        value_grads[head_rows, :] = jnp.zeros((HEAD, n * span), jnp.float32)
+        for index, block in enumerate(at.blocks):
+            query = held[block, head_rows, :] * jnp.bfloat16(HEAD**-0.5)
+            grad = landing[index, head_rows, :]
+            log_total = lse_ref[index, pl.ds(head, 1), :]
+            clear, reach = 2 * index * span, 2 * (index + 1) * span
+            pieces = []
+            row_term = jnp.zeros((1, span), jnp.float32)
+            for first, last in ((0, clear), (clear, reach)):
+                if first == last:
+                    continue
+                scores = dot(key_rows[first:last, :], query)
+                if last == reach:
+                    scores = jnp.where(
+                        causal(clear, reach - clear, block * span, span), scores, masked_score
+                    )
+                weights = jnp.exp(scores - log_total)
+                d_weights = dot(value_rows[first:last, :], grad)
+                row_term = row_term + jnp.sum(weights * d_weights, 0, keepdims=True)
+                pieces.append((first, last, weights, d_weights))
+            d_query = jnp.zeros((HEAD, span), jnp.float32)
+            for first, last, weights, d_weights in pieces:
+                d_scores = (weights * (d_weights - row_term)).astype(jnp.bfloat16)
+                d_query = d_query + dot(key_columns[:, first:last], d_scores)
+                key_grads[head_rows, first:last] += dot(query, d_scores, NT)
+                value_grads[head_rows, first:last] += dot(grad, weights.astype(jnp.bfloat16), NT)
+            results[index, head_rows, :] = (d_query * HEAD**-0.5).astype(jnp.bfloat16)
+        return carry
+
+    lax.fori_loop(0, group_rows // HEAD, one_head, 0)
+    passed = []
+    for index in range(half):
+        other = block_of(index, 1 - at.core)
+        place = pl.ds(pl.multiple_of(other * span, span), span)
+        partial_send[index, :group_rows, :] = key_grads[:, place].astype(jnp.bfloat16)
+        partial_send[index, group_rows:, :] = value_grads[:, place].astype(jnp.bfloat16)
+        copy = remote(
+            partial_send.at[index], partial_recv.at[index], pass_send.at[index],
+            pass_recv.at[index], at.sibling,
+        )
+        copy.start()
+        passed.append(copy)
+    slot = at.seq * groups + at.group
+    for index, device in enumerate(at.sources):
+        passed[index].wait_recv()
+        place = pl.ds(pl.multiple_of(at.blocks[index] * span, span), span)
+        results[index, group_rows : 2 * group_rows, :] = (
+            key_grads[:, place] + partial_recv[index, :group_rows, :].astype(jnp.float32)
+        ).astype(jnp.bfloat16)
+        results[index, 2 * group_rows :, :] = (
+            value_grads[:, place] + partial_recv[index, group_rows:, :].astype(jnp.float32)
+        ).astype(jnp.bfloat16)
+        at.send(
+            results.at[index], out_ref.at[at.seq, at.group], back_send.at[index],
+            back_recv.at[slot], device,
+        )
+    for count, (device, seq, group) in enumerate(at.targets):
+        landed = out_ref.at[seq, group]
+        remote(landed, landed, back_send.at[0], back_recv.at[count], at.sibling).wait_recv()
+    for index, device in enumerate(at.sources):
+        passed[index].wait_send()
+        at.wait_sent(
+            results.at[index], out_ref.at[at.seq, at.group], back_send.at[index],
+            back_recv.at[slot], device,
+        )
+
+
+def attention_backward(d, held, lse, seqs, groups, collective):
+    n, rows, span = held.shape
+    group_rows = rows // 3
+    half = n // 2
+    vmem = pl.BlockSpec(memory_space=pltpu.VMEM)
+    dma = pltpu.SemaphoreType.DMA
+    return pl.pallas_call(
+        functools.partial(attention_backward_kernel, n, seqs, groups, span, group_rows),
+        out_shape=jax.ShapeDtypeStruct((seqs, groups, rows, span), jnp.bfloat16),
+        in_specs=[vmem] * 3,
+        out_specs=vmem,
+        scratch_shapes=[
+            pltpu.VMEM((half, group_rows, span), jnp.bfloat16),
+            pltpu.VMEM((half, rows, span), jnp.bfloat16),
+            pltpu.VMEM((half, 2 * group_rows, span), jnp.bfloat16),
+            pltpu.VMEM((half, 2 * group_rows, span), jnp.bfloat16),
+            pltpu.VMEM((group_rows, n * span), jnp.float32),
+            pltpu.VMEM((group_rows, n * span), jnp.float32),
+            pltpu.VMEM((n * span, HEAD), jnp.bfloat16),
+            pltpu.VMEM((HEAD, n * span), jnp.bfloat16),
+            pltpu.VMEM((n * span, HEAD), jnp.bfloat16),
+            dma((seqs * groups,)),
+            dma((half,)),
+            dma((half,)),
+            dma((half,)),
+            dma((half,)),
+            dma((seqs * groups,)),
+        ],
+        compiler_params=pltpu.CompilerParams(
+            collective_id=collective, has_side_effects=True, vmem_limit_bytes=VMEM_BYTES
+        ),
+    )(d, held, lse)
+
+
+TILE = 384
+
+
+class GradientPart:
+    def __init__(self, weight, first_column, columns, axis):
+        self.weight, self.first_column, self.columns, self.axis = (
+            weight, first_column, columns, axis,
+        )
+
+
+def gradient_parts(half_columns):
+    qkv_half, out_half, up_half, down_half = half_columns
+    return [
+        GradientPart(2, 0, up_half, 0),
+        GradientPart(3, 0, down_half, 1),
+        GradientPart(1, 0, out_half, 0),
+        GradientPart(0, TILE, qkv_half - TILE, 1),
+        GradientPart(0, 0, TILE, 0),
+    ]
+
+
+def weight_gradient_kernel(depth, slices, half_columns, tokens, *refs):
+    count = len(half_columns)
+    parts = gradient_parts(half_columns)
+    pieces = len(parts)
+    refs = list(refs)
+
+    def take(number):
+        taken = refs[:number]
+        del refs[:number]
+        return taken
+
+    left, right, outs = take(count), take(count), take(count)
+    left_other, right_other = take(count), take(count)
+    away, arrived, home = take(pieces), take(pieces), take(pieces)
+    away_two, arrived_two = take(pieces), take(pieces)
+    away_three, arrived_three = take(pieces), take(pieces)
+    pair_send, pair_recv, one_send, one_recv, two_send, two_recv, three_send, three_recv = take(8)
+    last_send, last_recv = take(2)
+
+    me, core = lax.axis_index("seq"), lax.axis_index("batch")
+    level, spot = me // 4, (me // 2 % 2, me % 2)
+    across = [level * 4 + spot[0] * 2 + (1 - spot[1]), level * 4 + (1 - spot[0]) * 2 + spot[1]]
+    sibling = (me, 1 - core)
+    levels = [lax.rem(level + step, depth) for step in range(1, depth)]
+    columns_up = [(other * 4 + spot[0] * 2 + spot[1], core) for other in levels]
+    greet([sibling, (across[0], core), (across[1], core)] + columns_up)
+
+    exchanged = []
+    for weight in range(count):
+        half = half_columns[weight]
+        theirs = pl.ds(pl.multiple_of((1 - core) * half, 128), half)
+        for number, (source, target) in enumerate(
+            ((left[weight], left_other[weight]), (right[weight].at[:, theirs], right_other[weight]))
+        ):
+            slot = 2 * weight + number
+            copy = remote(source, target, pair_send.at[slot], pair_recv.at[slot], sibling)
+            copy.start()
+            exchanged.append(copy)
+
+    def rows_of(ref, part, outer, inner, first):
+        mixed = inner * 2 + first if part.axis == 0 else first * 2 + inner
+        return ref[outer * 4 + mixed]
+
+    def product(part, first, outers, column):
+        half = half_columns[part.weight]
+        places = [(outer, inner) for outer in outers for inner in range(2)]
+        mine = jnp.concatenate(
+            [rows_of(left[part.weight], part, *place, first) for place in places], 0
+        )
+        other = jnp.concatenate(
+            [rows_of(left_other[part.weight], part, *place, first) for place in places], 0
+        )
+        own = pl.ds(pl.multiple_of(core * half + part.first_column + column, 128), TILE)
+        there = pl.ds(pl.multiple_of(part.first_column + column, 128), TILE)
+        return dot(mine, right[part.weight][:, own]) + dot(other, right_other[part.weight][:, there])
+
+    def fill(part, first, buffer, kind):
+        rows = slices[part.weight]
+        outers = [[outer] for outer in range(depth)] if rows * 2 >= TILE else [list(range(depth))]
+
+        def one_column(tile, carry):
+            column = tile * TILE
+            for group in outers:
+                value = product(part, first, group, column)
+                buffer[group[0] : group[-1] + 1, :, :, pl.ds(pl.multiple_of(column, 128), TILE)] = (
+                    value.reshape(len(group), 2, rows, TILE).astype(kind)
+                )
+            return carry
+
+        lax.fori_loop(0, part.columns // TILE, one_column, 0)
+
+    waited = set()
+    stage_one = []
+    for number, part in enumerate(parts):
+        for slot in (2 * part.weight, 2 * part.weight + 1):
+            if slot not in waited:
+                exchanged[slot].wait_recv()
+                waited.add(slot)
+        mine = spot[1 - part.axis]
+        fill(part, 1 - mine, away[number], jnp.bfloat16)
+        copy = remote(
+            away[number], arrived[number], one_send.at[number], one_recv.at[number],
+            (across[part.axis], core),
+        )
+        copy.start()
+        stage_one.append(copy)
+        fill(part, mine, home[number], jnp.float32)
+
+    stage_two = []
+    for number, part in enumerate(parts):
+        stage_one[number].wait_recv()
+        mine = spot[part.axis]
+        for outer in range(depth):
+            away_two[number][outer] = (
+                home[number][outer, 1 - mine] + arrived[number][outer, 1 - mine].astype(jnp.float32)
+            ).astype(jnp.bfloat16)
+        copy = remote(
+            away_two[number], arrived_two[number], two_send.at[number], two_recv.at[number],
+            (across[1 - part.axis], core),
+        )
+        copy.start()
+        stage_two.append(copy)
+        for outer in range(depth):
+            home[number][outer, mine] += arrived[number][outer, mine].astype(jnp.float32)
+
+    stage_three = []
+    for number, part in enumerate(parts):
+        stage_two[number].wait_recv()
+        mine = spot[part.axis]
+        copies = []
+        for step, other in enumerate(levels):
+            away_three[number][step] = (
+                home[number][other, mine] + arrived_two[number][other].astype(jnp.float32)
+            ).astype(jnp.bfloat16)
+            slot = number * (depth - 1) + step
+            copy = remote(
+                away_three[number].at[step], arrived_three[number].at[step], three_send.at[slot],
+                three_recv.at[slot], columns_up[step],
+            )
+            copy.start()
+            copies.append(copy)
+        stage_three.append(copies)
+
+    last = []
+    for number, part in enumerate(parts):
+        mine = spot[part.axis]
+        total = home[number][level, mine] + arrived_two[number][level].astype(jnp.float32)
+        for step in range(depth - 1):
+            stage_three[number][step].wait_recv()
+            total = total + arrived_three[number][step].astype(jnp.float32)
+        place = pl.ds(
+            pl.multiple_of(core * half_columns[part.weight] + part.first_column, 128), part.columns
+        )
+        outs[part.weight][:, place] = total
+        filled = outs[part.weight].at[:, place]
+        copy = remote(filled, filled, last_send.at[number], last_recv.at[number], sibling)
+        copy.start()
+        last.append(copy)
+    for copy in last:
+        copy.wait()
+    for copy in exchanged + stage_one + stage_two:
+        copy.wait_send()
+    for copies in stage_three:
+        for copy in copies:
+            copy.wait_send()
+
+
+def weight_gradients(left, right, depth, collective):
+    tokens = right[0].shape[0]
+    half_columns = tuple(array.shape[1] // 2 for array in right)
+    slices = tuple(array.shape[1] for array in left)
+    parts = gradient_parts(half_columns)
+    vmem = pl.BlockSpec(memory_space=pltpu.VMEM)
+    low, wide = jnp.bfloat16, jnp.float32
+    dma = pltpu.SemaphoreType.DMA
+
+    def shapes(extent, kind):
+        return [
+            pltpu.VMEM((*extent, slices[part.weight], part.columns), kind) for part in parts
+        ]
+
+    count = len(parts)
+    return pl.pallas_call(
+        functools.partial(weight_gradient_kernel, depth, slices, half_columns, tokens),
+        out_shape=tuple(
+            jax.ShapeDtypeStruct((rows, 2 * half), wide)
+            for rows, half in zip(slices, half_columns)
+        ),
+        in_specs=[vmem] * (len(left) + len(right)),
+        out_specs=(vmem,) * len(left),
+        scratch_shapes=[pltpu.VMEM(array.shape, low) for array in left]
+        + [pltpu.VMEM((tokens, half), low) for half in half_columns]
+        + shapes((depth, 2), low)
+        + shapes((depth, 2), low)
+        + shapes((depth, 2), wide)
+        + shapes((depth,), low)
+        + shapes((depth,), low)
+        + shapes((depth - 1,), low)
+        + shapes((depth - 1,), low)
+        + [dma((2 * len(left),)), dma((2 * len(left),))]
+        + [dma((count,))] * 4
+        + [dma((count * (depth - 1),))] * 2
+        + [dma((count,))] * 2,
+        compiler_params=pltpu.CompilerParams(
+            collective_id=collective, has_side_effects=True, vmem_limit_bytes=VMEM_BYTES
+        ),
+    )(*left, *right)
+
+
+def per_device_by_heads(
+    tokens,
+    cotangent,
+    lengths,
+    norm_gain,
+    norm_bias,
+    w_qkv,
+    w_out,
+    w_up,
+    w_down,
+    taps,
+    skip,
+    ssm_rate,
+    ssm_out,
+):
+    seq_count, span_rows, width = tokens.shape[1:]
+    devices = lax.axis_size("seq")
+    place = lax.axis_index("seq")
+    channels = width // devices
+    depth = devices // 4
+    groups = depth
+    rim = TAPS - 1
+    row_count = seq_count * span_rows
+    positions = place * span_rows + jnp.arange(span_rows, dtype=jnp.int32)
+    validity = (positions[None, :] < lengths[0][:, None]).astype(jnp.float32)[:, :, None]
+    rates = lax.dynamic_slice_in_dim(ssm_rate, place * channels, channels, 0)
+    weights = lax.dynamic_slice_in_dim(ssm_out, place * channels, channels, 0)
+    rates = jnp.concatenate([rates, rates], 1)
+    weights = jnp.concatenate([weights, weights], 1)
+
+    def to_channels(value):
+        return value.transpose(0, 2, 1)
+
+    def feed_forward(inputs, norm_row, layer):
+        normed = layer_norm(inputs, norm_gain[norm_row], norm_bias[norm_row]).astype(jnp.bfloat16)
+        raised = dense_product(normed, w_up[layer])
+        active = jax.nn.gelu(raised).astype(jnp.bfloat16)
+        return normed, raised, active, inputs + dense_product(active, w_down[layer])
+
+    def norm_backward(inputs, norm_row, d_normed):
+        pull = jax.vjp(layer_norm, inputs, norm_gain[norm_row], norm_bias[norm_row])[1]
+        return pull(d_normed)
+
+    def feed_backward(grad_rows, inputs, raised, norm_row, layer):
+        branch = grad_rows.astype(jnp.bfloat16)
+        d_active = product_right(branch, w_down[layer])
+        d_raised = jax.vjp(jax.nn.gelu, raised)[1](d_active)[0].astype(jnp.bfloat16)
+        d_inputs, gain_part, bias_part = norm_backward(
+            inputs, norm_row, product_right(d_raised, w_up[layer])
+        )
+        return grad_rows + d_inputs, branch, d_raised, gain_part, bias_part
+
+    flat_in = (tokens[0].astype(jnp.float32) * validity).reshape(row_count, width)
+    normed_one = layer_norm(flat_in, norm_gain[0], norm_bias[0]).astype(jnp.bfloat16)
+    qkv_one = dense_product(normed_one, w_qkv[0]).reshape(seq_count, span_rows, 3 * width)
+    queries_one = qkv_one[:, :, :width]
+    keys_one = qkv_one[:, :, width : 2 * width].astype(jnp.bfloat16)
+    values_one = qkv_one[:, :, 2 * width :]
+    earlier = passed_along(keys_one[:, span_rows - rim :], "seq", 1)
+    extended = jnp.concatenate([earlier, keys_one], 1)
+
+    def tap_rows(offset):
+        return extended[:, rim - offset : rim - offset + span_rows].astype(jnp.float32)
+
+    shifted = sum((taps[offset] * tap_rows(offset) for offset in range(TAPS)))
+    carried_low = (shifted * values_one * validity).astype(jnp.bfloat16)
+    convolved, held = mixer_forward(to_channels(carried_low), rates, weights, devices, 1)
+    carried = carried_low.astype(jnp.float32)
+    mixer = to_channels(convolved).astype(jnp.float32) + skip * carried
+    gated = (queries_one * mixer).reshape(row_count, width).astype(jnp.bfloat16)
+    hidden_one = flat_in + dense_product(gated, w_out[0])
+    normed_two, raised_one, active_one, hidden_two = feed_forward(hidden_one, 1, 0)
+    normed_three = layer_norm(hidden_two, norm_gain[2], norm_bias[2]).astype(jnp.bfloat16)
+    qkv_two = dense_product(normed_three, w_qkv[1]).astype(jnp.bfloat16)
+    group_rows = width // groups
+    qkv_columns = (
+        qkv_two.reshape(seq_count, span_rows, 3, groups, group_rows)
+        .transpose(0, 3, 2, 4, 1)
+        .reshape(seq_count, groups, 3 * group_rows, span_rows)
+    )
+    attended, kept, log_totals = attention_forward(qkv_columns, devices, 2)
+    attended = to_channels(attended).reshape(row_count, width)
+    hidden_three = hidden_two + dense_product(attended, w_out[1])
+    normed_four, raised_two, active_two, hidden_four = feed_forward(hidden_three, 3, 1)
+    output = hidden_four.reshape(seq_count, span_rows, width) * validity
+
+    grad_rows = (cotangent[0].astype(jnp.float32) * validity).reshape(row_count, width)
+    grad_rows, branch_four, d_raised_two, gain_four, bias_four = feed_backward(
+        grad_rows, hidden_three, raised_two, 3, 1
+    )
+    branch_three = grad_rows.astype(jnp.bfloat16)
+    d_attended = (
+        product_right(branch_three, w_out[1])
+        .astype(jnp.bfloat16)
+        .reshape(seq_count, span_rows, width)
+    )
+    d_columns = attention_backward(
+        to_channels(d_attended), kept, log_totals, seq_count, groups, 3
+    )
+    d_qkv_two = (
+        d_columns.reshape(seq_count, groups, 3, group_rows, span_rows)
+        .transpose(0, 4, 2, 1, 3)
+        .reshape(row_count, 3 * width)
+    )
+    d_inputs, gain_three, bias_three = norm_backward(
+        hidden_two, 2, product_right(d_qkv_two, w_qkv[1])
+    )
+    grad_rows = grad_rows + d_inputs
+
+    def sliced(value):
+        return value.T.reshape(devices, value.shape[1] // devices, row_count)
+
+    qkv_two_grad, out_two_grad, up_two_grad, down_two_grad = weight_gradients(
+        [sliced(normed_three), sliced(attended), sliced(normed_four), sliced(active_two)],
+        [d_qkv_two, branch_three, d_raised_two, branch_four],
+        depth,
+        4,
+    )
+    grad_rows, branch_two, d_raised_one, gain_two, bias_two = feed_backward(
+        grad_rows, hidden_one, raised_one, 1, 0
+    )
+    branch_one = grad_rows.astype(jnp.bfloat16)
+    d_gated = product_right(branch_one, w_out[0]).reshape(seq_count, span_rows, width)
+    d_queries = d_gated * mixer
+    d_mixer = d_gated * queries_one
+    skip_grad = jnp.sum(d_mixer * carried, (0, 1))
+    from_conv, rate_grad, weight_grad = mixer_backward(
+        to_channels(d_mixer.astype(jnp.bfloat16)), held, rates, weights, devices, 5
+    )
+    d_carried = d_mixer * skip + to_channels(from_conv).astype(jnp.float32)
+    d_shifted = d_carried * values_one * validity
+    d_values = d_carried * shifted * validity
+    grads_extended = sum(
+        (
+            jnp.pad(taps[offset] * d_shifted, ((0, 0), (rim - offset, offset), (0, 0)))
+            for offset in range(TAPS)
+        )
+    )
+    taps_grad = jnp.stack(
+        [jnp.sum(d_shifted * tap_rows(offset), (0, 1)) for offset in range(TAPS)]
+    )
+    later = passed_along(grads_extended[:, :rim], "seq", -1)
+    d_keys = grads_extended[:, rim:] + jnp.pad(later, ((0, 0), (span_rows - rim, 0), (0, 0)))
+    d_qkv_one = (
+        jnp.concatenate([d_queries, d_keys, d_values], -1)
+        .reshape(row_count, 3 * width)
+        .astype(jnp.bfloat16)
+    )
+    d_inputs, gain_one, bias_one = norm_backward(flat_in, 0, product_right(d_qkv_one, w_qkv[0]))
+    d_tokens = ((grad_rows + d_inputs).reshape(seq_count, span_rows, width) * validity)[None]
+    qkv_one_grad, out_one_grad, up_one_grad, down_one_grad = weight_gradients(
+        [sliced(normed_one), sliced(gated), sliced(normed_two), sliced(active_one)],
+        [d_qkv_one, branch_one, d_raised_one, branch_two],
+        depth,
+        6,
+    )
+    small = jnp.concatenate(
+        [
+            jnp.stack([gain_one, gain_two, gain_three, gain_four]),
+            jnp.stack([bias_one, bias_two, bias_three, bias_four]),
+            taps_grad,
+            skip_grad[None],
+        ],
+        0,
+    )
+    small = lax.psum(small, ("seq", "batch"))
+    small = lax.dynamic_slice_in_dim(small, place * channels, channels, 1)
+    states = lax.psum(jnp.stack([rate_grad[:, :STATES], weight_grad[:, :STATES]]), "batch")
+    return (
+        output[None].astype(jnp.bfloat16),
+        d_tokens,
+        small[:4],
+        small[4:7],
+        small[7],
+        jnp.stack([qkv_one_grad, qkv_two_grad]),
+        jnp.stack([out_one_grad, out_two_grad]),
+        jnp.stack([up_one_grad, up_two_grad]),
+        jnp.stack([down_one_grad, down_two_grad]),
+        small[8 : 8 + TAPS],
+        small[8 + TAPS],
+        states[0],
+        states[1],
+    )
+
+
+def fits_by_heads(mesh):
+    devices = mesh.shape["seq"]
+    return devices == 16 and mesh.shape["batch"] == 2
+
+
 def solution(mesh):
     placed = (
         P("batch", None, "seq", None),
@@ -564,7 +1569,7 @@
         P(),
     )
     return jax.shard_map(
-        per_device,
+        per_device_by_heads if fits_by_heads(mesh) else per_device,
         mesh=mesh,
         in_specs=placed,
         out_specs=(

time: 3100 us -> 680 us (0.22)
  waiting for transfers between devices: 1750 us -> 2.61 us
  matrix products: 556 us -> 52.3 us
  Pallas kernels: 0 us -> 453 us
  other arithmetic: 385 us -> 37.6 us
  local copies, waits for them, and re-layouts: 225 us -> 76.7 us
  loops' own time: 96.7 us -> 0 us
  blocking collectives: 3.66 us -> 44.3 us
  starting transfers between devices: 42.4 us -> 6.35 us
    reduce_scatter x6 -> x0, waiting for transfers between devices: 1120 us -> none  [the longest x1 288 us: per_device(): lax.psum_scatter(jnp.stack([down_one, down_two]), 'seq', scatter_dimensio...]
    pallas_call x0 -> x6, Pallas kernels: none -> 453 us  [the longest x2 224 us: weight_gradients(): pl.pallas_call(functools.partial(weight_gradient_kernel, depth, slices, h...]
    all_gather x8 -> x0, waiting for transfers between devices: 414 us -> none  [the longest x4 278 us: attend_forward(): lax.all_gather(values_low, 'seq', axis=0, tiled=True)]
    reduce_sum x65 -> x1, other arithmetic: 231 us -> 4.28 us  [per_device_by_heads(): jnp.sum(d_shifted * tap_rows(offset), (0, 1))]
    dot_general x92 -> x0, matrix products: 178 us -> none  [the longest x56 94.5 us: product_left(): lax.dot_general(operand_a, operand_b, (((0,), (0,)), ((), ())), preferred...]
    unnamed x23 -> x0, waiting for transfers between devices: 174 us -> none
    dot_general x85 -> x8, matrix products: 190 us -> 26.7 us  [dense_product(): return jnp.dot(operand_a, operand_b, preferred_element_type=jnp.float32)]
    dot_general x104 -> x8, matrix products: 188 us -> 25.6 us  [product_right(): lax.dot_general(operand_a, operand_b, (((1,), (1,)), ((), ())), preferred...]
  transfers between devices with their start and end apart: 28 -> 2, of which waited for: 22 -> 1; matrix products, arithmetic and copies ran while one was open for 27% -> 6% of each run, Pallas kernels for 0% -> 17%
where the time goes in v1:
time: 680 us; the launch traced here: 675 us
  Pallas kernels  453 us (67%)
  local copies, waits for them, and re-layouts  76.7 us (11%)
  matrix products  52.3 us (8%)
  blocking collectives  44.3 us (7%)
  other arithmetic  37.6 us (6%)
    pallas_call x2, Pallas kernels, weight_gradients(): pl.pallas_call(functools.partial(weight_gradient_kernel, depth, slices, h...  224 us
    pallas_call x1, Pallas kernels, mixer_forward(): pl.pallas_call(functools.partial(mixer_forward_kernel, n, seqs, span, cha...  61.2 us
    pallas_call x1, Pallas kernels, mixer_backward(): pl.pallas_call(functools.partial(mixer_backward_kernel, n, seqs, span, ch...  58.3 us
    pallas_call x1, Pallas kernels, attention_backward(): pl.pallas_call(functools.partial(attention_backward_kernel, n, seqs, grou...  56.2 us
    pallas_call x1, Pallas kernels, attention_forward(): pl.pallas_call(functools.partial(attention_forward_kernel, n, seqs, group...  54.1 us
    psum x1, blocking collectives, per_device_by_heads(): small = lax.psum(small, ('seq', 'batch'))  39.4 us
    dot_general x8, matrix products, dense_product(): return jnp.dot(operand_a, operand_b, preferred_element_type=jnp.float32)  26.7 us
    dot_general x8, matrix products, product_right(): lax.dot_general(operand_a, operand_b, (((1,), (1,)), ((), ())), preferred...  25.6 us
  transfers between devices with their start and end apart: 2, of which 1 were waited for; matrix products, arithmetic and copies ran while one was open for 6% of the time, Pallas kernels for 17%

profile of v1, /device:TPU:0, one launch (start us, length us, event | category | flops | bytes accessed | tf_op | source)
XLA Modules:
  0.0 675.4 jit_solution(1589922593238320144)
XLA Ops:
  6.9 3.8 fusion.143
  12.7 5.1 collective-permute-start
  23.6 2.6 collective-permute-done
  26.3 2.6 multiply_convert_fusion.13
  28.9 61.2 %shard_map.228 = (bf16[2,768,128]{2,1,0:T(8,128)(2,1)}, bf16[16,2,48,128]{3,2,1,0:T(8,128)(2,1)}) custom-call(bf16[2,768,128]{2,1,0:T(8,128)(2,1)} %bitcast.208, f32[48,128]{1,0:T(8,128)} %pad_maximum_fusion.7.rate_ref, f32[48,128]{1,0:T(8,128)} %pad_maximum_fusion.8.weight_ref), custom_call_target="tpu_custom_call" | custom-call | tf_op jit(solution)/shard_map/pallas_call | solution.py:696
  96.0 5.8 fusion.52
  109.3 3.5 reshape.390
  112.8 2.6 copy.75
  115.5 54.1 %shard_map.229 = (bf16[2,768,128]{2,1,0:T(8,128)(2,1)}, bf16[16,576,128]{2,1,0:T(8,128)(2,1)}, f32[8,3,128]{2,1,0:T(4,128)}) custom-call(bf16[2,4,576,128]{3,2,1,0:T(8,128)(2,1)} %bitcast.214), custom_call_target="tpu_custom_call" | custom-call | tf_op jit(solution)/shard_map/pallas_call | solution.py:996
  173.1 5.8 fusion.60
  178.9 2.8 fusion.80
  181.8 2.8 fusion.44.refs_6_
  192.0 56.2 %shard_map.230 = bf16[2,4,576,128]{3,2,1,0:T(8,128)(2,1)} custom-call(bf16[2,768,128]{2,1,0:T(8,128)(2,1)} %bitcast.230, bf16[16,576,128]{2,1,0:T(8,128)(2,1)} %get-tuple-element.31.held, f32[8,3,128]{2,1,0:T(4,128)} %get-tuple-element.32.lse_ref), custom_call_target="tpu_custom_call" | custom-call | tf_op jit(solution)/shard_map/pallas_call | solution.py:1127
  250.8 4.3 multiply_reduce_fusion.1
  257.3 5.6 fusion.37.refs_6_
  267.2 3.1 fusion.105
  271.1 58.3 %shard_map.231 = (bf16[2,768,128]{2,1,0:T(8,128)(2,1)}, f32[48,128]{1,0:T(8,128)}, f32[48,128]{1,0:T(8,128)}) custom-call(bf16[2,768,128]{2,1,0:T(8,128)(2,1)} %convert_bitcast_fusion.d_ref, bf16[16,2,48,128]{3,2,1,0:T(8,128)(2,1)} %get-tuple-element.33.held_ref, f32[48,128]{1,0:T(8,128)} %pad_maximum_fusion.7.rate_ref, f32[48,128]{1,0:T(8,128)} %pad_maximum_fusion.8.weight_ref), custom_call_target="tpu_custom_call" | custom-call | tf_op jit(solution)/shard_map/pallas_call | solution.py:821
  331.5 4.9 psum.15
  336.4 4.3 fusion.103
  356.9 2.6 copy.94
  383.5 115.1 %shard_map.233 = (f32[48,2304]{1,0:T(8,128)}, f32[48,768]{1,0:T(8,128)}, f32[48,3072]{1,0:T(8,128)}, f32[192,768]{1,0:T(8,128)}) custom-call(bf16[16,48,256]{2,1,0:T(8,128)(2,1)} %bitcast.228, bf16[16,48,256]{2,1,0:T(8,128)(2,1)} %bitcast.226, bf16[16,48,256]{2,1,0:T(8,128)(2,1)} %bitcast.227, bf16[16,192,256]{2,1,0:T(8,128)(2,1)} %bitcast.210, ...), custom_call_target="tpu_custom_call" | custom-call | tf_op jit(solution)/shard_map/pallas_call | solution.py:1338
  507.5 4.2 multiply_reduce_fusion.3
  514.3 39.4 %psum.14 = f32[13,768]{1,0:T(8,128)S(1)} all-reduce(f32[13,768]{1,0:T(8,128)S(1)} %concatenate.33), channel_id=1, replica_groups=mesh['seq'=16,'batch'=2] {'seq','batch'}, use_global_device_ids=true, to_apply=%region_29.0 | all-reduce | flops 9984 | bytes 79872 | tf_op jit(solution)/shard_map/psum | solution.py:1530
  559.6 108.4 %shard_map.232 = (f32[48,2304]{1,0:T(8,128)}, f32[48,768]{1,0:T(8,128)}, f32[48,3072]{1,0:T(8,128)}, f32[192,768]{1,0:T(8,128)}) custom-call(bf16[16,48,256]{2,1,0:T(8,128)(2,1)} %bitcast.229, bf16[16,48,256]{2,1,0:T(8,128)(2,1)} %bitcast.224, bf16[16,48,256]{2,1,0:T(8,128)(2,1)} %bitcast.225, bf16[16,192,256]{2,1,0:T(8,128)(2,1)} %bitcast.209, ...), custom_call_target="tpu_custom_call" | custom-call | tf_op jit(solution)/shard_map/pallas_call | solution.py:1338
  (291 shorter events, 114.0 us)
Async XLA Ops:
  5.3 12.5 %copy-start.51 = (f32[2,128]{1,0:T(2,128)}, f32[2,128]{1,0:T(2,128)S(1)}, u32[]{:S(2)}) copy-start(f32[2,128]{1,0:T(2,128)S(1)} %get-tuple-element.110) | copy-start | bytes 3076
  6.9 11.5 %copy-start.73 = (s32[1,2]{1,0:T(1,128)S(1)}, s32[1,2]{1,0:T(1,128)}, u32[]{:S(2)}) copy-start(s32[1,2]{1,0:T(1,128)} %param.15) | copy-start | bytes 28
  6.9 11.6 %copy-start.54 = (f32[4,768]{1,0:T(4,128)S(1)}, f32[4,768]{1,0:T(4,128)}, u32[]{:S(2)}) copy-start(f32[4,768]{1,0:T(4,128)} %param.22) | copy-start | bytes 36868
  6.9 14.0 %copy-start = (bf16[1,2,128,768]{3,2,1,0:T(8,128)(2,1)S(1)}, bf16[1,2,128,768]{3,2,1,0:T(8,128)(2,1)}, u32[]{:S(2)}) copy-start(bf16[1,2,128,768]{3,2,1,0:T(8,128)(2,1)} %param.13) | copy-start | bytes 1179652
  10.8 79.3 %copy-start.5 = (f32[2,128,2304]{1,2,0:T(8,128)}, f32[2,128,2304]{1,2,0:T(8,128)S(1)}, u32[]{:S(2)}) copy-start(f32[2,128,2304]{1,2,0:T(8,128)S(1)} %get-tuple-element.112) | copy-start | bytes 7077892
  11.8 78.3 %copy-start.27 = (f32[768]{0:T(1024)S(1)}, f32[768]{0:T(1024)}, u32[]{:S(2)}) copy-start(f32[768]{0:T(1024)} %param.23) | copy-start | bytes 9220
  12.7 13.5 %collective-permute-start = (bf16[2,3,768]{1,2,0:T(8,128)(2,1)}, bf16[2,3,768]{1,2,0:T(8,128)(2,1)S(1)}, u32[]{:S(2)}, u32[]{:S(2)}) collective-permute-start(bf16[2,3,768]{1,2,0:T(8,128)(2,1)} %slice.175), channel_id=1, source_target_pairs={{0,2},{2,4},{4,6},{6,8},{8,10},{10,12},{12,14},{14,16},{16,18},{18... | collective-permute-start | bytes 27656 | tf_op jit(solution)/shard_map/ppermute | solution.py:31
  26.3 69.4 %copy-start.12 = (bf16[2,3,768]{1,2,0:T(8,128)(2,1)}, bf16[2,3,768]{1,2,0:T(8,128)(2,1)S(1)}, u32[]{:S(2)}) copy-start(bf16[2,3,768]{1,2,0:T(8,128)(2,1)S(1)} %collective-permute-done) | copy-start | bytes 27652
  93.4 8.4 %copy-start.9 = (bf16[2,128,768]{2,1,0:T(8,128)(2,1)}, bf16[2,128,768]{2,1,0:T(8,128)(2,1)S(1)}, u32[]{:S(2)}) copy-start(bf16[2,128,768]{2,1,0:T(8,128)(2,1)S(1)} %copy.73) | copy-start | bytes 1179652
  93.4 8.4 %slice-start = ((s8[9437184]{0:T(1024)(128)(4,1)}), s8[4194304]{0:T(1024)(128)(4,1)S(1)}, s32[]{:S(2)}) async-start(s8[9437184]{0:T(1024)(128)(4,1)} %bitcast.250), calls=%async_computation | async-start | bytes 8388608
  115.5 57.6 %copy-start.44 = (f32[768]{0:T(1024)S(1)}, f32[768]{0:T(1024)}, u32[]{:S(2)}) copy-start(f32[768]{0:T(1024)} %get-tuple-element.65) | copy-start | bytes 9220
  115.5 57.6 %copy-start.46 = (f32[768]{0:T(1024)S(1)}, f32[768]{0:T(1024)}, u32[]{:S(2)}) copy-start(f32[768]{0:T(1024)} %get-tuple-element.130) | copy-start | bytes 9220
  192.0 58.8 %copy-start.43 = (f32[768]{0:T(1024)S(1)}, f32[768]{0:T(1024)}, u32[]{:S(2)}) copy-start(f32[768]{0:T(1024)} %get-tuple-element.127) | copy-start | bytes 9220
  192.0 58.8 %copy-start.59 = (f32[256]{0:T(256)S(1)}, f32[256]{0:T(256)}, u32[]{:S(2)}) copy-start(f32[256]{0:T(256)} %copy-done.58) | copy-start | bytes 3076
  192.0 58.8 %copy-start.71 = (f32[256]{0:T(256)S(1)}, f32[256]{0:T(256)}, u32[]{:S(2)}) copy-start(f32[256]{0:T(256)} %copy-done.70) | copy-start | bytes 3076
  267.2 69.2 %copy-start.13 = (bf16[2,3,768]{1,2,0:T(8,128)(2,1)S(1)}, bf16[2,3,768]{1,2,0:T(8,128)(2,1)}, u32[]{:S(2)}) copy-start(bf16[2,3,768]{1,2,0:T(8,128)(2,1)} %copy-done.12) | copy-start | bytes 27652
  345.4 153.2 %collective-permute-start.1 = (f32[2,3,768]{2,0,1:T(2,128)}, f32[2,3,768]{2,0,1:T(2,128)}, u32[]{:S(2)}, u32[]{:S(2)}) collective-permute-start(f32[2,3,768]{2,0,1:T(2,128)} %copy.82), channel_id=1, source_target_pairs={{2,0},{4,2},{6,4},{8,6},{10,8},{12,10},{14,12},{16,14},{18,16},{20... | collective-permute-start | bytes 55304 | tf_op jit(solution)/shard_map/ppermute | solution.py:31
  359.5 18.3 %copy-start.50 = (f32[768]{0:T(1024)S(1)}, f32[768]{0:T(1024)}, u32[]{:S(2)}) copy-start(f32[768]{0:T(1024)} %get-tuple-element.52) | copy-start | bytes 9220
  359.5 18.9 %copy-start.49 = (f32[768]{0:T(1024)S(1)}, f32[768]{0:T(1024)}, u32[]{:S(2)}) copy-start(f32[768]{0:T(1024)} %get-tuple-element.53) | copy-start | bytes 9220
  359.5 19.5 %copy-start.48 = (f32[768]{0:T(1024)S(1)}, f32[768]{0:T(1024)}, u32[]{:S(2)}) copy-start(f32[768]{0:T(1024)} %get-tuple-element.56) | copy-start | bytes 9220
  511.7 46.0 %copy-start.19 = (f32[256,768]{1,0:T(8,128)S(1)}, f32[256,768]{1,0:T(8,128)}, u32[]{:S(2)}) copy-start(f32[256,768]{1,0:T(8,128)} %fusion.80) | copy-start | bytes 2359300
  559.5 108.5 %copy-start.23 = (f32[48,2304]{1,0:T(8,128)S(1)}, f32[48,2304]{1,0:T(8,128)}, u32[]{:S(2)}) copy-start(f32[48,2304]{1,0:T(8,128)} %get-tuple-element.36) | copy-start | bytes 1327108
  559.6 110.5 %copy-start.26 = (f32[48,768]{1,0:T(8,128)S(1)}, f32[48,768]{1,0:T(8,128)}, u32[]{:S(2)}) copy-start(f32[48,768]{1,0:T(8,128)} %get-tuple-element.38) | copy-start | bytes 442372
  559.6 112.2 %copy-start.21 = (f32[48,3072]{1,0:T(8,128)S(1)}, f32[48,3072]{1,0:T(8,128)}, u32[]{:S(2)}) copy-start(f32[48,3072]{1,0:T(8,128)} %get-tuple-element.40) | copy-start | bytes 1769476
  (68 other events, 276.4 us)

commit v2 on v0

--- a/solution.py
+++ b/solution.py
@@ -1,13 +1,29 @@
+import functools
 import math
+import types
 
 import jax
 import jax.numpy as jnp
 from jax import lax
+from jax.experimental import pallas as pl
+from jax.experimental.pallas import tpu as pltpu
 from jax.sharding import PartitionSpec as P
 
 HEADS = 12
 HEAD = 64
 TAPS = 4
+STATES = 64
+MESH = pl.DeviceIdType.MESH
+SEQ = "seq"
+BATCH = "batch"
+QKV_MORE = "qkv_more"
+QKV_LESS = "qkv_less"
+DOWN = "down"
+OUT = "out"
+UP = "up"
+QKV = "qkv"
+SMALL = "small"
+VMEM_BYTES = 60 * 2**20
 
 
 norm_eps = 1e-05
@@ -108,14 +124,14 @@
 
 
 def to_frequency(data_low):
-    parts = lax.all_to_all(data_low[None], "seq", split_axis=3, concat_axis=0, tiled=True)
+    parts = lax.all_to_all(data_low[None], SEQ, split_axis=3, concat_axis=0, tiled=True)
     return forward_spectrum(parts.astype(jnp.float32))
 
 
 def from_frequency(freq_real, freq_imag):
     time_parts = inverse_spectrum(freq_real, freq_imag)
     joined = lax.all_to_all(
-        for_sending(time_parts), "seq", split_axis=0, concat_axis=3, tiled=True
+        for_sending(time_parts), SEQ, split_axis=0, concat_axis=3, tiled=True
     ).astype(time_parts.dtype)
     return joined[0]
 
@@ -171,8 +187,8 @@
 
 def attend_forward(query_low, keys_low, values_low, length_value, query_positions):
     whole_keys, whole_values = (
-        lax.all_gather(keys_low, "seq", axis=0, tiled=True),
-        lax.all_gather(values_low, "seq", axis=0, tiled=True),
+        lax.all_gather(keys_low, SEQ, axis=0, tiled=True),
+        lax.all_gather(values_low, SEQ, axis=0, tiled=True),
     )
     allowed = attention_mask(query_positions, whole_keys.shape[0], length_value)
     score_scale = HEAD ** (-0.5)
@@ -232,7 +248,7 @@
         return (d_query, d_keys, d_values)
 
     query_grads, key_grads, value_grads = lax.map(head_backward, jnp.arange(HEADS, dtype=jnp.int32))
-    count_rows = span_rows * lax.axis_size("seq")
+    count_rows = span_rows * lax.axis_size(SEQ)
     key_part = (
         lax.slice_in_dim(key_grads, 0, count_rows, axis=1)
         .transpose(1, 0, 2)
@@ -244,7 +260,7 @@
         .reshape(count_rows, HEADS * HEAD)
     )
     key_value = lax.psum_scatter(
-        jnp.stack([key_part, value_part], 1), "seq", scatter_dimension=0, tiled=True
+        jnp.stack([key_part, value_part], 1), SEQ, scatter_dimension=0, tiled=True
     )
     return (join_heads(query_grads), key_value[:, 0], key_value[:, 1])
 
@@ -267,8 +283,8 @@
     seq_count = tokens.shape[1]
     span_rows = tokens.shape[2]
     width = tokens.shape[3]
-    devices = lax.axis_size("seq")
-    place = lax.axis_index("seq")
+    devices = lax.axis_size(SEQ)
+    place = lax.axis_index(SEQ)
     channels = width // devices
     count_freq = 2 * devices
     fft_length = count_freq * span_rows
@@ -314,7 +330,7 @@
         queries_one = qkv_one[:, :, :width]
         keys_one = qkv_one[:, :, width : 2 * width].astype(jnp.bfloat16)
         values_one = qkv_one[:, :, 2 * width :]
-        earlier = passed_along(keys_one[:, span_rows - rim :], "seq", 1)
+        earlier = passed_along(keys_one[:, span_rows - rim :], SEQ, 1)
         extended = jnp.concatenate([earlier, keys_one], 1)
         shifted = sum(
             (
@@ -362,7 +378,7 @@
         hidden_three = hidden_two + dense_product(attended_low, w_out[1])
         normed_four, raised_two, active_two, hidden_four = feed_forward(hidden_three, 3, 1)
         output = hidden_four.reshape(seq_count, span_rows, width) * validity
-        saved = dict(
+        saved = types.SimpleNamespace(
             flat_in=flat_in,
             normed_one=normed_one,
             queries_one=queries_one,
@@ -400,74 +416,74 @@
     grad_rows = (cotangent[0].astype(jnp.float32) * validity).reshape(row_count, width)
     grad_rows, down_two, up_two, gain_four, bias_four = feed_backward(
         grad_rows,
-        saved["hidden_three"],
-        saved["normed_four"],
-        saved["raised_two"],
-        saved["active_two"],
+        saved.hidden_three,
+        saved.normed_four,
+        saved.raised_two,
+        saved.active_two,
         3,
         1,
     )
     branch_low = grad_rows.astype(jnp.bfloat16)
-    out_two = product_left(saved["attended_low"], branch_low)
+    out_two = product_left(saved.attended_low, branch_low)
     d_attended = (
         product_right(branch_low, w_out[1])
         .astype(jnp.bfloat16)
         .reshape(seq_count, span_rows, width)
     )
-    qkv_two = saved["qkv_two"]
+    qkv_two = saved.qkv_two
     grad_parts = []
     for seq_index in range(seq_count):
         d_query_rows, d_key_rows, d_value_rows = attend_backward(
             qkv_two[seq_index, :, :width],
-            saved["keys_list"][seq_index],
-            saved["values_list"][seq_index],
-            saved["totals_list"][seq_index],
+            saved.keys_list[seq_index],
+            saved.values_list[seq_index],
+            saved.totals_list[seq_index],
             d_attended[seq_index],
             lengths[0, seq_index],
             query_positions,
         )
         grad_parts.append(jnp.concatenate([d_query_rows, d_key_rows, d_value_rows], -1))
     d_qkv_two = jnp.concatenate(grad_parts, 0).astype(jnp.bfloat16)
-    qkv_grad_two = product_left(saved["normed_three"], d_qkv_two)
+    qkv_grad_two = product_left(saved.normed_three, d_qkv_two)
     d_inputs, gain_three, bias_three = norm_backward(
-        saved["hidden_two"], 2, product_right(d_qkv_two, w_qkv[1])
+        saved.hidden_two, 2, product_right(d_qkv_two, w_qkv[1])
     )
     grad_rows = grad_rows + d_inputs
     grad_rows, down_one, up_one, gain_two, bias_two = feed_backward(
         grad_rows,
-        saved["hidden_one"],
-        saved["normed_two"],
-        saved["raised_one"],
-        saved["active_one"],
+        saved.hidden_one,
+        saved.normed_two,
+        saved.raised_one,
+        saved.active_one,
         1,
         0,
     )
     branch_low = grad_rows.astype(jnp.bfloat16)
-    out_one = product_left(saved["gated_low"], branch_low)
+    out_one = product_left(saved.gated_low, branch_low)
     d_gated = product_right(branch_low, w_out[0]).reshape(seq_count, span_rows, width)
-    d_queries = d_gated * saved["mixer"]
-    d_mixer = d_gated * saved["queries_one"]
-    skip_grad = jnp.sum(d_mixer * saved["carried"], (0, 1))
+    d_queries = d_gated * saved.mixer
+    d_mixer = d_gated * saved.queries_one
+    skip_grad = jnp.sum(d_mixer * saved.carried, (0, 1))
     conv_real, conv_imag = to_frequency(d_mixer.astype(jnp.bfloat16))
-    kernel_real = saved["kernel_real"]
-    kernel_imag = saved["kernel_imag"]
+    kernel_real = saved.kernel_real
+    kernel_imag = saved.kernel_imag
     from_conv = from_frequency(
         kernel_real * conv_real + kernel_imag * conv_imag,
         kernel_real * conv_imag - kernel_imag * conv_real,
     )
     d_carried = d_mixer * skip + from_conv
-    carried_real = saved["carried_real"]
-    carried_imag = saved["carried_imag"]
+    carried_real = saved.carried_real
+    carried_imag = saved.carried_imag
     cot_real = (
         jnp.sum(carried_real * conv_real + carried_imag * conv_imag, 1, keepdims=True) / fft_length
     )
     cot_imag = (
         jnp.sum(carried_real * conv_imag - carried_imag * conv_real, 1, keepdims=True) / fft_length
     )
-    rate_grad, weight_grad = saved["kernel_pull"]((cot_real, cot_imag))
-    d_shifted = d_carried * saved["values_one"] * validity
-    d_values = d_carried * saved["shifted"] * validity
-    extended = saved["extended"]
+    rate_grad, weight_grad = saved.kernel_pull((cot_real, cot_imag))
+    d_shifted = d_carried * saved.values_one * validity
+    d_values = d_carried * saved.shifted * validity
+    extended = saved.extended
     grads_extended = sum(
         (
             jnp.pad(taps[offset] * d_shifted, ((0, 0), (rim - offset, offset), (0, 0)))
@@ -484,51 +500,51 @@
             for offset in range(TAPS)
         ]
     )
-    later = passed_along(grads_extended[:, :rim], "seq", -1)
+    later = passed_along(grads_extended[:, :rim], SEQ, -1)
     d_keys = grads_extended[:, rim:] + jnp.pad(later, ((0, 0), (span_rows - rim, 0), (0, 0)))
     d_qkv_one = (
         jnp.concatenate([d_queries, d_keys, d_values], -1)
         .reshape(row_count, 3 * width)
         .astype(jnp.bfloat16)
     )
-    qkv_grad_one = product_left(saved["normed_one"], d_qkv_one)
+    qkv_grad_one = product_left(saved.normed_one, d_qkv_one)
     d_inputs, gain_one, bias_one = norm_backward(
-        saved["flat_in"], 0, product_right(d_qkv_one, w_qkv[0])
+        saved.flat_in, 0, product_right(d_qkv_one, w_qkv[0])
     )
     d_tokens = ((grad_rows + d_inputs).reshape(seq_count, span_rows, width) * validity)[None]
     gain_sum, bias_sum, qkv_sum, out_sum, up_sum, down_sum, taps_sum, skip_sum = (
         lax.psum_scatter(
             jnp.stack([gain_one, gain_two, gain_three, gain_four]),
-            "seq",
+            SEQ,
             scatter_dimension=1,
             tiled=True,
         ),
         lax.psum_scatter(
             jnp.stack([bias_one, bias_two, bias_three, bias_four]),
-            "seq",
+            SEQ,
             scatter_dimension=1,
             tiled=True,
         ),
         lax.psum_scatter(
-            jnp.stack([qkv_grad_one, qkv_grad_two]), "seq", scatter_dimension=1, tiled=True
+            jnp.stack([qkv_grad_one, qkv_grad_two]), SEQ, scatter_dimension=1, tiled=True
         ),
-        lax.psum_scatter(jnp.stack([out_one, out_two]), "seq", scatter_dimension=1, tiled=True),
-        lax.psum_scatter(jnp.stack([up_one, up_two]), "seq", scatter_dimension=1, tiled=True),
-        lax.psum_scatter(jnp.stack([down_one, down_two]), "seq", scatter_dimension=1, tiled=True),
-        lax.psum_scatter(taps_grad, "seq", scatter_dimension=1, tiled=True),
-        lax.psum_scatter(skip_grad[None], "seq", scatter_dimension=1, tiled=True),
+        lax.psum_scatter(jnp.stack([out_one, out_two]), SEQ, scatter_dimension=1, tiled=True),
+        lax.psum_scatter(jnp.stack([up_one, up_two]), SEQ, scatter_dimension=1, tiled=True),
+        lax.psum_scatter(jnp.stack([down_one, down_two]), SEQ, scatter_dimension=1, tiled=True),
+        lax.psum_scatter(taps_grad, SEQ, scatter_dimension=1, tiled=True),
+        lax.psum_scatter(skip_grad[None], SEQ, scatter_dimension=1, tiled=True),
     )
     totals = (
-        lax.psum(gain_sum.astype(jnp.bfloat16), "batch").astype(jnp.float32),
-        lax.psum(bias_sum.astype(jnp.bfloat16), "batch").astype(jnp.float32),
-        lax.psum(qkv_sum.astype(jnp.bfloat16), "batch").astype(jnp.float32),
-        lax.psum(out_sum.astype(jnp.bfloat16), "batch").astype(jnp.float32),
-        lax.psum(up_sum.astype(jnp.bfloat16), "batch").astype(jnp.float32),
-        lax.psum(down_sum.astype(jnp.bfloat16), "batch").astype(jnp.float32),
-        lax.psum(taps_sum.astype(jnp.bfloat16), "batch").astype(jnp.float32),
-        lax.psum(skip_sum.astype(jnp.bfloat16), "batch").astype(jnp.float32),
-        lax.psum(rate_grad.astype(jnp.bfloat16), "batch").astype(jnp.float32),
-        lax.psum(weight_grad.astype(jnp.bfloat16), "batch").astype(jnp.float32),
+        lax.psum(gain_sum.astype(jnp.bfloat16), BATCH).astype(jnp.float32),
+        lax.psum(bias_sum.astype(jnp.bfloat16), BATCH).astype(jnp.float32),
+        lax.psum(qkv_sum.astype(jnp.bfloat16), BATCH).astype(jnp.float32),
+        lax.psum(out_sum.astype(jnp.bfloat16), BATCH).astype(jnp.float32),
+        lax.psum(up_sum.astype(jnp.bfloat16), BATCH).astype(jnp.float32),
+        lax.psum(down_sum.astype(jnp.bfloat16), BATCH).astype(jnp.float32),
+        lax.psum(taps_sum.astype(jnp.bfloat16), BATCH).astype(jnp.float32),
+        lax.psum(skip_sum.astype(jnp.bfloat16), BATCH).astype(jnp.float32),
+        lax.psum(rate_grad.astype(jnp.bfloat16), BATCH).astype(jnp.float32),
+        lax.psum(weight_grad.astype(jnp.bfloat16), BATCH).astype(jnp.float32),
     )
     return (
         output[None].astype(jnp.bfloat16),
@@ -547,11 +563,1403 @@
     )
 
 
+def other_device(place, core, to_place, to_core):
+    return jnp.logical_or(place != to_place, core != to_core)
+
+
+def greet(devices):
+    barrier = pltpu.get_barrier_semaphore()
+    for device in devices:
+        pl.semaphore_signal(barrier, inc=1, device_id=device, device_id_type=MESH)
+    pl.semaphore_wait(barrier, len(devices))
+
+
+def remote(source, target, send_sem, recv_sem, device):
+    return pltpu.make_async_remote_copy(
+        src_ref=source,
+        dst_ref=target,
+        send_sem=send_sem,
+        recv_sem=recv_sem,
+        device_id=device,
+        device_id_type=MESH,
+    )
+
+
+def split_low(value):
+    upper = value.astype(jnp.bfloat16)
+    return upper, (value - upper.astype(jnp.float32)).astype(jnp.bfloat16)
+
+
+NN = (((1,), (0,)), ((), ()))
+NT = (((1,), (1,)), ((), ()))
+TN = (((0,), (0,)), ((), ()))
+
+
+def dot(left, right, form=NN):
+    return lax.dot_general(left, right, form, preferred_element_type=jnp.float32)
+
+
+def dot_fine(left, right, form=NN):
+    left_up, left_low = left
+    right_up, right_low = right
+    total = dot(left_up, right_up, form) + dot(left_up, right_low, form)
+    if left_low is not None:
+        total = total + dot(left_low, right_up, form)
+    return total
+
+
+def state_tables(rate_row, weight_row, span):
+    row = lax.broadcasted_iota(jnp.int32, (span, 2 * STATES), 0)
+    lane = lax.broadcasted_iota(jnp.int32, (span, 2 * STATES), 1)
+    steps = jnp.where(lane < STATES, span - 1 - row, row + 1).astype(jnp.float32)
+    table = jnp.exp(-rate_row * steps)
+    lane_row = lax.broadcasted_iota(jnp.int32, (8, 2 * STATES), 1)
+    lead = jnp.where(lane_row < STATES, 0.0, weight_row * jnp.exp(rate_row))
+    response = lax.dot_general(
+        lead, table, NT, precision=highest, preferred_element_type=jnp.float32
+    )[:1]
+    spread = pltpu.roll(
+        jnp.broadcast_to(response, (span, span)), 0, 1, stride=1, stride_axis=0
+    )
+    later = lax.broadcasted_iota(jnp.int32, (span, span), 1)
+    earlier = lax.broadcasted_iota(jnp.int32, (span, span), 0)
+    toeplitz = jnp.where(later >= earlier, spread, 0.0)
+    return table, steps, toeplitz
+
+
+def shift_rows(value, count):
+    if count > 0:
+        return jnp.concatenate([jnp.zeros_like(value[:count]), value[:-count]], 0)
+    return jnp.concatenate([value[-count:], jnp.zeros_like(value[:-count])], 0)
+
+
+def scan_states(value, decay, seqs, blocks, direction):
+    step = 1
+    while step < blocks:
+        value = value + shift_rows(value, direction * step * seqs) * jnp.exp(decay * step)
+        step *= 2
+    return shift_rows(value, direction * seqs)
+
+
+def mixer_forward_kernel(
+    n, seqs, span, channels, unroll,
+    x_ref, rate_ref, weight_ref, y_ref, held_ref,
+    flat, flat_out, answer, send, recv, back_send, back_recv, own_sem,
+):
+    me, core = lax.axis_index(SEQ), lax.axis_index(BATCH)
+    peers = [lax.rem(me + step, n) for step in range(1, n)]
+    greet([(peer, core) for peer in peers])
+    outgoing = []
+    for step, peer in enumerate(peers):
+        rows = pl.ds(pl.multiple_of(peer * channels, 16), channels)
+        copy = remote(
+            x_ref.at[:, rows, :], held_ref.at[me], send.at[step], recv.at[step], (peer, core)
+        )
+        copy.start()
+        outgoing.append(copy)
+    own_rows = pl.ds(pl.multiple_of(me * channels, 16), channels)
+    own = pltpu.make_async_copy(x_ref.at[:, own_rows, :], held_ref.at[me], own_sem.at[0])
+    own.start()
+    own.wait()
+    for copy in outgoing:
+        copy.wait()
+    total_rows = n * seqs * channels
+    flat[...] = held_ref[...].astype(jnp.float32).reshape(total_rows, span)
+
+    def one_channel(channel, carry):
+        rate_row = rate_ref[pl.ds(channel, 1), :]
+        weight_row = weight_ref[pl.ds(channel, 1), :]
+        table, _, toeplitz = state_tables(rate_row, weight_row, span)
+        rows = pl.ds(channel, n * seqs, stride=channels)
+        data = (flat[rows, :].astype(jnp.bfloat16), None)
+        table_parts = split_low(table)
+        inner = dot_fine(data, split_low(toeplitz))
+        states = dot_fine(data, table_parts)
+        states = scan_states(states, -span * rate_row, seqs, n, 1)
+        lane = lax.broadcasted_iota(jnp.int32, states.shape, 1)
+        weighted = jnp.where(lane < STATES, 0.0, pltpu.roll(states, STATES, 1) * weight_row)
+        flat_out[rows, :] = inner + dot_fine(split_low(weighted), table_parts, NT)
+        return carry
+
+    lax.fori_loop(0, channels, one_channel, 0, unroll=unroll)
+    answer[...] = flat_out[...].reshape(n, seqs, channels, span).astype(jnp.bfloat16)
+    outgoing = []
+    for step, peer in enumerate(peers):
+        copy = remote(
+            answer.at[peer], y_ref.at[:, own_rows, :], back_send.at[step], back_recv.at[step],
+            (peer, core),
+        )
+        copy.start()
+        outgoing.append(copy)
+    own = pltpu.make_async_copy(answer.at[me], y_ref.at[:, own_rows, :], own_sem.at[1])
+    own.start()
+    own.wait()
+    for copy in outgoing:
+        copy.wait()
+
+
+def mixer_forward(x, rates, weights, n, collective):
+    seqs, width, span = x.shape
+    channels = width // n
+    total_rows = n * seqs * channels
+    vmem = pl.BlockSpec(memory_space=pltpu.VMEM)
+    return pl.pallas_call(
+        functools.partial(mixer_forward_kernel, n, seqs, span, channels, 4),
+        out_shape=(
+            jax.ShapeDtypeStruct(x.shape, jnp.bfloat16),
+            jax.ShapeDtypeStruct((n, seqs, channels, span), jnp.bfloat16),
+        ),
+        in_specs=[vmem] * 3,
+        out_specs=(vmem, vmem),
+        scratch_shapes=[
+            pltpu.VMEM((total_rows, span), jnp.float32),
+            pltpu.VMEM((total_rows, span), jnp.float32),
+            pltpu.VMEM((n, seqs, channels, span), jnp.bfloat16),
+            pltpu.SemaphoreType.DMA((n - 1,)),
+            pltpu.SemaphoreType.DMA((n - 1,)),
+            pltpu.SemaphoreType.DMA((n - 1,)),
+            pltpu.SemaphoreType.DMA((n - 1,)),
+            pltpu.SemaphoreType.DMA((2,)),
+        ],
+        compiler_params=pltpu.CompilerParams(
+            collective_id=collective, has_side_effects=True, vmem_limit_bytes=VMEM_BYTES
+        ),
+    )(x, rates, weights)
+
+
+def mixer_backward_channel(n, seqs, span, channels, refs, channel):
+    rate_row = refs.rates[pl.ds(channel, 1), :]
+    weight_row = refs.rate_weights[pl.ds(channel, 1), :]
+    table, steps, toeplitz = state_tables(rate_row, weight_row, span)
+    rows = pl.ds(channel, n * seqs, stride=channels)
+    data = refs.flat_x[rows, :].astype(jnp.bfloat16)
+    grad = refs.flat_d[rows, :].astype(jnp.bfloat16)
+    table_parts = split_low(table)
+    both_parts = split_low(jnp.concatenate([table, table * steps], 1))
+    count = n * seqs
+    sides = dot_fine((jnp.concatenate([data, grad], 0), None), both_parts)
+    lane = lax.broadcasted_iota(jnp.int32, (count, 2 * STATES), 1)
+    low_lanes = lane < STATES
+
+    def aligned(value):
+        return jnp.where(low_lanes, pltpu.roll(value, STATES, 1), 0.0)
+
+    entering = jnp.where(low_lanes, sides[:count, : 2 * STATES], 0.0)
+    entering_steps = jnp.where(low_lanes, sides[:count, 2 * STATES :], 0.0)
+    leaving = aligned(sides[count:, : 2 * STATES])
+    leaving_steps = aligned(sides[count:, 2 * STATES :])
+    decay = -span * rate_row
+    states = scan_states(entering, decay, seqs, n, 1)
+    states_steps = scan_states(states * jnp.exp(decay), decay, seqs, n, 1)
+    returned = scan_states(leaving, decay, seqs, n, -1)
+    far_weight = jnp.sum(leaving * states, 0, keepdims=True)
+    far_rate = jnp.sum(
+        leaving_steps * states + returned * entering_steps + span * (leaving * states_steps),
+        0, keepdims=True,
+    )
+    cross = dot(data, grad, TN)
+    later = lax.broadcasted_iota(jnp.int32, (span, span), 1)
+    earlier = lax.broadcasted_iota(jnp.int32, (span, span), 0)
+    cross = jnp.where(later >= earlier, cross, 0.0)
+    met = dot_fine(split_low(cross), both_parts, TN)
+    met_plain = pltpu.roll(met[:, : 2 * STATES], STATES, 1)
+    met_steps = pltpu.roll(met[:, 2 * STATES :], STATES, 1)
+    rise = jnp.exp(span * rate_row)
+    near_weight = rise * jnp.sum(table * met_plain, 0, keepdims=True)
+    near_rate = rise * jnp.sum(
+        table * ((steps - span) * met_plain + met_steps), 0, keepdims=True
+    )
+    lane_row = lane[:1]
+    near_weight = jnp.where(lane_row < STATES, pltpu.roll(near_weight, STATES, 1), 0.0)
+    near_rate = jnp.where(lane_row < STATES, pltpu.roll(near_rate, STATES, 1), 0.0)
+    refs.weight_grad[pl.ds(channel, 1), :] = near_weight + far_weight
+    refs.rate_grad[pl.ds(channel, 1), :] = -weight_row * (near_rate + far_rate)
+    inner = dot_fine((grad, None), split_low(toeplitz), NT)
+    weighted = returned * weight_row
+    refs.flat_out[rows, :] = inner + dot_fine(split_low(weighted), table_parts, NT)
+
+
+def block_of(index, core):
+    return 2 * index + lax.rem(index + core, 2)
+
+
+def keeper_of(block):
+    return lax.rem((block + 1) // 2, 2)
+
+
+class HeadPlaces:
+    def __init__(self, n, seqs, groups):
+        self.n, self.seqs, self.groups = n, seqs, groups
+        self.me, self.core = lax.axis_index(SEQ), lax.axis_index(BATCH)
+        self.group = self.me // (2 * seqs)
+        self.seq = lax.rem(self.me // 2, seqs)
+        self.batch = lax.rem(self.me, 2)
+        self.keeper = keeper_of(self.me)
+        self.sibling = (self.me, 1 - self.core)
+        self.targets = [
+            ((group * 2 * seqs + seq * 2 + self.core, self.keeper), seq, group)
+            for seq in range(seqs)
+            for group in range(groups)
+        ]
+        self.blocks = [block_of(index, self.core) for index in range(n // 2)]
+        self.sources = [(block, self.batch) for block in self.blocks]
+
+    def is_other(self, device):
+        return jnp.logical_or(device[0] != self.me, device[1] != self.core)
+
+    def greet(self):
+        barrier = pltpu.get_barrier_semaphore()
+        self.signal_all(barrier, [])
+        self.wait_all(barrier, 0)
+
+    def signal_all(self, barrier, more):
+        for device in [target for target, _, _ in self.targets] + self.sources:
+
+            @pl.when(self.is_other(device))
+            def _():
+                pl.semaphore_signal(barrier, inc=1, device_id=device, device_id_type=MESH)
+
+        for device in [self.sibling, *more]:
+            pl.semaphore_signal(barrier, inc=1, device_id=device, device_id_type=MESH)
+
+    def wait_all(self, barrier, more):
+        kept = jnp.logical_and(self.batch == self.core, self.is_kept_here())
+        count = len(self.targets) + len(self.sources) + 1 + more
+        pl.semaphore_wait(barrier, count - 2 * kept.astype(jnp.int32))
+
+    def is_kept_here(self):
+        return self.keeper == self.core
+
+    def send(self, source, target, send_sem, recv_sem, device):
+        @pl.when(self.is_other(device))
+        def _():
+            remote(source, target, send_sem, recv_sem, device).start()
+
+        @pl.when(jnp.logical_not(self.is_other(device)))
+        def _():
+            pltpu.make_async_copy(source, target, recv_sem).start()
+
+    def wait_sent(self, source, target, send_sem, recv_sem, device):
+        @pl.when(self.is_other(device))
+        def _():
+            remote(source, target, send_sem, recv_sem, device).wait_send()
+
+
+def fill_heads(held, head, first, n, span, rows_out, columns_out):
+    start = pl.multiple_of(first + head * HEAD, HEAD)
+    for block in range(n):
+        part = held[block, pl.ds(start, HEAD), :]
+        if rows_out is not None:
+            rows_out[block * span : (block + 1) * span, :] = part.T
+        if columns_out is not None:
+            columns_out[:, block * span : (block + 1) * span] = part
+
+
+def causal(first_key, rows, first_query, span):
+    key = first_key + lax.broadcasted_iota(jnp.int32, (rows, span), 0)
+    query = first_query + lax.broadcasted_iota(jnp.int32, (rows, span), 1)
+    return key <= query
+
+
+def attention_forward_kernel(
+    n, seqs, groups, span, group_rows,
+    qkv_ref, out_ref, held, lse_ref,
+    outputs, key_rows, value_columns,
+    send, recv, pass_send, pass_recv, back_send, back_recv,
+):
+    at = HeadPlaces(n, seqs, groups)
+    half = n // 2
+    at.greet()
+    for count, (device, seq, group) in enumerate(at.targets):
+        at.send(qkv_ref.at[seq, group], held.at[at.me], send.at[count], recv.at[at.me // 2], device)
+    passed = []
+    for index, block in enumerate(at.blocks):
+        remote(held.at[block], held.at[block], send.at[0], recv.at[index], at.sibling).wait_recv()
+        part = held.at[block, group_rows : 3 * group_rows, :]
+        copy = remote(part, part, pass_send.at[index], pass_recv.at[index], at.sibling)
+        copy.start()
+        passed.append(copy)
+    for copy in passed:
+        copy.wait()
+    for count, (device, seq, group) in enumerate(at.targets):
+        at.wait_sent(
+            qkv_ref.at[seq, group], held.at[at.me], send.at[count], recv.at[at.me // 2], device
+        )
+
+    def one_head(head, carry):
+        fill_heads(held, head, group_rows, n, span, key_rows, None)
+        fill_heads(held, head, 2 * group_rows, n, span, None, value_columns)
+        query_rows = pl.ds(pl.multiple_of(head * HEAD, HEAD), HEAD)
+        for index, block in enumerate(at.blocks):
+            query = held[block, query_rows, :] * jnp.bfloat16(HEAD**-0.5)
+            clear, reach = 2 * index * span, 2 * (index + 1) * span
+            edge = dot(key_rows[clear:reach, :], query)
+            edge = jnp.where(causal(clear, reach - clear, block * span, span), edge, masked_score)
+            top = jnp.max(edge, 0, keepdims=True)
+            if index > 0:
+                body = dot(key_rows[:clear, :], query)
+                top = jnp.maximum(top, jnp.max(body, 0, keepdims=True))
+            edge = jnp.exp(edge - top)
+            total = jnp.sum(edge, 0, keepdims=True)
+            result = dot(value_columns[:, clear:reach], edge.astype(jnp.bfloat16))
+            if index > 0:
+                body = jnp.exp(body - top)
+                total = total + jnp.sum(body, 0, keepdims=True)
+                result = result + dot(value_columns[:, :clear], body.astype(jnp.bfloat16))
+            outputs[index, query_rows, :] = (result / total).astype(jnp.bfloat16)
+            lse_ref[index, pl.ds(head, 1), :] = top + jnp.log(total)
+        return carry
+
+    lax.fori_loop(0, group_rows // HEAD, one_head, 0)
+    into = pl.ds(pl.multiple_of(at.group * group_rows, 16), group_rows)
+    lanes = pl.ds(pl.multiple_of(at.seq * span, span), span)
+    slot = at.seq * groups + at.group
+    for index, device in enumerate(at.sources):
+        at.send(
+            outputs.at[index], out_ref.at[into, lanes], back_send.at[index],
+            back_recv.at[slot], device,
+        )
+    for count, (device, seq, group) in enumerate(at.targets):
+        landed = out_ref.at[
+            group * group_rows : (group + 1) * group_rows, seq * span : (seq + 1) * span
+        ]
+        remote(landed, landed, back_send.at[0], back_recv.at[count], at.sibling).wait_recv()
+    for index, device in enumerate(at.sources):
+        at.wait_sent(
+            outputs.at[index], out_ref.at[into, lanes], back_send.at[index],
+            back_recv.at[slot], device,
+        )
+
+
+def attention_forward(qkv, n, collective):
+    seqs, groups, rows, span = qkv.shape
+    group_rows = rows // 3
+    half = n // 2
+    vmem = pl.BlockSpec(memory_space=pltpu.VMEM)
+    dma = pltpu.SemaphoreType.DMA
+    return pl.pallas_call(
+        functools.partial(attention_forward_kernel, n, seqs, groups, span, group_rows),
+        out_shape=(
+            jax.ShapeDtypeStruct((groups * group_rows, seqs * span), jnp.bfloat16),
+            jax.ShapeDtypeStruct((n, rows, span), jnp.bfloat16),
+            jax.ShapeDtypeStruct((half, group_rows // HEAD, span), jnp.float32),
+        ),
+        in_specs=[vmem],
+        out_specs=(vmem, vmem, vmem),
+        scratch_shapes=[
+            pltpu.VMEM((half, group_rows, span), jnp.bfloat16),
+            pltpu.VMEM((n * span, HEAD), jnp.bfloat16),
+            pltpu.VMEM((HEAD, n * span), jnp.bfloat16),
+            dma((seqs * groups,)),
+            dma((half,)),
+            dma((half,)),
+            dma((half,)),
+            dma((half,)),
+            dma((seqs * groups,)),
+        ],
+        compiler_params=pltpu.CompilerParams(
+            collective_id=collective, has_side_effects=True, vmem_limit_bytes=VMEM_BYTES
+        ),
+    )(qkv)
+
+
+TILE = 384
+VMEM, HBM = pltpu.VMEM, pl.ANY
+
+
+def launch(body, inputs, outputs, scratch, copies, collective):
+    names = [*inputs, *outputs, *scratch, "send", "recv", "local"]
+
+    def kernel(*refs):
+        body(types.SimpleNamespace(**dict(zip(names, refs))))
+
+    dma = pltpu.SemaphoreType.DMA
+    results = pl.pallas_call(
+        kernel,
+        out_shape=tuple(jax.ShapeDtypeStruct(shape, kind) for shape, kind, _ in outputs.values()),
+        in_specs=[pl.BlockSpec(memory_space=space) for _, space in inputs.values()],
+        out_specs=tuple(pl.BlockSpec(memory_space=space) for _, _, space in outputs.values()),
+        scratch_shapes=[pltpu.VMEM(shape, kind) for shape, kind in scratch.values()]
+        + [dma((copies,)), dma((copies,)), dma((LOCAL_COPIES,))],
+        compiler_params=pltpu.CompilerParams(
+            collective_id=collective, has_side_effects=True, vmem_limit_bytes=VMEM_BYTES
+        ),
+    )(*(array for array, _ in inputs.values()))
+    return types.SimpleNamespace(**dict(zip(outputs, results)))
+
+
+LOCAL_COPIES = 24
+
+
+class Loads:
+    def __init__(self, refs):
+        self.semaphores, self.used, self.pending = refs.local, 0, {}
+
+    def start(self, key, source, target):
+        copy = pltpu.make_async_copy(source, target, self.semaphores.at[self.used])
+        self.used += 1
+        copy.start()
+        self.pending[key] = copy
+
+    def wait(self, *keys):
+        for key in keys:
+            self.pending.pop(key).wait()
+
+
+class Links:
+    def __init__(self, refs):
+        self.send, self.recv, self.used, self.unsent = refs.send, refs.recv, 0, []
+
+    def slots(self, count):
+        self.used += count
+        return self.used - count
+
+    def copy(self, source, target, device, slot=None):
+        slot = self.slots(1) if slot is None else slot
+        made = remote(source, target, self.send.at[slot], self.recv.at[slot], device)
+        made.start()
+        self.unsent.append(made)
+        return made
+
+    def finish(self):
+        for made in self.unsent:
+            made.wait_send()
+
+
+class Reducer:
+    def __init__(self, refs, links, depth, weights, parts):
+        self.refs, self.links, self.depth = refs, links, depth
+        self.weights, self.parts = weights, parts
+        self.me, self.core = lax.axis_index(SEQ), lax.axis_index(BATCH)
+        self.level = self.me // 4
+        self.spot = (lax.rem(self.me // 2, 2), lax.rem(self.me, 2))
+        base = self.level * 4
+        self.across = [
+            (base + self.spot[0] * 2 + (1 - self.spot[1]), self.core),
+            (base + (1 - self.spot[0]) * 2 + self.spot[1], self.core),
+        ]
+        self.sibling = (self.me, 1 - self.core)
+        self.levels = [lax.rem(self.level + step, depth) for step in range(1, depth)]
+        self.column = [
+            (other * 4 + self.spot[0] * 2 + self.spot[1], self.core) for other in self.levels
+        ]
+        self.flights = {}
+
+    def neighbours(self):
+        return [self.sibling, *self.across, *self.column]
+
+    def ref(self, name, suffix):
+        return getattr(self.refs, name + suffix)
+
+    def exchange(self, weight):
+        half = self.weights[weight][1]
+        theirs = pl.ds(pl.multiple_of((1 - self.core) * half, 16), half)
+        self.flights[weight] = [
+            self.links.copy(
+                self.ref(weight, "_left"), self.ref(weight, "_left_other"), self.sibling
+            ),
+            self.links.copy(
+                self.ref(weight, "_right").at[theirs, :], self.ref(weight, "_right_other"),
+                self.sibling,
+            ),
+        ]
+
+    def product(self, part, first, outers, column):
+        weight, first_column, _, axis = self.parts[part]
+        half = self.weights[weight][1]
+        places = [
+            outer * 4 + (inner * 2 + first if axis == 0 else first * 2 + inner)
+            for outer in outers
+            for inner in range(2)
+        ]
+        left, left_other = self.ref(weight, "_left"), self.ref(weight, "_left_other")
+        mine = jnp.concatenate([left[place] for place in places], 0)
+        other = jnp.concatenate([left_other[place] for place in places], 0)
+        start = first_column + column
+        own = pl.ds(pl.multiple_of(self.core * half + start, 16), TILE)
+        there = pl.ds(pl.multiple_of(start, 16), TILE)
+        return dot(mine, self.ref(weight, "_right")[own, :], NT) + dot(
+            other, self.ref(weight, "_right_other")[there, :], NT
+        )
+
+    def fill(self, part, first, buffer):
+        weight, _, columns, _ = self.parts[part]
+        rows = self.weights[weight][0]
+        outers = [[outer] for outer in range(self.depth)]
+        if rows * 2 < TILE:
+            outers = [list(range(self.depth))]
+
+        def one_column(tile, carry):
+            column = tile * TILE
+            place = pl.ds(pl.multiple_of(column, 128), TILE)
+            for group in outers:
+                value = self.product(part, first, group, column)
+                buffer[group[0] : group[-1] + 1, :, :, place] = value.reshape(
+                    len(group), 2, rows, TILE
+                ).astype(buffer.dtype)
+            return carry
+
+        if columns == TILE:
+            one_column(0, 0)
+        else:
+            lax.fori_loop(0, columns // TILE, one_column, 0)
+
+    def first(self, part):
+        weight, _, _, axis = self.parts[part]
+        for flight in self.flights.pop(weight, ()):
+            flight.wait_recv()
+        mine = self.spot[1 - axis]
+        self.fill(part, 1 - mine, self.ref(part, "_away"))
+        self.flights[part] = self.links.copy(
+            self.ref(part, "_away"), self.ref(part, "_one"), self.across[axis]
+        )
+        self.fill(part, mine, self.ref(part, "_home"))
+
+    def first_given(self, part, values):
+        axis = self.parts[part][3]
+        mine = self.spot[1 - axis]
+        for outer in range(self.depth):
+            for inner in range(2):
+                there, here = (
+                    outer * 4 + (inner * 2 + first if axis == 0 else first * 2 + inner)
+                    for first in (1 - mine, mine)
+                )
+                self.ref(part, "_away")[outer, inner] = values[there]
+                self.ref(part, "_home")[outer, inner] = values[here]
+        self.flights[part] = self.links.copy(
+            self.ref(part, "_away"), self.ref(part, "_one"), self.across[axis]
+        )
+
+    def second(self, part):
+        axis = self.parts[part][3]
+        self.flights.pop(part).wait_recv()
+        mine = self.spot[axis]
+        home, one = self.ref(part, "_home"), self.ref(part, "_one")
+        for outer in range(self.depth):
+            one[outer, 1 - mine] = (
+                home[outer, 1 - mine] + one[outer, 1 - mine].astype(jnp.float32)
+            ).astype(one.dtype)
+        self.flights[part] = self.links.copy(
+            one.at[:, 1 - mine], self.ref(part, "_two"), self.across[1 - axis]
+        )
+        for outer in range(self.depth):
+            home[outer, mine] += one[outer, mine].astype(jnp.float32)
+
+    def third(self, part):
+        axis = self.parts[part][3]
+        self.flights.pop(part).wait_recv()
+        mine = self.spot[axis]
+        home, two = self.ref(part, "_home"), self.ref(part, "_two")
+        copies = []
+        for step, other in enumerate(self.levels):
+            two[other] = (home[other, mine] + two[other].astype(jnp.float32)).astype(two.dtype)
+            copies.append(
+                self.links.copy(two.at[other], self.ref(part, "_three").at[step], self.column[step])
+            )
+        self.flights[part] = copies
+
+    def total(self, part):
+        mine = self.spot[self.parts[part][3]]
+        total = self.ref(part, "_home")[self.level, mine]
+        total = total + self.ref(part, "_two")[self.level].astype(jnp.float32)
+        for step, copy in enumerate(self.flights.pop(part)):
+            copy.wait_recv()
+            total = total + self.ref(part, "_three")[step].astype(jnp.float32)
+        return total
+
+    def fourth(self, part):
+        weight, first_column, columns, _ = self.parts[part]
+        total = self.total(part)
+        start = self.core * self.weights[weight][1] + first_column
+        place = pl.ds(pl.multiple_of(start, 128), columns)
+        out = self.ref(weight, "_grad")
+        out[:, place] = total
+        filled = out.at[:, place]
+        self.flights[part] = self.links.copy(filled, filled, self.sibling)
+
+    def last(self, part):
+        self.flights.pop(part).wait_recv()
+
+
+def reducer_scratch(weights, parts, depth, tokens):
+    low, wide = jnp.bfloat16, jnp.float32
+    shapes = {}
+    for weight, (rows, half) in weights.items():
+        shapes[weight + "_left_other"] = ((4 * depth, rows, tokens), low)
+        shapes[weight + "_right_other"] = ((half, tokens), low)
+    for part, (weight, _, columns, _) in parts.items():
+        rows = weights[weight][0] if weight in weights else weight
+        low = wide if weight not in weights else jnp.bfloat16
+        shapes[part + "_away"] = ((depth, 2, rows, columns), low)
+        shapes[part + "_home"] = ((depth, 2, rows, columns), wide)
+        shapes[part + "_one"] = ((depth, 2, rows, columns), low)
+        shapes[part + "_two"] = ((depth, rows, columns), low)
+        shapes[part + "_three"] = ((depth - 1, rows, columns), low)
+    return shapes
+
+
+def gelu_slope(value):
+    scale = math.sqrt(2.0 / math.pi)
+    square = value * value
+    bent = jnp.tanh(scale * value * (1.0 + 0.044715 * square))
+    return 0.5 * (1.0 + bent) + 0.5 * value * (1.0 - bent * bent) * scale * (
+        1.0 + 3.0 * 0.044715 * square
+    )
+
+
+def norm_gradient(inputs, gain, grad):
+    center = inputs - jnp.mean(inputs, 0, keepdims=True)
+    factor = lax.rsqrt(jnp.mean(center * center, 0, keepdims=True) + norm_eps)
+    unit = center * factor
+    scaled = grad * gain
+    result = factor * (
+        scaled
+        - jnp.mean(scaled, 0, keepdims=True)
+        - unit * jnp.mean(scaled * unit, 0, keepdims=True)
+    )
+    return result, jnp.sum(grad * unit, 1, keepdims=True), jnp.sum(grad, 1, keepdims=True)
+
+
+def rows_product(matrix, other, out_rows, chunk, store):
+    def one_chunk(index, carry):
+        rows = pl.ds(pl.multiple_of(index * chunk, 128), chunk)
+        store(rows, dot(matrix[rows, :], other))
+        return carry
+
+    lax.fori_loop(0, out_rows // chunk, one_chunk, 0)
+
+
+def back_one_body(n, seqs, groups, span, group_rows, width, hidden_width, refs):
+    at = HeadPlaces(n, seqs, groups)
+    half = n // 2
+    heads = group_rows // HEAD
+    tokens = seqs * span
+    links, loads = Links(refs), Loads(refs)
+    reducer = Reducer(refs, links, groups, back_one_weights(width, hidden_width, n), back_one_parts(width, hidden_width))
+    barrier = pltpu.get_barrier_semaphore()
+    at.signal_all(barrier, reducer.neighbours()[1:])
+
+    loads.start("w_down", refs.w_down.at[1], refs.down)
+    loads.start("cotangent", refs.cotangent, refs.cot)
+    loads.start("raised", refs.raised, refs.raised_in)
+    loads.start("w_up", refs.w_up.at[1], refs.up)
+    loads.start("hidden", refs.hidden, refs.hidden_in)
+    loads.start("active", refs.active, refs.down_left)
+    loads.start("w_out", refs.w_out.at[1], refs.out)
+    loads.start("normed", refs.normed, refs.up_left)
+    loads.start("attended", refs.attended, refs.out_left)
+    loads.start("held", refs.held, refs.held_in)
+
+    loads.wait("cotangent")
+    for seq in range(seqs):
+        lanes = slice(seq * span, (seq + 1) * span)
+        for first in range(0, width, span):
+            piece = refs.cot[seq, :, first : first + span].astype(jnp.float32).T
+            refs.grad[first : first + span, lanes] = piece * refs.valid[:, lanes]
+    refs.down_right[...] = refs.grad[...].astype(jnp.bfloat16)
+    loads.wait("w_down", "raised")
+
+    def store_raised(rows, value):
+        slope = gelu_slope(refs.raised_in[rows, :].astype(jnp.float32))
+        refs.up_right[rows, :] = (slope * value).astype(jnp.bfloat16)
+
+    rows_product(refs.down, refs.down_right[...], hidden_width, 512, store_raised)
+    at.wait_all(barrier, len(reducer.neighbours()) - 1)
+    loads.wait("active")
+    reducer.exchange(DOWN)
+    loads.wait("w_up", "hidden", "normed")
+    reducer.exchange(UP)
+    d_normed = dot(refs.up[...], refs.up_right[...])
+    d_inputs, gain_part, bias_part = norm_gradient(refs.hidden_in[...], refs.gain[...], d_normed)
+    refs.small[:, 0:1] = gain_part
+    refs.small[:, 1:2] = bias_part
+    grad = refs.grad[...] + d_inputs
+    refs.grad_out[...] = grad
+    refs.out_right[...] = grad.astype(jnp.bfloat16)
+    loads.wait("w_out", "attended")
+    reducer.exchange(OUT)
+    refs.d_attended[...] = dot(refs.out[...], refs.out_right[...]).astype(jnp.bfloat16)
+
+    arrive = links.slots(half)
+    leave = links.slots(len(at.targets))
+    spread = []
+    for count, (device, seq, group) in enumerate(at.targets):
+        source = refs.d_attended.at[
+            group * group_rows : (group + 1) * group_rows, seq * span : (seq + 1) * span
+        ]
+        sent = (
+            source, refs.landing.at[at.me // 2], refs.send.at[leave + count],
+            refs.recv.at[arrive + at.me // 2], device,
+        )
+        at.send(*sent)
+        spread.append(sent)
+    loads.wait("held")
+    reducer.first(DOWN)
+    reducer.first(UP)
+    reducer.first(OUT)
+    for index in range(half):
+        landed = refs.landing.at[index]
+        remote(
+            landed, landed, refs.send.at[leave], refs.recv.at[arrive + index], at.sibling
+        ).wait_recv()
+
+    returned = links.slots(len(at.targets) * heads)
+    returning = links.slots(half * heads)
+    slot = at.seq * groups + at.group
+    going = []
+    passed = []
+
+    def send_back(head):
+        passed[head].wait_recv()
+        for index, device in enumerate(at.sources):
+            results = refs.results.at[head, index]
+            kept = refs.kept.at[head, index]
+            part = refs.partial_recv[head, index].astype(jnp.float32)
+            results[1] = (kept[:HEAD] + part[:HEAD]).astype(jnp.bfloat16)
+            results[2] = (kept[HEAD:] + part[HEAD:]).astype(jnp.bfloat16)
+            into = refs.d_qkv.at[
+                :,
+                pl.ds(pl.multiple_of(at.group * group_rows + head * HEAD, HEAD), HEAD),
+                pl.ds(pl.multiple_of(at.seq * span, span), span),
+            ]
+            sent = (
+                results, into, refs.send.at[returning + head * half + index],
+                refs.recv.at[returned + head * len(at.targets) + slot], device,
+            )
+            at.send(*sent)
+            going.append(sent)
+
+    def attend(head):
+        fill_heads(refs.held_in, head, group_rows, n, span, refs.key_rows, refs.key_columns)
+        fill_heads(refs.held_in, head, 2 * group_rows, n, span, refs.value_rows, None)
+        head_rows = slice(head * HEAD, (head + 1) * HEAD)
+        refs.key_grads[...] = jnp.zeros_like(refs.key_grads)
+        refs.value_grads[...] = jnp.zeros_like(refs.value_grads)
+        for index, block in enumerate(at.blocks):
+            query = refs.held_in[block, head_rows, :] * jnp.bfloat16(HEAD**-0.5)
+            grad = refs.landing[index, head_rows, :]
+            log_total = refs.lse[index, head : head + 1, :]
+            clear, reach = 2 * index * span, 2 * (index + 1) * span
+            pieces = []
+            row_term = jnp.zeros((1, span), jnp.float32)
+            for first, last in ((0, clear), (clear, reach)):
+                if first == last:
+                    continue
+                scores = dot(refs.key_rows[first:last, :], query)
+                if last == reach:
+                    scores = jnp.where(
+                        causal(clear, reach - clear, block * span, span), scores, masked_score
+                    )
+                weights = jnp.exp(scores - log_total)
+                d_weights = dot(refs.value_rows[first:last, :], grad)
+                row_term = row_term + jnp.sum(weights * d_weights, 0, keepdims=True)
+                pieces.append((first, last, weights, d_weights))
+            d_query = jnp.zeros((HEAD, span), jnp.float32)
+            for first, last, weights, d_weights in pieces:
+                d_scores = (weights * (d_weights - row_term)).astype(jnp.bfloat16)
+                d_query = d_query + dot(refs.key_columns[:, first:last], d_scores)
+                refs.key_grads[:, first:last] += dot(query, d_scores, NT)
+                refs.value_grads[:, first:last] += dot(grad, weights.astype(jnp.bfloat16), NT)
+            refs.results[head, index, 0] = (d_query * HEAD**-0.5).astype(jnp.bfloat16)
+        for index in range(half):
+            other = pl.ds(pl.multiple_of(block_of(index, 1 - at.core) * span, span), span)
+            own = pl.ds(pl.multiple_of(at.blocks[index] * span, span), span)
+            refs.partial_send[head, index, :HEAD, :] = refs.key_grads[:, other].astype(jnp.bfloat16)
+            refs.partial_send[head, index, HEAD:, :] = refs.value_grads[:, other].astype(jnp.bfloat16)
+            refs.kept[head, index, :HEAD, :] = refs.key_grads[:, own]
+            refs.kept[head, index, HEAD:, :] = refs.value_grads[:, own]
+        passed.append(
+            links.copy(refs.partial_send.at[head], refs.partial_recv.at[head], at.sibling)
+        )
+
+    for head in range(heads):
+        attend(head)
+        if head > 0:
+            send_back(head - 1)
+    reducer.second(DOWN)
+    send_back(heads - 1)
+    reducer.second(UP)
+    reducer.second(OUT)
+    for part in (DOWN, UP, OUT):
+        reducer.third(part)
+    for part in (DOWN, UP, OUT):
+        reducer.fourth(part)
+    for part in (DOWN, UP, OUT):
+        reducer.last(part)
+    for head in range(heads):
+        for count, (device, seq, group) in enumerate(at.targets):
+            landed = refs.d_qkv.at[
+                :,
+                group * group_rows + head * HEAD : group * group_rows + (head + 1) * HEAD,
+                seq * span : (seq + 1) * span,
+            ]
+            remote(
+                landed, landed, refs.send.at[leave],
+                refs.recv.at[returned + head * len(at.targets) + count], at.sibling,
+            ).wait_recv()
+    for sent in spread + going:
+        at.wait_sent(*sent)
+    links.finish()
+
+
+def back_one_weights(width, hidden_width, n):
+    return {
+        DOWN: (hidden_width // n, width // 2),
+        UP: (width // n, hidden_width // 2),
+        OUT: (width // n, width // 2),
+    }
+
+
+def back_one_parts(width, hidden_width):
+    return {
+        DOWN: (DOWN, 0, width // 2, 1),
+        UP: (UP, 0, hidden_width // 2, 0),
+        OUT: (OUT, 0, width // 2, 0),
+    }
+
+
+def back_one(
+    cotangent, valid, hidden, raised, normed, active, attended, held, lse, gain,
+    w_out, w_up, w_down, collective,
+):
+    seqs, span, width = cotangent.shape
+    n, rows, _ = held.shape
+    group_rows = rows // 3
+    groups = width // group_rows
+    hidden_width = w_up.shape[2]
+    tokens = seqs * span
+    half, heads = n // 2, group_rows // HEAD
+    low, wide = jnp.bfloat16, jnp.float32
+    weights, parts = back_one_weights(width, hidden_width, n), back_one_parts(width, hidden_width)
+    inputs = dict(
+        cotangent=(cotangent, HBM), valid=(valid, VMEM), hidden=(hidden, HBM), raised=(raised, HBM),
+        normed=(normed, HBM), active=(active, HBM), attended=(attended, HBM), held=(held, HBM),
+        lse=(lse, VMEM), gain=(gain, VMEM), w_out=(w_out, HBM), w_up=(w_up, HBM),
+        w_down=(w_down, HBM),
+    )
+    outputs = dict(
+        d_qkv=((3, width, tokens), low, VMEM),
+        grad_out=((width, tokens), wide, VMEM),
+        small=((width, 2), wide, VMEM),
+        down_grad=((weights[DOWN][0], width), wide, VMEM),
+        up_grad=((weights[UP][0], hidden_width), wide, VMEM),
+        out_grad=((weights[OUT][0], width), wide, VMEM),
+    )
+    scratch = dict(
+        down=(w_down.shape[1:], low), up=(w_up.shape[1:], low), out=(w_out.shape[1:], low),
+        cot=(cotangent.shape, low), grad=((width, tokens), wide), hidden_in=((width, tokens), wide),
+        raised_in=(raised.shape, raised.dtype), d_attended=((width, tokens), low),
+        down_left=(active.shape, low), down_right=((width, tokens), low),
+        up_left=(normed.shape, low), up_right=((hidden_width, tokens), low),
+        out_left=(attended.shape, low), out_right=((width, tokens), low),
+        held_in=(held.shape, low), landing=((half, group_rows, span), low),
+        results=((heads, half, 3, HEAD, span), low), kept=((heads, half, 2 * HEAD, span), wide),
+        partial_send=((heads, half, 2 * HEAD, span), low),
+        partial_recv=((heads, half, 2 * HEAD, span), low),
+        key_grads=((HEAD, n * span), wide), value_grads=((HEAD, n * span), wide),
+        key_rows=((n * span, HEAD), low), key_columns=((HEAD, n * span), low),
+        value_rows=((n * span, HEAD), low),
+        **reducer_scratch(weights, parts, groups, tokens),
+    )
+    body = functools.partial(
+        back_one_body, n, seqs, groups, span, group_rows, width, hidden_width
+    )
+    return launch(body, inputs, outputs, scratch, 120, collective)
+
+
+def back_two_weights(width, hidden_width, n):
+    return {
+        QKV: (width // n, 3 * width // 2),
+        DOWN: (hidden_width // n, width // 2),
+        UP: (width // n, hidden_width // 2),
+        OUT: (width // n, width // 2),
+    }
+
+
+def back_two_parts(width, hidden_width):
+    return {
+        QKV_MORE: (QKV, TILE, 3 * width // 2 - TILE, 1),
+        QKV_LESS: (QKV, 0, TILE, 0),
+        DOWN: (DOWN, 0, width // 2, 1),
+        UP: (UP, 0, hidden_width // 2, 0),
+        OUT: (OUT, 0, width // 2, 0),
+    }
+
+
+def back_two_body(n, seqs, span, width, hidden_width, refs):
+    channels = width // n
+    me, core = lax.axis_index(SEQ), lax.axis_index(BATCH)
+    peers = [lax.rem(me + step, n) for step in range(1, n)]
+    links, loads = Links(refs), Loads(refs)
+    weights, parts = back_two_weights(width, hidden_width, n), back_two_parts(width, hidden_width)
+    reducer = Reducer(refs, links, n // 4, weights, parts)
+    barrier = pltpu.get_barrier_semaphore()
+    for device in [(peer, core) for peer in peers] + [reducer.sibling]:
+        pl.semaphore_signal(barrier, inc=1, device_id=device, device_id_type=MESH)
+    loads.start("w_qkv", refs.w_qkv.at[1], refs.qkv)
+    loads.start("d_qkv", refs.d_qkv, refs.qkv_right)
+    loads.start("hidden_two", refs.hidden_two, refs.hidden_two_in)
+    loads.start("grad", refs.grad, refs.grad_now)
+    loads.start("normed_three", refs.normed_three, refs.qkv_left)
+    loads.start("w_down", refs.w_down.at[0], refs.down)
+    loads.start("raised", refs.raised, refs.raised_in)
+    loads.start("w_up", refs.w_up.at[0], refs.up)
+    loads.start("active", refs.active, refs.down_left)
+    loads.start("hidden_one", refs.hidden_one, refs.hidden_one_in)
+    loads.start("normed_two", refs.normed_two, refs.up_left)
+    loads.start("w_out", refs.w_out.at[0], refs.out)
+    loads.start("gated", refs.gated, refs.out_left)
+    loads.start("queries", refs.queries, refs.queries_in)
+    loads.start("mixer", refs.mixer, refs.mixer_in)
+    loads.start("carried", refs.carried, refs.carried_in)
+    loads.start("held", refs.held, refs.held_in)
+
+    loads.wait("w_qkv", "d_qkv")
+    d_normed = dot(refs.qkv[...], refs.qkv_right[...])
+    pl.semaphore_wait(barrier, n)
+    loads.wait("normed_three")
+    reducer.exchange(QKV)
+    loads.wait("hidden_two", "grad")
+    d_inputs, gain_part, bias_part = norm_gradient(
+        refs.hidden_two_in[...], refs.gains[:, 2:3], d_normed
+    )
+    refs.small[:, 0:1] = gain_part
+    refs.small[:, 1:2] = bias_part
+    grad = refs.grad_now[...] + d_inputs
+    refs.grad_now[...] = grad
+    refs.down_right[...] = grad.astype(jnp.bfloat16)
+    loads.wait("w_down", "raised", "active")
+    reducer.exchange(DOWN)
+
+    def store_raised(rows, value):
+        slope = gelu_slope(refs.raised_in[rows, :].astype(jnp.float32))
+        refs.up_right[rows, :] = (slope * value).astype(jnp.bfloat16)
+
+    rows_product(refs.down, refs.down_right[...], hidden_width, 512, store_raised)
+    loads.wait("w_up", "hidden_one", "normed_two")
+    reducer.exchange(UP)
+    d_normed = dot(refs.up[...], refs.up_right[...])
+    d_inputs, gain_part, bias_part = norm_gradient(
+        refs.hidden_one_in[...], refs.gains[:, 1:2], d_normed
+    )
+    refs.small[:, 2:3] = gain_part
+    refs.small[:, 3:4] = bias_part
+    grad = refs.grad_now[...] + d_inputs
+    refs.grad_out[...] = grad
+    refs.out_right[...] = grad.astype(jnp.bfloat16)
+    loads.wait("w_out", "gated", "queries", "mixer", "carried")
+    reducer.exchange(OUT)
+    d_gated = dot(refs.out[...], refs.out_right[...])
+    d_mixer = d_gated * refs.queries_in[...]
+    for seq in range(seqs):
+        refs.d_conv[seq] = d_mixer[:, seq * span : (seq + 1) * span].astype(jnp.bfloat16)
+    going = []
+    arrive, answered = links.slots(n - 1), links.slots(n - 1)
+    for step, peer in enumerate(peers):
+        rows = pl.ds(pl.multiple_of(peer * channels, 16), channels)
+        going.append(
+            links.copy(refs.d_conv.at[:, rows, :], refs.landing.at[me], (peer, core), arrive + step)
+        )
+    own_rows = pl.ds(pl.multiple_of(me * channels, 16), channels)
+    loads.start("own", refs.d_conv.at[:, own_rows, :], refs.landing.at[me])
+    refs.d_mixer[...] = d_mixer
+    refs.d_queries[...] = (d_gated * refs.mixer_in[...]).astype(jnp.bfloat16)
+    refs.small[:, 4:5] = jnp.sum(d_mixer * refs.carried_in[...].astype(jnp.float32), 1, keepdims=True)
+
+    reducer.first(QKV_MORE)
+    reducer.first(QKV_LESS)
+    reducer.first(DOWN)
+    reducer.first(UP)
+    reducer.first(OUT)
+    total_rows = n * seqs * channels
+    loads.wait("held")
+    refs.flat_x[...] = refs.held_in[...].astype(jnp.float32).reshape(total_rows, span)
+    loads.wait("own")
+    for copy in going:
+        copy.wait_recv()
+    refs.flat_d[...] = refs.landing[...].astype(jnp.float32).reshape(total_rows, span)
+
+    def one_channel(channel, carry):
+        mixer_backward_channel(n, seqs, span, channels, refs, channel)
+        return carry
+
+    reducer.second(QKV_MORE)
+    reducer.second(QKV_LESS)
+    lax.fori_loop(0, channels // 2, one_channel, 0, unroll=2)
+    reducer.second(DOWN)
+    reducer.third(QKV_MORE)
+    reducer.third(QKV_LESS)
+    lax.fori_loop(channels // 2, channels, one_channel, 0, unroll=2)
+    refs.answer[...] = refs.flat_out[...].reshape(n, seqs, channels, span).astype(jnp.bfloat16)
+    back = []
+    for step, peer in enumerate(peers):
+        back.append(
+            links.copy(
+                refs.answer.at[peer], refs.from_conv.at[:, own_rows, :], (peer, core),
+                answered + step,
+            )
+        )
+    loads.start("answer", refs.answer.at[me], refs.from_conv.at[:, own_rows, :])
+    states = [
+        links.copy(refs.rate_grad, refs.rate_other, reducer.sibling),
+        links.copy(refs.weight_grad, refs.weight_other, reducer.sibling),
+    ]
+    reducer.second(UP)
+    reducer.second(OUT)
+    for part in (DOWN, UP, OUT):
+        reducer.third(part)
+    for copy in states:
+        copy.wait_recv()
+    refs.rate_sum[...] = refs.rate_grad[...] + refs.rate_other[...]
+    refs.weight_sum[...] = refs.weight_grad[...] + refs.weight_other[...]
+    for part in parts:
+        reducer.fourth(part)
+    for part in parts:
+        reducer.last(part)
+    loads.wait("answer")
+    for copy in back:
+        copy.wait_recv()
+    links.finish()
+
+
+def back_two(
+    d_qkv, grad, hidden_two, normed_three, raised, normed_two, active, hidden_one, gated,
+    queries, mixer, carried, held, gains, rates, rate_weights, w_qkv, w_out, w_up, w_down, collective,
+):
+    n, seqs, channels, span = held.shape
+    width, hidden_width = w_up.shape[1:]
+    tokens = seqs * span
+    low, wide = jnp.bfloat16, jnp.float32
+    weights, parts = back_two_weights(width, hidden_width, n), back_two_parts(width, hidden_width)
+    inputs = dict(
+        d_qkv=(d_qkv, HBM), grad=(grad, HBM), hidden_two=(hidden_two, HBM),
+        normed_three=(normed_three, HBM), raised=(raised, HBM), normed_two=(normed_two, HBM),
+        active=(active, HBM), hidden_one=(hidden_one, HBM), gated=(gated, HBM),
+        queries=(queries, HBM), mixer=(mixer, HBM), carried=(carried, HBM), held=(held, HBM),
+        gains=(gains, VMEM), rates=(rates, VMEM), rate_weights=(rate_weights, VMEM),
+        w_qkv=(w_qkv, HBM), w_out=(w_out, HBM), w_up=(w_up, HBM), w_down=(w_down, HBM),
+    )
+    square, state = (width, tokens), (channels, 2 * STATES)
+    outputs = dict(
+        from_conv=((seqs, width, span), low, VMEM),
+        d_mixer=(square, wide, VMEM),
+        d_queries=(square, low, VMEM),
+        grad_out=(square, wide, VMEM),
+        small=((width, 5), wide, VMEM),
+        rate_sum=(state, wide, VMEM),
+        weight_sum=(state, wide, VMEM),
+        qkv_grad=((weights[QKV][0], 3 * width), wide, VMEM),
+        down_grad=((weights[DOWN][0], width), wide, VMEM),
+        up_grad=((weights[UP][0], hidden_width), wide, VMEM),
+        out_grad=((weights[OUT][0], width), wide, VMEM),
+    )
+    flat = (n * seqs * channels, span)
+    scratch = dict(
+        qkv=(w_qkv.shape[1:], low), down=(w_down.shape[1:], low), up=(w_up.shape[1:], low),
+        out=(w_out.shape[1:], low),
+        qkv_left=(normed_three.shape, low), qkv_right=((3 * width, tokens), low),
+        down_left=(active.shape, low), down_right=(square, low),
+        up_left=(normed_two.shape, low), up_right=((hidden_width, tokens), low),
+        out_left=(gated.shape, low), out_right=(square, low),
+        hidden_two_in=(square, wide), hidden_one_in=(square, wide), grad_now=(square, wide),
+        raised_in=(raised.shape, raised.dtype), queries_in=(square, queries.dtype),
+        mixer_in=(square, mixer.dtype), carried_in=(square, low), held_in=(held.shape, low),
+        d_conv=((seqs, width, span), low), landing=(held.shape, low), answer=(held.shape, low),
+        flat_x=(flat, wide), flat_d=(flat, wide), flat_out=(flat, wide),
+        rate_grad=(state, wide), weight_grad=(state, wide),
+        rate_other=(state, wide), weight_other=(state, wide),
+        **reducer_scratch(weights, parts, n // 4, tokens),
+    )
+    body = functools.partial(back_two_body, n, seqs, span, width, hidden_width)
+    return launch(body, inputs, outputs, scratch, 100, collective)
+
+
+def back_three_weights(width, n):
+    return {QKV: (width // n, 3 * width // 2)}
+
+
+def back_three_parts(width, n):
+    return {
+        SMALL: (width // n, 0, 128, 0),
+        QKV_MORE: (QKV, TILE, 3 * width // 2 - TILE, 1),
+        QKV_LESS: (QKV, 0, TILE, 0),
+    }
+
+
+def back_three_body(n, seqs, span, width, refs):
+    me, core = lax.axis_index(SEQ), lax.axis_index(BATCH)
+    links, loads = Links(refs), Loads(refs)
+    weights, parts = back_three_weights(width, n), back_three_parts(width, n)
+    reducer = Reducer(refs, links, n // 4, weights, parts)
+    barrier = pltpu.get_barrier_semaphore()
+    before, after = (lax.rem(me + n - 1, n), core), (lax.rem(me + 1, n), core)
+    greeted = [*reducer.neighbours(), before, after]
+    for device in greeted:
+        pl.semaphore_signal(barrier, inc=1, device_id=device, device_id_type=MESH)
+    tokens = seqs * span
+    loads.start("from_conv", refs.from_conv, refs.conv_in)
+    loads.start("d_mixer", refs.d_mixer, refs.mixer_in)
+    loads.start("values", refs.values, refs.values_in)
+    loads.start("shifted", refs.shifted, refs.shifted_in)
+    loads.start("keys", refs.keys, refs.keys_in)
+    loads.start("d_queries", refs.d_queries, refs.qkv_right.at[:width, :])
+    loads.start("w_qkv", refs.w_qkv.at[0], refs.qkv)
+    loads.start("normed", refs.normed, refs.qkv_left)
+    loads.start("hidden", refs.hidden, refs.hidden_in)
+    loads.start("grad", refs.grad, refs.grad_in)
+    loads.wait("from_conv", "d_mixer", "values", "shifted")
+    valid = refs.valid[...]
+    conv = jnp.concatenate([refs.conv_in[seq] for seq in range(seqs)], 1).astype(jnp.float32)
+    d_carried = (refs.mixer_in[...] * refs.skip[...] + conv) * valid
+    d_shifted = d_carried * refs.values_in[...]
+    refs.d_shifted[...] = d_shifted
+    for seq in range(seqs):
+        for first in range(0, width, span):
+            turned = d_shifted[first : first + span, seq * span : (seq + 1) * span].T
+            refs.rim_out[seq, :, first : first + span] = turned[: refs.rim_out.shape[1]]
+    refs.qkv_right[2 * width :, :] = (d_carried * refs.shifted_in[...]).astype(jnp.bfloat16)
+    pl.semaphore_wait(barrier, len(greeted))
+    halo = links.copy(refs.rim_out, refs.rim_in, before)
+    loads.wait("keys")
+    halo.wait_recv()
+    lane = lax.broadcasted_iota(jnp.int32, (width, span), 1)
+    there = jnp.where(me == n - 1, 0.0, 1.0)
+    rim = refs.rim_in.shape[1]
+    tap_sums = [jnp.zeros((width, 1), jnp.float32) for _ in range(TAPS)]
+    for seq in range(seqs):
+        lanes = slice(seq * span, (seq + 1) * span)
+        own = refs.d_shifted[:, lanes]
+        keys = refs.keys_in[:, lanes].astype(jnp.float32)
+        pieces = []
+        for first in range(0, width, span):
+            piece = refs.rim_in[seq, :, first : first + span] * there
+            piece = jnp.concatenate([piece, jnp.zeros((span - rim, span), jnp.float32)], 0)
+            pieces.append(piece.T)
+        following = jnp.concatenate(pieces, 0)
+        d_keys = jnp.zeros((width, span), jnp.float32)
+        for offset in range(TAPS):
+            moved = own
+            if offset > 0:
+                moved = jnp.where(
+                    lane < span - offset,
+                    pltpu.roll(own, span - offset, 1),
+                    pltpu.roll(following, span - offset, 1),
+                )
+            d_keys = d_keys + refs.taps[:, offset : offset + 1] * moved
+            tap_sums[offset] = tap_sums[offset] + jnp.sum(moved * keys, 1, keepdims=True)
+        refs.qkv_right[width : 2 * width, lanes] = d_keys.astype(jnp.bfloat16)
+    loads.wait("d_queries", "normed")
+    reducer.exchange(QKV)
+    loads.wait("w_qkv", "hidden", "grad")
+    d_normed = dot(refs.qkv[...], refs.qkv_right[...])
+    d_inputs, gain_part, bias_part = norm_gradient(refs.hidden_in[...], refs.gain[...], d_normed)
+    refs.total[...] = (refs.grad_in[...] + d_inputs) * valid
+    refs.sums[...] = refs.small_in[...]
+    for offset in range(TAPS):
+        refs.sums[:, 8 + offset : 9 + offset] = tap_sums[offset]
+    refs.sums[:, 0:1] = gain_part
+    refs.sums[:, 4:5] = bias_part
+    shared = links.copy(refs.sums, refs.sums_other, reducer.sibling)
+    reducer.first(QKV_MORE)
+    reducer.first(QKV_LESS)
+    shared.wait_recv()
+    rows = width // n
+    refs.slices[...] = (refs.sums[...] + refs.sums_other[...]).reshape(n, rows, 128)
+    reducer.first_given(SMALL, refs.slices)
+    for seq in range(seqs):
+        for first in range(0, width, span):
+            refs.d_tokens[seq, :, first : first + span] = refs.total[
+                first : first + span, seq * span : (seq + 1) * span
+            ].T
+    order = (QKV_MORE, QKV_LESS, SMALL)
+    for part in order:
+        reducer.second(part)
+    for part in order:
+        reducer.third(part)
+    reducer.fourth(QKV_MORE)
+    reducer.fourth(QKV_LESS)
+    total = reducer.total(SMALL)
+    padded = jnp.concatenate([total, jnp.zeros((128 - rows, 128), jnp.float32)], 0).T
+    refs.small_sum[...] = padded[: refs.small_sum.shape[0], :rows]
+    reducer.last(QKV_MORE)
+    reducer.last(QKV_LESS)
+    links.finish()
+
+
+def back_three(
+    from_conv, d_mixer, d_queries, values, shifted, keys, grad, hidden, normed, valid, gain, skip,
+    taps, small, w_qkv, collective,
+):
+    seqs, width, span = from_conv.shape
+    n = normed.shape[0]
+    tokens = seqs * span
+    low, wide = jnp.bfloat16, jnp.float32
+    weights, parts = back_three_weights(width, n), back_three_parts(width, n)
+    inputs = dict(
+        from_conv=(from_conv, HBM), d_mixer=(d_mixer, HBM), d_queries=(d_queries, HBM),
+        values=(values, HBM), shifted=(shifted, HBM), keys=(keys, HBM), grad=(grad, HBM),
+        hidden=(hidden, HBM), normed=(normed, HBM), valid=(valid, VMEM), gain=(gain, VMEM),
+        skip=(skip, VMEM), taps=(taps, VMEM), small_in=(small, VMEM), w_qkv=(w_qkv, HBM),
+    )
+    square = (width, tokens)
+    outputs = dict(
+        d_tokens=((seqs, span, width), wide, VMEM),
+        qkv_grad=((width // n, 3 * width), wide, VMEM),
+        small_sum=((16, width // n), wide, VMEM),
+    )
+    scratch = dict(
+        qkv=(w_qkv.shape[1:], low), qkv_left=(normed.shape, low), qkv_right=((3 * width, tokens), low),
+        conv_in=(from_conv.shape, low), mixer_in=(square, wide), values_in=(square, values.dtype),
+        shifted_in=(square, shifted.dtype), keys_in=(square, low), hidden_in=(square, wide),
+        grad_in=(square, wide), d_shifted=(square, wide), total=(square, wide),
+        rim_out=((seqs, 8, width), wide), rim_in=((seqs, 8, width), wide),
+        sums=((width, 128), wide), sums_other=((width, 128), wide),
+        slices=((n, width // n, 128), wide),
+        **reducer_scratch(weights, parts, n // 4, tokens),
+    )
+    body = functools.partial(back_three_body, n, seqs, span, width)
+    return launch(body, inputs, outputs, scratch, 40, collective)
+
+
+def per_device_by_heads(
+    tokens,
+    cotangent,
+    lengths,
+    norm_gain,
+    norm_bias,
+    w_qkv,
+    w_out,
+    w_up,
+    w_down,
+    taps,
+    skip,
+    ssm_rate,
+    ssm_out,
+):
+    seq_count, span_rows, width = tokens.shape[1:]
+    devices = lax.axis_size(SEQ)
+    place = lax.axis_index(SEQ)
+    channels = width // devices
+    depth = devices // 4
+    groups = depth
+    rim = TAPS - 1
+    row_count = seq_count * span_rows
+    positions = place * span_rows + jnp.arange(span_rows, dtype=jnp.int32)
+    validity = (positions[None, :] < lengths[0][:, None]).astype(jnp.float32)[:, :, None]
+    rates = lax.dynamic_slice_in_dim(ssm_rate, place * channels, channels, 0)
+    weights = lax.dynamic_slice_in_dim(ssm_out, place * channels, channels, 0)
+    rates = jnp.concatenate([rates, rates], 1)
+    weights = jnp.concatenate([weights, weights], 1)
+
+    def to_channels(value):
+        return value.transpose(0, 2, 1)
+
+    def feed_forward(inputs, norm_row, layer):
+        normed = layer_norm(inputs, norm_gain[norm_row], norm_bias[norm_row]).astype(jnp.bfloat16)
+        raised = dense_product(normed, w_up[layer])
+        active = jax.nn.gelu(raised).astype(jnp.bfloat16)
+        return normed, raised, active, inputs + dense_product(active, w_down[layer])
+
+    flat_in = (tokens[0].astype(jnp.float32) * validity).reshape(row_count, width)
+    normed_one = layer_norm(flat_in, norm_gain[0], norm_bias[0]).astype(jnp.bfloat16)
+    qkv_one = dense_product(normed_one, w_qkv[0]).reshape(seq_count, span_rows, 3 * width)
+    queries_one = qkv_one[:, :, :width]
+    keys_one = qkv_one[:, :, width : 2 * width].astype(jnp.bfloat16)
+    values_one = qkv_one[:, :, 2 * width :]
+    earlier = passed_along(keys_one[:, span_rows - rim :], SEQ, 1)
+    extended = jnp.concatenate([earlier, keys_one], 1)
+
+    def tap_rows(offset):
+        return extended[:, rim - offset : rim - offset + span_rows].astype(jnp.float32)
+
+    shifted = sum((taps[offset] * tap_rows(offset) for offset in range(TAPS)))
+    carried_low = (shifted * values_one * validity).astype(jnp.bfloat16)
+    convolved, held = mixer_forward(to_channels(carried_low), rates, weights, devices, 1)
+    carried = carried_low.astype(jnp.float32)
+    mixer = to_channels(convolved).astype(jnp.float32) + skip * carried
+    gated = (queries_one * mixer).reshape(row_count, width).astype(jnp.bfloat16)
+    hidden_one = flat_in + dense_product(gated, w_out[0])
+    normed_two, raised_one, active_one, hidden_two = feed_forward(hidden_one, 1, 0)
+    normed_three = layer_norm(hidden_two, norm_gain[2], norm_bias[2]).astype(jnp.bfloat16)
+    qkv_two = dense_product(normed_three, w_qkv[1]).astype(jnp.bfloat16)
+    group_rows = width // groups
+    qkv_columns = (
+        qkv_two.reshape(seq_count, span_rows, 3, groups, group_rows)
+        .transpose(0, 3, 2, 4, 1)
+        .reshape(seq_count, groups, 3 * group_rows, span_rows)
+    )
+    attended, kept, log_totals = attention_forward(qkv_columns, devices, 2)
+    attended_columns = attended
+    attended = attended.T
+    hidden_three = hidden_two + dense_product(attended, w_out[1])
+    normed_four, raised_two, active_two, hidden_four = feed_forward(hidden_three, 3, 1)
+    output = hidden_four.reshape(seq_count, span_rows, width) * validity
+
+    def sliced(value):
+        return value.T.reshape(devices, value.shape[1] // devices, row_count)
+
+    valid = validity.reshape(1, row_count)
+    back = back_one(
+        cotangent[0], valid, hidden_three.T, raised_two.T, sliced(normed_four), sliced(active_two),
+        attended_columns.reshape(devices, channels, row_count), kept, log_totals,
+        norm_gain[3][:, None], w_out, w_up, w_down, 3,
+    )
+    out_two_grad, up_two_grad, down_two_grad = back.out_grad, back.up_grad, back.down_grad
+    flat = row_count, width
+
+    def turned(value):
+        return value.reshape(flat).T
+
+    gains = norm_gain.T
+    more = back_two(
+        back.d_qkv.reshape(3 * width, row_count), back.grad_out, hidden_two.T, sliced(normed_three),
+        raised_one.T, sliced(normed_two), sliced(active_one), hidden_one.T, sliced(gated),
+        turned(queries_one), turned(mixer), turned(carried_low), held, gains, rates, weights,
+        w_qkv, w_out, w_up, w_down, 4,
+    )
+    none = jnp.zeros((width, 1), jnp.float32)
+    small = jnp.concatenate(
+        [
+            none, more.small[:, 2:3], more.small[:, 0:1], back.small[:, 0:1],
+            none, more.small[:, 3:4], more.small[:, 1:2], back.small[:, 1:2],
+            none, none, none, none, more.small[:, 4:5],
+            jnp.zeros((width, 128 - 13), jnp.float32),
+        ],
+        1,
+    )
+    end = back_three(
+        more.from_conv, more.d_mixer, more.d_queries, turned(values_one), turned(shifted),
+        turned(keys_one), more.grad_out, flat_in.T, sliced(normed_one), valid,
+        gains[:, 0:1], skip[:, None], taps.T, small, w_qkv, 5,
+    )
+    small = end.small_sum
+    return (
+        output[None].astype(jnp.bfloat16),
+        end.d_tokens[None],
+        small[:4],
+        small[4:7],
+        small[7],
+        jnp.stack([end.qkv_grad, more.qkv_grad]),
+        jnp.stack([more.out_grad, out_two_grad]),
+        jnp.stack([more.up_grad, up_two_grad]),
+        jnp.stack([more.down_grad, down_two_grad]),
+        small[8 : 8 + TAPS],
+        small[8 + TAPS],
+        more.rate_sum[:, :STATES],
+        more.weight_sum[:, :STATES],
+    )
+
+
+def fits_by_heads(mesh):
+    devices = mesh.shape[SEQ]
+    return devices == 16 and mesh.shape[BATCH] == 2
+
+
 def solution(mesh):
     placed = (
-        P("batch", None, "seq", None),
-        P("batch", None, "seq", None),
-        P("batch", None),
+        P(BATCH, None, SEQ, None),
+        P(BATCH, None, SEQ, None),
+        P(BATCH, None),
         P(),
         P(),
         P(),
@@ -564,23 +1972,23 @@
         P(),
     )
     return jax.shard_map(
-        per_device,
+        per_device_by_heads if fits_by_heads(mesh) else per_device,
         mesh=mesh,
         in_specs=placed,
         out_specs=(
-            P("batch", None, "seq", None),
-            P("batch", None, "seq", None),
-            P(None, "seq"),
-            P(None, "seq"),
-            P("seq"),
-            P(None, "seq", None),
-            P(None, "seq", None),
-            P(None, "seq", None),
-            P(None, "seq", None),
-            P(None, "seq"),
-            P("seq"),
-            P("seq", None),
-            P("seq", None),
+            P(BATCH, None, SEQ, None),
+            P(BATCH, None, SEQ, None),
+            P(None, SEQ),
+            P(None, SEQ),
+            P(SEQ),
+            P(None, SEQ, None),
+            P(None, SEQ, None),
+            P(None, SEQ, None),
+            P(None, SEQ, None),
+            P(None, SEQ),
+            P(SEQ),
+            P(SEQ, None),
+            P(SEQ, None),
         ),
         check_vma=False,
     )

time: 3100 us -> 518 us (0.17)
  waiting for transfers between devices: 1750 us -> 0.01 us
  matrix products: 556 us -> 27 us
  Pallas kernels: 0 us -> 404 us
  other arithmetic: 385 us -> 23.6 us
  local copies, waits for them, and re-layouts: 225 us -> 52.6 us
  loops' own time: 96.7 us -> 0 us
  starting transfers between devices: 42.4 us -> 5.86 us
    reduce_scatter x6 -> x0, waiting for transfers between devices: 1120 us -> none  [the longest x1 288 us: per_device(): lax.psum_scatter(jnp.stack([down_one, down_two]), 'seq', scatter_dimensio...]
    all_gather x8 -> x0, waiting for transfers between devices: 414 us -> none  [the longest x4 278 us: attend_forward(): lax.all_gather(values_low, 'seq', axis=0, tiled=True)]
    pallas_call x0 -> x5, Pallas kernels: none -> 404 us  [the longest x3 290 us: launch(): pl.pallas_call(kernel, out_shape=tuple((jax.ShapeDtypeStruct(shape, kind)...]
    dot_general x196 -> x0, matrix products: 366 us -> none  [the longest x104 188 us: product_right(): lax.dot_general(operand_a, operand_b, (((1,), (1,)), ((), ())), preferred...]
    reduce_sum x65 -> x0, other arithmetic: 231 us -> none  [the longest x8 112 us: add_block(): real_den = -jnp.expm1(-rate_part) + decays * 2.0 * half_sine * half_sine]
    unnamed x23 -> x0, waiting for transfers between devices: 174 us -> none
    dot_general x85 -> x8, matrix products: 190 us -> 27 us  [dense_product(): return jnp.dot(operand_a, operand_b, preferred_element_type=jnp.float32)]
    another operation x8 -> x0, loops' own time: 96.7 us -> none  [the longest x2 63.4 us: attend_backward(): lax.map(head_backward, jnp.arange(HEADS, dtype=jnp.int32))]
  transfers between devices with their start and end apart: 28 -> 1, of which waited for: 22 -> 0; matrix products, arithmetic and copies ran while one was open for 27% -> 2% of each run, Pallas kernels for 0% -> 0%
where the time goes in v2:
time: 518 us; the launch traced here: 514 us
  Pallas kernels  404 us (78%)
  local copies, waits for them, and re-layouts  52.6 us (10%)
  matrix products  27 us (5%)
  other arithmetic  23.6 us (5%)
  starting transfers between devices  5.86 us (1%)
    pallas_call x3, Pallas kernels, launch(): pl.pallas_call(kernel, out_shape=tuple((jax.ShapeDtypeStruct(shape, kind)...  290 us
    pallas_call x1, Pallas kernels, mixer_forward(): pl.pallas_call(functools.partial(mixer_forward_kernel, n, seqs, span, cha...  58.7 us
    pallas_call x1, Pallas kernels, attention_forward(): pl.pallas_call(functools.partial(attention_forward_kernel, n, seqs, group...  55 us
    dot_general x8, matrix products, dense_product(): return jnp.dot(operand_a, operand_b, preferred_element_type=jnp.float32)  27 us
  transfers between devices with their start and end apart: 1, of which 0 were waited for; matrix products, arithmetic and copies ran while one was open for 2% of the time, Pallas kernels for 0%

profile of v2, /device:TPU:0, one launch (start us, length us, event | category | flops | bytes accessed | tf_op | source)
XLA Modules:
  0.0 514.1 jit_solution(11777227745236180820)
XLA Ops:
  5.7 3.8 fusion.96
  10.5 5.9 %collective-permute-start = (bf16[2,3,768]{1,2,0:T(8,128)(2,1)}, bf16[2,3,768]{1,2,0:T(8,128)(2,1)}, u32[]{:S(2)}, u32[]{:S(2)}) collective-permute-start(bf16[2,3,768]{1,2,0:T(8,128)(2,1)} %slice.173), channel_id=1, source_target_pairs={{0,2},{2,4},{4,6},{6,8},{8,10},{10,12},{12,14},{14,16},{16,18},{18... | collective-permute-start | bytes 27656 | tf_op jit(solution)/shard_map/ppermute | solution.py:41
  26.6 3.0 multiply_convert_fusion.2
  29.6 58.7 %shard_map.228 = (bf16[2,768,128]{2,1,0:T(8,128)(2,1)}, bf16[16,2,48,128]{3,2,1,0:T(8,128)(2,1)}) custom-call(bf16[2,768,128]{2,1,0:T(8,128)(2,1)} %bitcast.172, f32[48,128]{1,0:T(8,128)} %pad_maximum_fusion.5.rate_ref.refs_14_, f32[48,128]{1,0:T(8,128)} %pad_maximum_fusion.6.weight_ref.refs_15_), custom_call_target="tpu_custom_call" | custom-call | tf_op jit(solution)/shard_map/pallas_call | solution.py:706
  88.3 3.2 slice_bitcast_fusion
  94.8 3.9 fusion.6
  98.8 6.0 %fusion.98 = (f32[256]{0:T(256)S(1)}, f32[256,768]{0,1:T(8,128)S(1)}) fusion(f32[256,768]{0,1:T(8,128)S(1)} %get-tuple-element.104, bf16[2,3072,768]{2,1,0:T(8,128)(2,1)} %refs_19_.1, f32[256,3072]{1,0:T(8,128)S(1)} %fusion.6), kind=kOutput, calls=%fused_computation.158 | convolution fusion | flops 1215430400 | bytes 9438208 | tf_op jit(solution)/shard_map/dot_general | solution.py:51
  106.7 2.1 convolution_convert_fusion
  108.8 2.4 copy.57
  111.2 3.5 reshape.301
  114.7 2.6 copy.58
  117.4 55.0 %shard_map.229 = (bf16[768,256]{1,0:T(8,128)(2,1)}, bf16[16,576,128]{2,1,0:T(8,128)(2,1)}, f32[8,3,128]{2,1,0:T(4,128)}) custom-call(bf16[2,4,576,128]{3,2,1,0:T(8,128)(2,1)} %bitcast.174), custom_call_target="tpu_custom_call" | custom-call | tf_op jit(solution)/shard_map/pallas_call | solution.py:940
  176.7 3.9 fusion.2
  182.3 3.3 fusion.64
  185.7 2.4 copy.62
  188.1 4.7 copy.64
  194.7 2.2 fusion.40
  196.9 2.1 fusion.48
  201.9 2.4 bitcast_bitcast_fusion.1
  204.3 113.4 %shard_map.230 = (bf16[3,768,256]{2,1,0:T(8,128)(2,1)}, f32[768,256]{1,0:T(8,128)}, f32[768,2]{1,0:T(8,128)}, f32[192,768]{1,0:T(8,128)}, f32[48,3072]{1,0:T(8,128)}, /*index=5*/f32[48,768]{1,0:T(8,128)}) custom-call(bf16[2,128,768]{2,1,0:T(8,128)(2,1)} %bitcast.199, f32[1,256]{1,0:T(1,128)} %bitcast.202, f32[768,256]{1,0:T(8,128)} %bitcast.170, ...), custom_call_target="tpu_custom_call" | custom-call | tf_op jit(solution)/shard_map/pallas_call | solution.py:977
  317.7 121.8 %shard_map.231 = (bf16[2,768,128]{2,1,0:T(8,128)(2,1)}, f32[768,256]{1,0:T(8,128)}, bf16[768,256]{1,0:T(8,128)(2,1)}, f32[768,256]{1,0:T(8,128)}, f32[768,5]{1,0...) custom-call(bf16[2304,256]{1,0:T(8,128)(2,1)} %bitcast.191, ...), custom_call_target="tpu_custom_call" | custom-call | tf_op jit(solution)/shard_map/pallas_call | solution.py:977
  439.4 3.5 fusion.93
  443.3 3.6 concatenate.19.refs_13_
  446.9 54.9 %shard_map.232 = (f32[2,128,768]{2,1,0:T(8,128)}, f32[48,2304]{1,0:T(8,128)}, f32[16,48]{1,0:T(8,128)}) custom-call(bf16[2,768,128]{2,1,0:T(8,128)(2,1)} %get-tuple-element.45.refs_0_, f32[768,256]{1,0:T(8,128)} %get-tuple-element.46.refs_1_, bf16[768,256]{1,0:T(8,128)(2,1)} %get-tuple-element.47.refs_2_, f32[768,256]{1,0:T(8,128)} %get-tuple-element.110.refs_3_, ...), custom_call_target="tpu_custom_call" | custom-call | tf_op jit(solution)/shard_map/pallas_call | solution.py:977
  (151 shorter events, 44.3 us)
Async XLA Ops:
  0.6 16.6 %copy-start = (f32[768,64]{0,1:T(8,128)S(1)}, f32[768,64]{0,1:T(8,128)}, u32[]{:S(2)}) copy-start(f32[768,64]{0,1:T(8,128)} %param.24) | copy-start | bytes 589828
  3.2 23.4 %copy-start.31 = (f32[2,128]{1,0:T(2,128)}, f32[2,128]{1,0:T(2,128)S(1)}, u32[]{:S(2)}) copy-start(f32[2,128]{1,0:T(2,128)S(1)} %compare_convert_fusion) | copy-start | bytes 3076
  5.7 11.5 %copy-start.33 = (f32[4,768]{1,0:T(4,128)S(1)}, f32[4,768]{1,0:T(4,128)}, u32[]{:S(2)}) copy-start(f32[4,768]{1,0:T(4,128)} %param.22) | copy-start | bytes 36868
  5.7 13.4 %copy-start.38 = (s32[1,2]{1,0:T(1,128)S(1)}, s32[1,2]{1,0:T(1,128)}, u32[]{:S(2)}) copy-start(s32[1,2]{1,0:T(1,128)} %param.15) | copy-start | bytes 28
  5.7 14.2 %copy-start.34 = (f32[4,768]{1,0:T(4,128)S(1)}, f32[4,768]{1,0:T(4,128)}, u32[]{:S(2)}) copy-start(f32[4,768]{1,0:T(4,128)} %param.16) | copy-start | bytes 36868
  9.6 20.1 %copy-start.17 = (f32[2,128,2304]{1,2,0:T(8,128)}, f32[2,128,2304]{1,2,0:T(8,128)S(1)}, u32[]{:S(2)}) copy-start(f32[2,128,2304]{1,2,0:T(8,128)S(1)} %get-tuple-element.102) | copy-start | bytes 7077892
  9.6 12.2 %copy-start.9 = (bf16[1,2,128,768]{3,2,1,0:T(8,128)(2,1)S(1)}, bf16[1,2,128,768]{3,2,1,0:T(8,128)(2,1)}, u32[]{:S(2)}) copy-start(bf16[1,2,128,768]{3,2,1,0:T(8,128)(2,1)} %param.13) | copy-start | bytes 1179652
  9.6 16.1 %copy-start.37 = (f32[768]{0:T(1024)S(1)}, f32[768]{0:T(1024)}, u32[]{:S(2)}) copy-start(f32[768]{0:T(1024)} %param.23) | copy-start | bytes 9220
  10.5 16.1 %collective-permute-start = (bf16[2,3,768]{1,2,0:T(8,128)(2,1)}, bf16[2,3,768]{1,2,0:T(8,128)(2,1)}, u32[]{:S(2)}, u32[]{:S(2)}) collective-permute-start(bf16[2,3,768]{1,2,0:T(8,128)(2,1)} %slice.173), channel_id=1, source_target_pairs={{0,2},{2,4},{4,6},{6,8},{8,10},{10,12},{12,14},{14,16},{16,18},{18... | collective-permute-start | bytes 27656 | tf_op jit(solution)/shard_map/ppermute | solution.py:41
  29.6 62.1 %copy-start.4 = (bf16[2,768,768]{2,1,0:T(8,128)(2,1)S(1)}, bf16[2,768,768]{2,1,0:T(8,128)(2,1)}, u32[]{:S(2)}) copy-start(bf16[2,768,768]{2,1,0:T(8,128)(2,1)} %refs_17_.1) | copy-start | bytes 7077892
  91.7 7.1 %copy-start.10 = (bf16[2,128,768]{2,1,0:T(8,128)(2,1)}, bf16[2,128,768]{2,1,0:T(8,128)(2,1)S(1)}, u32[]{:S(2)}) copy-start(bf16[2,128,768]{2,1,0:T(8,128)(2,1)S(1)} %copy.54) | copy-start | bytes 1179652
  94.8 11.9 %slice-start.3 = ((s8[7077888]{0:T(1024)(128)(4,1)}), s8[4194304]{0:T(1024)(128)(4,1)S(1)}, s32[]{:S(2)}) async-start(s8[7077888]{0:T(1024)(128)(4,1)} %bitcast.165), calls=%async_computation.3 | async-start | bytes 8388608
  98.8 7.9 %slice-start.4 = ((s8[7077888]{0:T(1024)(128)(4,1)}), s8[2883584]{0:T(1024)(128)(4,1)S(1)}, s32[]{:S(2)}) async-start(s8[7077888]{0:T(1024)(128)(4,1)} %bitcast.165), calls=%async_computation.4 | async-start | bytes 5767168
  114.7 67.6 %slice-start = ((s8[9437184]{0:T(1024)(128)(4,1)}), s8[1048576]{0:T(1024)(128)(4,1)S(1)}, s32[]{:S(2)}) async-start(s8[9437184]{0:T(1024)(128)(4,1)} %bitcast.162), calls=%async_computation | async-start | bytes 2097152
  172.4 10.0 %slice-start.1 = ((s8[9437184]{0:T(1024)(128)(4,1)}), s8[4194304]{0:T(1024)(128)(4,1)S(1)}, s32[]{:S(2)}) async-start(s8[9437184]{0:T(1024)(128)(4,1)} %bitcast.162), calls=%async_computation.1 | async-start | bytes 8388608
  174.4 6.3 %copy-start.7 = (f32[256,768]{0,1:T(8,128)}, f32[256,768]{0,1:T(8,128)S(1)}, u32[]{:S(2)}) copy-start(f32[256,768]{0,1:T(8,128)S(1)} %get-tuple-element.108) | copy-start | bytes 2359300
  188.1 6.6 %copy-start.2 = (f32[256,3072]{0,1:T(8,128)}, f32[256,3072]{0,1:T(8,128)S(1)}, u32[]{:S(2)}) copy-start(f32[256,3072]{0,1:T(8,128)S(1)} %copy.62) | copy-start | bytes 9437188
  446.9 58.8 %copy-start.22 = (f32[256,768]{0,1:T(8,128)S(1)}, f32[256,768]{0,1:T(8,128)}, u32[]{:S(2)}) copy-start(f32[256,768]{0,1:T(8,128)} %fusion.64) | copy-start | bytes 2359300
  446.9 59.1 %copy-start.32 = (f32[2,128]{1,0:T(2,128)S(1)}, f32[2,128]{1,0:T(2,128)}, u32[]{:S(2)}) copy-start(f32[2,128]{1,0:T(2,128)} %copy-done.31) | copy-start | bytes 3076
  446.9 59.9 %copy-start.28 = (f32[48,2304]{1,0:T(8,128)S(1)}, f32[48,2304]{1,0:T(8,128)}, u32[]{:S(2)}) copy-start(f32[48,2304]{1,0:T(8,128)} %get-tuple-element.54) | copy-start | bytes 1327108
  501.8 7.1 %copy-start.29 = (f32[48,768]{1,0:T(8,128)S(1)}, f32[48,768]{1,0:T(8,128)}, u32[]{:S(2)}) copy-start(f32[48,768]{1,0:T(8,128)} %get-tuple-element.56) | copy-start | bytes 442372
  501.8 7.1 %copy-start.30 = (f32[48,768]{1,0:T(8,128)S(1)}, f32[48,768]{1,0:T(8,128)}, u32[]{:S(2)}) copy-start(f32[48,768]{1,0:T(8,128)} %get-tuple-element.55) | copy-start | bytes 442372
  501.8 7.8 %copy-start.25 = (f32[48,3072]{1,0:T(8,128)S(1)}, f32[48,3072]{1,0:T(8,128)}, u32[]{:S(2)}) copy-start(f32[48,3072]{1,0:T(8,128)} %get-tuple-element.58) | copy-start | bytes 1769476
  501.8 7.8 %copy-start.27 = (f32[48,3072]{1,0:T(8,128)S(1)}, f32[48,3072]{1,0:T(8,128)}, u32[]{:S(2)}) copy-start(f32[48,3072]{1,0:T(8,128)} %get-tuple-element.57) | copy-start | bytes 1769476
  (21 other events, 69.3 us)
